TPU v7x, 32 devices: a whole 2x2x4 slice. The times are simulated.
32 devices in a mesh: seq: 8 (over z, y), rows: 4 (over x, core).
Axes of the slice: x: 2, y: 2, z: 4, core: 2. Of those that a mesh axis runs over, the one named last changes fastest.
Arguments:
- tokens: bfloat16 [8, 1024, 768], P('rows', 'seq'), may hold values from -6 to 6
- pair_lengths: int32 [8, 16], P('rows'), may hold values from 1 to 512, as said below
- joint_weight: bfloat16 [768, 2304], replicated, may hold values from -0.21875 to 0.21875
- query_bias: float32 [768], replicated, may hold values from -1.2 to 1.2
- value_bias: float32 [768], replicated, may hold values from -0.3 to 0.3
- out_weight: bfloat16 [768, 768], replicated, may hold values from -2 to 2
- out_bias: float32 [768], replicated, may hold values from -3 to 3
- first_gain: float32 [768], replicated, may hold values from 0.25 to 1.75
- first_shift: float32 [768], replicated, may hold values from -3 to 3
- up_weight: bfloat16 [768, 3072], replicated, may hold values from -0.21875 to 0.21875
- up_bias: float32 [3072], replicated, may hold values from -3 to 3
- down_weight: bfloat16 [3072, 768], replicated, may hold values from -0.109375 to 0.109375
- down_bias: float32 [768], replicated, may hold values from -3 to 3
- second_gain: float32 [768], replicated, may hold values from 0.25 to 1.75
- second_shift: float32 [768], replicated, may hold values from -3 to 3
- cotangent: bfloat16 [8, 1024, 768], P('rows', 'seq'), may hold values from -6 to 6
Outputs:
- outputs: bfloat16 [8, 1024, 768], P('rows', 'seq')
- token_gradient: float32 [8, 1024, 768], P('rows', 'seq')
- joint_gradient: float32 [768, 2304], P('seq')
- query_bias_gradient: float32 [768], P('seq')
- value_bias_gradient: float32 [768], P('seq')
- out_gradient: float32 [768, 768], P('seq')
- out_bias_gradient: float32 [768], P('seq')
- first_gain_gradient: float32 [768], P('seq')
- first_shift_gradient: float32 [768], P('seq')
- up_gradient: float32 [768, 3072], P('seq')
- up_bias_gradient: float32 [3072], P('seq')
- down_gradient: float32 [3072, 768], P('seq')
- down_bias_gradient: float32 [768], P('seq')
- second_gain_gradient: float32 [768], P('seq')
- second_shift_gradient: float32 [768], P('seq')
Inputs may be any that keep to these rules, and one draw needn't show every extreme that they name: `pair_lengths`: in every packed row the 16 lengths add up to 1024; no pair is longer than 512 positions (BERT's 512 at most), and in every row one pair has exactly 512.
All inputs are finite; a program needn't handle non-finite values.
Results may differ from a plain program's by a relative error of at most 0.023.
Values may be sent and summed in bfloat16 or wider, within the bound.
No kernel may reach another device: no remote copies, remote signals or barrier semaphores. Data moves between devices by JAX's collectives and lax.ppermute only.
A program may use at most 128 MiB of HBM per device.

v0:
```python
import functools
import math

import jax
import jax.numpy as jnp
from jax import lax
from jax.experimental import pallas as pl
from jax.experimental.pallas import tpu as pltpu
from jax.sharding import PartitionSpec as P

HEADS = 12
HEAD_DIM = 64


NEGATIVE = -1e30
EPSILON = 1e-12


def from_behind(value, axis, steps):
    count = lax.axis_size(axis)
    pairs = [(source, (source + steps) % count) for source in range(count)]
    return lax.ppermute(value, axis, pairs)


def layer_norm(value, gain, shift):
    mean = jnp.mean(value, axis=-1, keepdims=True)
    centred = value - mean
    spread = jnp.mean(centred * centred, axis=-1, keepdims=True)
    return centred * lax.rsqrt(spread + EPSILON) * gain + shift


def gelu_exact(value):
    return jax.nn.gelu(value, approximate=False)


def pair_index(positions, ends):
    return jnp.sum((positions[None, :, None] >= ends[:, None, :]).astype(jnp.int32), axis=2)


def split_heads(array):
    return array.reshape(array.shape[0], array.shape[1], HEADS, HEAD_DIM)


def online_block(state, query_heads, query_pairs, key_block, value_block, key_pairs):
    highest, total, summed = state
    scores = jnp.einsum(
        "rqhd,rkhd->rhqk", query_heads, split_heads(key_block), preferred_element_type=jnp.float32
    ) * HEAD_DIM ** (-0.5)
    allowed = query_pairs[:, None, :, None] == key_pairs[:, None, None, :]
    masked = jnp.where(allowed, scores, NEGATIVE)
    new_high = jnp.maximum(highest, jnp.max(masked, axis=3))
    weights = jnp.where(allowed, jnp.exp(masked - new_high[..., None]), 0.0)
    factor = jnp.exp(highest - new_high)
    total = total * factor + jnp.sum(weights, axis=3)
    summed = summed * jnp.swapaxes(factor, 1, 2)[..., None] + jnp.einsum(
        "rhqk,rkhd->rqhd",
        weights.astype(jnp.bfloat16),
        split_heads(value_block),
        preferred_element_type=jnp.float32,
    )
    return (new_high, total, summed)


def tile_terms(queries, out_grad, log_total, delta, query_pairs, keys, values, key_pairs):
    scale = HEAD_DIM ** (-0.5)
    query_heads = split_heads(queries)
    grad_heads = split_heads(out_grad)
    key_heads = split_heads(keys)
    value_heads = split_heads(values)
    scores = (
        jnp.einsum("rqhd,rkhd->rhqk", query_heads, key_heads, preferred_element_type=jnp.float32)
        * scale
    )
    allowed = query_pairs[:, None, :, None] == key_pairs[:, None, None, :]
    weights = jnp.where(
        allowed, jnp.exp(jnp.where(allowed, scores, NEGATIVE) - log_total[..., None]), 0.0
    )
    weight_grad = jnp.einsum(
        "rqhd,rkhd->rhqk", grad_heads, value_heads, preferred_element_type=jnp.float32
    )
    score_grad = (weights * (weight_grad - delta[..., None])).astype(jnp.bfloat16)
    query_term = (
        jnp.einsum("rhqk,rkhd->rqhd", score_grad, key_heads, preferred_element_type=jnp.float32)
        * scale
    )
    key_term = (
        jnp.einsum("rhqk,rqhd->rkhd", score_grad, query_heads, preferred_element_type=jnp.float32)
        * scale
    )
    value_term = jnp.einsum(
        "rhqk,rqhd->rkhd",
        weights.astype(jnp.bfloat16),
        grad_heads,
        preferred_element_type=jnp.float32,
    )
    return (
        query_term.reshape(queries.shape),
        key_term.reshape(keys.shape),
        value_term.reshape(values.shape),
    )


def general_body(
    tokens,
    pair_lengths,
    joint_weight,
    query_bias,
    value_bias,
    out_weight,
    out_bias,
    first_gain,
    first_shift,
    up_weight,
    up_bias,
    down_weight,
    down_bias,
    second_gain,
    second_shift,
    cotangent,
):
    rows_here, seq_here, width = tokens.shape
    count = lax.axis_size("seq")
    cycle_index = lax.axis_index("seq")
    ends = jnp.cumsum(pair_lengths, axis=1)
    offsets = jnp.arange(seq_here, dtype=jnp.int32)
    own_pairs = pair_index(cycle_index * seq_here + offsets, ends)
    block_shape = (rows_here, seq_here, width)
    flat = tokens.reshape(rows_here * seq_here, width)
    projected = jnp.dot(flat, joint_weight, preferred_element_type=jnp.float32)
    queries = (projected[:, :width] + query_bias).astype(jnp.bfloat16).reshape(block_shape)
    keys = projected[:, width : 2 * width].astype(jnp.bfloat16).reshape(block_shape)
    values = (projected[:, 2 * width :] + value_bias).astype(jnp.bfloat16).reshape(block_shape)
    query_heads = split_heads(queries)
    initial = (
        jnp.full((rows_here, HEADS, seq_here), NEGATIVE, jnp.float32),
        jnp.zeros((rows_here, HEADS, seq_here), jnp.float32),
        jnp.zeros((rows_here, seq_here, HEADS, HEAD_DIM), jnp.float32),
    )
    key_piece = lax.all_gather(keys, "seq", axis=1, tiled=True)
    value_piece = lax.all_gather(values, "seq", axis=1, tiled=True)
    length = key_piece.shape[1]
    block = math.gcd(length, seq_here)

    def one_block(index, inner_state):
        first = index * block
        key_block = lax.dynamic_slice_in_dim(key_piece, first, block, 1)
        value_block = lax.dynamic_slice_in_dim(value_piece, first, block, 1)
        key_pairs = pair_index(first + jnp.arange(block, dtype=jnp.int32), ends)
        return online_block(inner_state, query_heads, own_pairs, key_block, value_block, key_pairs)

    highest, total, summed = lax.fori_loop(0, length // block, one_block, initial)
    log_total = highest + jnp.log(total)
    attended = (
        (summed / jnp.swapaxes(total, 1, 2)[..., None]).astype(jnp.bfloat16).reshape(flat.shape)
    )
    branch = jnp.dot(attended, out_weight, preferred_element_type=jnp.float32) + out_bias
    first_sum = flat.astype(jnp.float32) + branch
    normed, first_back = jax.vjp(layer_norm, first_sum, first_gain, first_shift)
    normed_low = normed.astype(jnp.bfloat16)
    inner = jnp.dot(normed_low, up_weight, preferred_element_type=jnp.float32) + up_bias
    activated_full, gelu_back = jax.vjp(gelu_exact, inner)
    activated = activated_full.astype(jnp.bfloat16)
    feed = jnp.dot(activated, down_weight, preferred_element_type=jnp.float32) + down_bias
    second_sum = normed + feed
    result, second_back = jax.vjp(layer_norm, second_sum, second_gain, second_shift)
    outputs = result.astype(jnp.bfloat16).reshape(tokens.shape)
    second_grad, second_gain_grad, second_shift_grad = second_back(
        cotangent.astype(jnp.float32).reshape(flat.shape)
    )
    feed_grad = second_grad.astype(jnp.bfloat16)
    down_grad = jnp.einsum("ti,tj->ij", activated, feed_grad, preferred_element_type=jnp.float32)
    down_bias_grad = jnp.sum(feed_grad.astype(jnp.float32), axis=0)
    activated_grad = jnp.einsum(
        "tj,ij->ti", feed_grad, down_weight, preferred_element_type=jnp.float32
    )
    inner_grad = gelu_back(activated_grad)[0].astype(jnp.bfloat16)
    up_grad = jnp.einsum("ti,tj->ij", normed_low, inner_grad, preferred_element_type=jnp.float32)
    up_bias_grad = jnp.sum(inner_grad.astype(jnp.float32), axis=0)
    normed_grad = second_grad + jnp.einsum(
        "tj,ij->ti", inner_grad, up_weight, preferred_element_type=jnp.float32
    )
    first_grad, first_gain_grad, first_shift_grad = first_back(normed_grad)
    branch_grad = first_grad.astype(jnp.bfloat16)
    out_grad = jnp.einsum("ti,tj->ij", attended, branch_grad, preferred_element_type=jnp.float32)
    out_bias_grad = jnp.sum(branch_grad.astype(jnp.float32), axis=0)
    attended_grad = jnp.einsum(
        "tj,ij->ti", branch_grad, out_weight, preferred_element_type=jnp.float32
    ).astype(jnp.bfloat16)
    delta = jnp.sum(
        (attended_grad.astype(jnp.float32) * attended.astype(jnp.float32)).reshape(
            rows_here, seq_here, HEADS, HEAD_DIM
        ),
        axis=3,
    )
    delta = jnp.swapaxes(delta, 1, 2)
    attended_grad = attended_grad.reshape(block_shape)
    zeros_block = jnp.zeros(block_shape, jnp.float32)

    def send_key_sums(sums):
        return (
            from_behind(sums[0].astype(jnp.bfloat16), "seq", 1).astype(jnp.float32),
            from_behind(sums[1].astype(jnp.bfloat16), "seq", 1).astype(jnp.float32),
        )

    def key_work(turn, pair_block, sums, query_sum):
        anchor = (cycle_index - turn) % count
        key_pairs = pair_index(anchor * seq_here + offsets, ends)
        query_term, key_term, value_term = tile_terms(
            queries,
            attended_grad,
            log_total,
            delta,
            own_pairs,
            pair_block[0],
            pair_block[1],
            key_pairs,
        )
        return ((sums[0] + key_term, sums[1] + value_term), query_sum + query_term)

    def key_turn(turn, state):
        pair_block, sums, query_sum = state
        sums, query_sum = key_work(turn, pair_block, sums, query_sum)
        sums = send_key_sums(sums)
        pair_block = from_behind((pair_block[0], pair_block[1]), "seq", 1)
        return (pair_block, sums, query_sum)

    pair_block, sums, query_sum = lax.fori_loop(
        0, count - 1, key_turn, ((keys, values), (zeros_block, zeros_block), zeros_block)
    )
    sums, query_sum = key_work(count - 1, pair_block, sums, query_sum)
    key_sum, value_sum = send_key_sums(sums)
    query_low = query_sum.astype(jnp.bfloat16).reshape(flat.shape)
    key_low = key_sum.astype(jnp.bfloat16).reshape(flat.shape)
    value_low = value_sum.astype(jnp.bfloat16).reshape(flat.shape)
    joint_low = jnp.concatenate([query_low, key_low, value_low], axis=1)
    joint_grad = jnp.einsum("ti,tj->ij", flat, joint_low, preferred_element_type=jnp.float32)
    query_bias_grad = jnp.sum(query_low.astype(jnp.float32), axis=0)
    value_bias_grad = jnp.sum(value_low.astype(jnp.float32), axis=0)
    token_grad = first_grad + jnp.einsum(
        "tj,ij->ti", joint_low, joint_weight, preferred_element_type=jnp.float32
    )
    gradients = (
        joint_grad,
        query_bias_grad,
        value_bias_grad,
        out_grad,
        out_bias_grad,
        first_gain_grad,
        first_shift_grad,
        up_grad,
        up_bias_grad,
        down_grad,
        down_bias_grad,
        second_gain_grad,
        second_shift_grad,
    )
    shares = (
        lax.psum_scatter(
            gradients[0].astype(jnp.bfloat16), "seq", scatter_dimension=0, tiled=True
        ).astype(jnp.float32),
        lax.psum_scatter(
            gradients[1].astype(jnp.bfloat16), "seq", scatter_dimension=0, tiled=True
        ).astype(jnp.float32),
        lax.psum_scatter(
            gradients[2].astype(jnp.bfloat16), "seq", scatter_dimension=0, tiled=True
        ).astype(jnp.float32),
        lax.psum_scatter(
            gradients[3].astype(jnp.bfloat16), "seq", scatter_dimension=0, tiled=True
        ).astype(jnp.float32),
        lax.psum_scatter(
            gradients[4].astype(jnp.bfloat16), "seq", scatter_dimension=0, tiled=True
        ).astype(jnp.float32),
        lax.psum_scatter(
            gradients[5].astype(jnp.bfloat16), "seq", scatter_dimension=0, tiled=True
        ).astype(jnp.float32),
        lax.psum_scatter(
            gradients[6].astype(jnp.bfloat16), "seq", scatter_dimension=0, tiled=True
        ).astype(jnp.float32),
        lax.psum_scatter(
            gradients[7].astype(jnp.bfloat16), "seq", scatter_dimension=0, tiled=True
        ).astype(jnp.float32),
        lax.psum_scatter(
            gradients[8].astype(jnp.bfloat16), "seq", scatter_dimension=0, tiled=True
        ).astype(jnp.float32),
        lax.psum_scatter(
            gradients[9].astype(jnp.bfloat16), "seq", scatter_dimension=0, tiled=True
        ).astype(jnp.float32),
        lax.psum_scatter(
            gradients[10].astype(jnp.bfloat16), "seq", scatter_dimension=0, tiled=True
        ).astype(jnp.float32),
        lax.psum_scatter(
            gradients[11].astype(jnp.bfloat16), "seq", scatter_dimension=0, tiled=True
        ).astype(jnp.float32),
        lax.psum_scatter(
            gradients[12].astype(jnp.bfloat16), "seq", scatter_dimension=0, tiled=True
        ).astype(jnp.float32),
    )
    shares = (
        lax.psum(shares[0].astype(jnp.bfloat16), "rows").astype(jnp.float32),
        lax.psum(shares[1].astype(jnp.bfloat16), "rows").astype(jnp.float32),
        lax.psum(shares[2].astype(jnp.bfloat16), "rows").astype(jnp.float32),
        lax.psum(shares[3].astype(jnp.bfloat16), "rows").astype(jnp.float32),
        lax.psum(shares[4].astype(jnp.bfloat16), "rows").astype(jnp.float32),
        lax.psum(shares[5].astype(jnp.bfloat16), "rows").astype(jnp.float32),
        lax.psum(shares[6].astype(jnp.bfloat16), "rows").astype(jnp.float32),
        lax.psum(shares[7].astype(jnp.bfloat16), "rows").astype(jnp.float32),
        lax.psum(shares[8].astype(jnp.bfloat16), "rows").astype(jnp.float32),
        lax.psum(shares[9].astype(jnp.bfloat16), "rows").astype(jnp.float32),
        lax.psum(shares[10].astype(jnp.bfloat16), "rows").astype(jnp.float32),
        lax.psum(shares[11].astype(jnp.bfloat16), "rows").astype(jnp.float32),
        lax.psum(shares[12].astype(jnp.bfloat16), "rows").astype(jnp.float32),
    )
    return (outputs, token_grad.reshape(tokens.shape)) + tuple(shares)


WIDTH = HEADS * HEAD_DIM
HALF = WIDTH // 2
FF = 4 * WIDTH
BLOCK = 128
OWN = 2 * BLOCK
LANES = 128
PAIRS_OF_HEADS = HALF // LANES
JOINT_ROWS = 80
JOINT_FIRST = 48
JOINT_SECOND = JOINT_ROWS - JOINT_FIRST
UP_ROWS = 128
DOWN_ROWS = 96
EXT = OWN + 16
DOWN_SENT = 2 * DOWN_ROWS
FLOAT = jnp.float32
LOW = jnp.bfloat16
AXES = ("seq", "rows")


def kernel_params(megabytes):
    return pltpu.CompilerParams(vmem_limit_bytes=megabytes << 20)


def shaped(shape, kind):
    return jax.ShapeDtypeStruct(shape, kind)


def whole(shape):
    return pl.BlockSpec(shape, lambda *_: (0,) * len(shape))


def cost(flops, moved, exps=0):
    return pl.CostEstimate(flops=1024, bytes_accessed=1024, transcendentals=0)


def dot(left, right):
    return lax.dot_general(left, right, (((1,), (0,)), ((), ())), preferred_element_type=FLOAT)


def dot_nt(left, right):
    return lax.dot_general(left, right, (((1,), (1,)), ((), ())), preferred_element_type=FLOAT)


def call(kernel, name, place, inputs, outputs, scratch=(), grid=(1,), scalars=(), after=(), megabytes=28, work=None, aliases=()):
    prefetch = 1 + len(scalars)
    given, made = len(inputs), len(outputs)

    def ordered(*refs):
        first = prefetch + given
        mark = refs[first + len(after) + made]
        mark[...] = jnp.zeros_like(mark)
        kernel(*refs[:first], *refs[first + len(after) : first + len(after) + made], *refs[first + len(after) + made + 1 :])

    results = pl.pallas_call(
        ordered,
        grid_spec=pltpu.PrefetchScalarGridSpec(
            num_scalar_prefetch=prefetch,
            grid=grid,
            in_specs=[spec for _, spec in inputs] + [pl.BlockSpec(memory_space=pl.ANY)] * len(after),
            out_specs=[spec for _, _, spec in outputs] + [whole((8, LANES))],
            scratch_shapes=list(scratch),
        ),
        out_shape=[shaped(shape, kind) for shape, kind, _ in outputs] + [shaped((8, LANES), FLOAT)],
        compiler_params=kernel_params(megabytes),
        cost_estimate=work,
        input_output_aliases={prefetch + source: target for source, target in aliases},
        name=name,
    )(place, *scalars, *[array for array, _ in inputs], *after)
    return results[:-1], results[-1]


def plain(array):
    return array, whole(array.shape)


def made(shape, kind):
    return shape, kind, whole(shape)


def device_at(z, y, x, c):
    return ((z * 2 + y) * 2 + x) * 2 + c


def permute(value, target):
    pairs = []
    for z in range(4):
        for y in range(2):
            for x in range(2):
                for c in range(2):
                    pairs.append((device_at(z, y, x, c), device_at(*target(z, y, x, c))))
    return lax.ppermute(value, AXES, pairs)


def core_swap(value):
    return permute(value, lambda z, y, x, c: (z, y, x, 1 - c))


def x_swap(value):
    return permute(value, lambda z, y, x, c: (z, y, 1 - x, c))


def y_swap(value):
    return permute(value, lambda z, y, x, c: (z, 1 - y, x, c))


def z_swap(value, bits):
    return permute(value, lambda z, y, x, c: (z ^ bits, y, x, c))


def row_swap(value, second):
    return permute(value, lambda z, y, x, c: (2 * c + (z % 2 ^ second), y, x, z // 2))


def first_positions(place):
    z, y, c = place[0], place[1], place[3]
    bases = []
    for core, line in ((c, y), (1 - c, y), (c, 1 - y), (1 - c, 1 - y)):
        for second in (0, 1):
            parity = z % 2
            parity = 1 - parity if second else parity
            bases.append((2 * (2 * core + parity) + line) * BLOCK)
    return bases


def pair_ends(place, own_lengths, peer_lengths):
    z, c = place[0], place[3]
    here = (z // 2) == c
    line = z % 2
    ends, end = [], 0
    for pair in range(own_lengths.shape[1]):
        end = end + jnp.where(here, own_lengths[line, pair], peer_lengths[line, pair])
        ends.append(end)
    return ends


def pairs_along(base, ends, axis):
    shape = (8, BLOCK) if axis == 1 else (BLOCK, LANES)
    position = base + lax.broadcasted_iota(jnp.int32, shape, axis)
    ids = jnp.zeros(shape, jnp.int32)
    for end in ends:
        ids = ids + (position >= end).astype(jnp.int32)
    return ids


def head_mask(rows):
    return lax.broadcasted_iota(jnp.int32, (rows, LANES), 1) < HEAD_DIM


def columns_kernel(place, columns, query_bias, value_bias, out, query_row, value_row):
    out[0] = columns[...]
    query_row[...] = query_bias[...]
    value_row[...] = value_bias[...]


def own_columns(place, joint_weight, query_bias, value_bias):
    half_row = pl.BlockSpec((1, HALF), lambda i, place: (0, place[3]))
    results, _ = call(
        columns_kernel,
        "own_columns",
        place,
        [
            (joint_weight, pl.BlockSpec((WIDTH, HALF), lambda i, place: (0, 2 * i + place[3]))),
            (row_of(query_bias), half_row),
            (row_of(value_bias), half_row),
        ],
        [((3, WIDTH, HALF), LOW, pl.BlockSpec((1, WIDTH, HALF), lambda i, place: (i, 0, 0)))]
        + [made((1, HALF), FLOAT)] * 2,
        grid=(3,),
        work=cost(1e6, 4e6),
    )
    return results


def first_attention_kernel(
    place, own_lengths, peer_lengths, t0, t1, t2, t3, columns, qb, vb, q_out, k_out, v_out, summed, stats, bias
):
    bases = first_positions(place)
    ends = pair_ends(place, own_lengths, peer_lengths)
    tokens = jnp.concatenate([block[...] for block in (t0, t1, t2, t3)], axis=0)
    queries = dot(tokens, columns[0]) + qb[...]
    q_out[...] = (queries.astype(LOW).astype(FLOAT) * HEAD_DIM**-0.5).astype(LOW)
    k_out[...] = dot(tokens, columns[1]).astype(LOW)
    v_out[...] = (dot(tokens, columns[2]) + vb[...]).astype(LOW)
    fill_bias(bias, bases[:4], bases[:4], ends)
    stats[...] = jnp.zeros_like(stats)
    for pair in range(PAIRS_OF_HEADS):
        lanes = pl.ds(pair * LANES, LANES)
        scores = masked_scores(k_out[:, lanes], q_out[:, lanes], bias)
        highest = jnp.max(scores, axis=0, keepdims=True)
        weights = jnp.exp(scores - highest)
        summed[pair] = dot(turned(v_out[:, lanes]), weights.astype(LOW))
        stats[2 * pair : 2 * pair + 1, :] = highest
        stats[2 * pair + 1 : 2 * pair + 2, :] = column_sum(weights)


def turned(array):
    return jnp.transpose(array.astype(FLOAT)).astype(LOW)


def masked_scores(keys, queries, bias):
    mask = bias[...]
    chosen = jnp.concatenate(halves_of(queries), axis=0)
    return dot_nt(keys, chosen) + jnp.concatenate([mask, mask], axis=1)


def fill_bias(bias, query_bases, key_bases, ends):
    key_ids = [pairs_along(base, ends, 1)[0:1] for base in key_bases]
    for i, base in enumerate(query_bases):
        query_ids = pairs_along(base, ends, 0)
        for j in range(len(key_bases)):
            bias[pl.ds(i * BLOCK, BLOCK), pl.ds(j * BLOCK, BLOCK)] = jnp.where(query_ids == key_ids[j], 0.0, NEGATIVE)


def halves_of(array):
    left = head_mask(array.shape[0])
    zeros = jnp.zeros_like(array)
    return jnp.where(left, array, zeros), jnp.where(left, zeros, array)


def first_attention(place, lengths, blocks, columns, query_bias, value_bias, after=()):
    return call(
        first_attention_kernel,
        "first_attention",
        place,
        [plain(array) for array in (*blocks, columns, query_bias, value_bias)],
        [made((512, HALF), LOW)] * 3 + [made((PAIRS_OF_HEADS, LANES, 1024), FLOAT), made((8, 1024), FLOAT)],
        scratch=[pltpu.VMEM((512, 512), FLOAT)],
        scalars=lengths,
        after=after,
        work=cost(4e9, 8e6, 3e6),
    )


def attention_kernel(
    place, own_lengths, peer_lengths, t0, t1, t2, t3, columns, vb, q, summed, stats,
    att_out, k_out, v_out, log_out, bias,
):
    bases = first_positions(place)
    ends = pair_ends(place, own_lengths, peer_lengths)
    tokens = jnp.concatenate([block[...] for block in (t0, t1, t2, t3)], axis=0)
    k_out[...] = dot(tokens, columns[1]).astype(LOW)
    v_out[...] = (dot(tokens, columns[2]) + vb[...]).astype(LOW)
    fill_bias(bias, bases[4:], bases[:4], ends)
    log_out[...] = jnp.zeros_like(log_out)
    top = lax.broadcasted_iota(jnp.int32, (LANES, 512), 0) < HEAD_DIM
    for pair in range(PAIRS_OF_HEADS):
        lanes = pl.ds(pair * LANES, LANES)
        scores = masked_scores(k_out[:, lanes], q[:, lanes], bias)
        before = stats[2 * pair : 2 * pair + 1, :]
        highest = jnp.maximum(before, jnp.max(scores, axis=0, keepdims=True))
        weights = jnp.exp(scores - highest)
        shrink = jnp.exp(before - highest)
        sums = column_sum(weights) + shrink * stats[2 * pair + 1 : 2 * pair + 2, :]
        total = (dot(turned(v_out[:, lanes]), weights.astype(LOW)) + shrink * summed[pair]) / sums
        att_out[:, lanes] = jnp.transpose(jnp.where(top, total[:, 0:512], total[:, 512:])).astype(LOW)
        logs = highest + jnp.log(sums)
        log_out[2 * pair : 2 * pair + 1, :] = logs[:, 0:512]
        log_out[2 * pair + 1 : 2 * pair + 2, :] = logs[:, 512:]


def attention(place, lengths, blocks, columns, value_bias, q, summed, stats, after=()):
    return call(
        attention_kernel,
        "attention",
        place,
        [plain(array) for array in (*blocks, columns, value_bias, q, summed, stats)],
        [made((512, HALF), LOW)] * 3 + [made((8, 512), FLOAT)],
        scratch=[pltpu.VMEM((512, 512), FLOAT)],
        scalars=lengths,
        after=after,
        work=cost(4e9, 8e6, 3e6),
    )


def centred_norm(value):
    mean = jnp.mean(value, axis=-1, keepdims=True)
    centred = value - mean
    spread = jnp.mean(centred * centred, axis=-1, keepdims=True)
    inverse = lax.rsqrt(spread + EPSILON)
    return centred * inverse, inverse


def norm_back(grad, unit, inverse):
    mean = jnp.mean(grad, axis=-1, keepdims=True)
    along = jnp.mean(grad * unit, axis=-1, keepdims=True)
    return (grad - mean - unit * along) * inverse


def column_sum(value):
    return jnp.sum(value, axis=0, keepdims=True)


def forward_kernel(
    place, att, att_got, wo_own, wo_other, out_bias, x0, x1, gain1, shift1, up, up_bias, down,
    down_bias, gain2, shift2, cot0, cot1,
    result0, result1, feed_ext, second_grad, act_keep, act_send, slope, unit1, inverse1, normed_low, normed_t, att_t, sums,
    act_t,
):
    c = place[3]
    tokens = jnp.concatenate([x0[...], x1[...]], axis=0).astype(FLOAT)
    att_own, att_other = att[0:OWN], att_got[OWN:]
    branch = dot(att_own, wo_own[...]) + dot(att_other, wo_other[...]) + out_bias[...]
    unit, inverse = centred_norm(tokens + branch)
    unit1[...] = unit
    inverse1[...] = jnp.broadcast_to(inverse, (OWN, LANES))
    normed = unit * gain1[...] + shift1[...]
    low = normed.astype(LOW)
    normed_low[...] = low
    normed_t[...] = jnp.transpose(normed).astype(LOW)
    mine = pl.ds(pl.multiple_of(c * HALF, HALF), HALF)
    other = pl.ds(pl.multiple_of((1 - c) * HALF, HALF), HALF)
    att_t[mine, :] = jnp.transpose(att[...].astype(FLOAT)).astype(LOW)
    att_t[other, 0:OWN] = jnp.transpose(att_other.astype(FLOAT)).astype(LOW)
    att_t[other, OWN:] = jnp.transpose(att_got[0:OWN].astype(FLOAT)).astype(LOW)
    inner = dot(low, up[...]) + up_bias[...]
    below = 0.5 + 0.5 * lax.erf(inner * math.sqrt(0.5))
    density = jnp.exp(inner * inner * -0.5) * (1.0 / math.sqrt(2.0 * math.pi))
    activated = inner * below
    slope[...] = (below + inner * density).astype(LOW)
    act_t[...] = jnp.transpose(activated).astype(LOW).reshape(16, 2, DOWN_ROWS, OWN)
    act_keep[...] = act_t[:, c]
    act_send[...] = act_t[:, 1 - c]
    feed = dot(activated.astype(LOW), down[...])
    unit, inverse = centred_norm(normed + feed + down_bias[...])
    result = (unit * gain2[...] + shift2[...]).astype(LOW)
    result0[...] = result[0:BLOCK]
    result1[...] = result[BLOCK:]
    cotangent = jnp.concatenate([cot0[0:BLOCK], cot1[0:BLOCK]], axis=0).astype(FLOAT)
    grad = norm_back(cotangent * gain2[...], unit, inverse)
    second_grad[...] = grad
    low_grad = grad.astype(LOW)
    rows = jnp.concatenate(
        [
            column_sum(cotangent * unit),
            column_sum(cotangent),
            column_sum(low_grad.astype(FLOAT)),
            jnp.zeros((5, WIDTH), FLOAT),
        ],
        axis=0,
    )
    sums[...] = rows
    feed_ext[0:OWN] = low_grad
    feed_ext[OWN:] = jnp.concatenate([rows, jnp.zeros_like(rows)], axis=0).astype(LOW)


def row_of(vector):
    return vector.reshape(1, vector.shape[0])


def forward(place, att, att_got, tokens, cotangents, weights, after=()):
    chunk = FF

    def vector(name):
        return plain(row_of(weights[name]))

    units = ((16, DOWN_ROWS, OWN), LOW, pl.BlockSpec((16, DOWN_ROWS, OWN), lambda i, place: (i, 0, 0)))
    return call(
        forward_kernel,
        "forward",
        place,
        [
            plain(att),
            plain(att_got),
            (weights["out"], pl.BlockSpec((HALF, WIDTH), lambda i, place: (place[3], 0))),
            (weights["out"], pl.BlockSpec((HALF, WIDTH), lambda i, place: (1 - place[3], 0))),
            vector("out_bias"), plain(tokens[0]), plain(tokens[1]), vector("gain1"), vector("shift1"),
            (weights["up"], pl.BlockSpec((WIDTH, chunk), lambda i, place: (0, i))),
            (row_of(weights["up_bias"]), pl.BlockSpec((1, chunk), lambda i, place: (0, i))),
            (weights["down"], pl.BlockSpec((chunk, WIDTH), lambda i, place: (i, 0))),
            vector("down_bias"), vector("gain2"), vector("shift2"), plain(cotangents[0]), plain(cotangents[1]),
        ],
        [
            made((BLOCK, WIDTH), LOW), made((BLOCK, WIDTH), LOW), made((EXT, WIDTH), LOW),
            made((OWN, WIDTH), FLOAT), units, units,
            ((OWN, FF), LOW, pl.BlockSpec((OWN, chunk), lambda i, place: (0, i))),
            made((OWN, WIDTH), FLOAT), made((OWN, LANES), FLOAT), made((OWN, WIDTH), LOW),
            made((WIDTH, OWN), LOW), made((WIDTH, 512), LOW), made((8, WIDTH), FLOAT),
        ],
        scratch=[pltpu.VMEM((16, 2, DOWN_ROWS, OWN), LOW)],
        after=after,
        work=cost(2.7e9, 20e6, 2e6),
    )


def split_units(place, units, px_send, px, qy_send, qy):
    y, x = place[1], place[2]
    half = units.shape[2] // 2
    for line in range(2):
        px[0, line] = units[line, x, 0:half]
        px_send[0, line] = units[line, 1 - x, 0:half]
    for side in range(2):
        qy[0, side] = units[y, side, half:]
        qy_send[0, side] = units[1 - y, side, half:]


def unit_outputs(rows, width):
    shape = (4, 2, rows // 2, width)
    return [(shape, LOW, pl.BlockSpec((1,) + shape[1:], lambda i, place: (i, 0, 0, 0)))] * 4


def down_kernel(place, act, act_got, feed, feed_got, px_send, px, qy_send, qy, units):
    shape = (4 * DOWN_ROWS, OWN)
    total = dot(act[...].reshape(shape), feed[0:OWN]) + dot(act_got[...].reshape(shape), feed_got[0:OWN])
    units[...] = total.astype(LOW).reshape(units.shape)
    split_units(place, units, px_send, px, qy_send, qy)


def down_units(place, act, act_got, feed, feed_got, after=()):
    block = pl.BlockSpec((4, DOWN_ROWS, OWN), lambda i, place: (i, 0, 0))
    return call(
        down_kernel,
        "down_units",
        place,
        [(act, block), (act_got, block), plain(feed), plain(feed_got)],
        unit_outputs(DOWN_ROWS, WIDTH),
        scratch=[pltpu.VMEM((2, 2, DOWN_ROWS, WIDTH), LOW)],
        grid=(4,),
        after=after,
        work=cost(0.6e9, 3.5e6),
    )


def backward_kernel(
    place, feed_ext, slope, up, down, second_grad, unit1, inverse1, gain1, wo_own, wo_other,
    inner0, inner1, send0, send1, first_grad, branch_own, back_own, misc, sums,
    inner, branch,
):
    c = place[3]
    grad = (dot_nt(feed_ext[0:OWN], down[...]) * slope[...].astype(FLOAT)).astype(LOW)
    inner[...] = grad
    for target, index in ((inner0, c), (inner1, 2 + c), (send0, 1 - c), (send1, 3 - c)):
        target[...] = inner[:, pl.ds(pl.multiple_of(index * WIDTH, LANES), WIDTH)]
    inner_sum = column_sum(grad.astype(FLOAT))
    total = second_grad[...] + dot_nt(grad, up[...])
    unit = unit1[...]
    grad1 = norm_back(total * gain1[...], unit, inverse1[:, 0:1])
    first_grad[...] = grad1
    low = grad1.astype(LOW)
    branch[...] = low
    rows = jnp.concatenate(
        [
            column_sum(total * unit),
            column_sum(total),
            column_sum(low.astype(FLOAT)),
            jnp.zeros((1, WIDTH), FLOAT),
        ]
        + [inner_sum[:, index * WIDTH : (index + 1) * WIDTH] for index in range(4)],
        axis=0,
    )
    sums[...] = rows
    branch_own[...] = branch[:, pl.ds(pl.multiple_of(c * HALF, LANES), HALF)]
    back_own[...] = dot_nt(low, wo_own[...]).astype(LOW)
    misc[0:OWN, 0:HALF] = branch[:, pl.ds(pl.multiple_of((1 - c) * HALF, LANES), HALF)]
    misc[0:OWN, HALF:] = dot_nt(low, wo_other[...]).astype(LOW)
    misc[OWN:] = jnp.concatenate([rows, jnp.zeros_like(rows)], axis=0).astype(LOW)


def backward(place, feed_ext, slope, second_grad, unit1, inverse1, weights, after=()):
    chunk = FF
    return call(
        backward_kernel,
        "backward",
        place,
        [
            plain(feed_ext),
            (slope, pl.BlockSpec((OWN, chunk), lambda i, place: (0, i))),
            (weights["up"], pl.BlockSpec((WIDTH, chunk), lambda i, place: (0, i))),
            (weights["down"], pl.BlockSpec((chunk, WIDTH), lambda i, place: (i, 0))),
            plain(second_grad), plain(unit1), plain(inverse1), plain(row_of(weights["gain1"])),
            (weights["out"], pl.BlockSpec((HALF, WIDTH), lambda i, place: (place[3], 0))),
            (weights["out"], pl.BlockSpec((HALF, WIDTH), lambda i, place: (1 - place[3], 0))),
        ],
        [made((OWN, WIDTH), LOW)] * 4
        + [
            made((OWN, WIDTH), FLOAT), made((OWN, HALF), LOW), made((OWN, HALF), LOW), made((EXT, WIDTH), LOW),
            made((8, WIDTH), FLOAT),
        ],
        scratch=[pltpu.VMEM((OWN, FF), LOW), pltpu.VMEM((OWN, WIDTH), LOW)],
        after=after,
        work=cost(2.7e9, 16e6),
    )


def up_kernel(
    place, normed_t, normed_got, inner0, inner1, got0, got1, att_t, branch, misc, sums0, sums1, feed_got,
    x_send, y_send, px, qy, units, normed_got_t,
):
    z = pl.program_id(0)
    y, x = place[1], place[2]

    @pl.when(z == 0)
    def _():
        normed_got_t[...] = jnp.transpose(normed_got[...].astype(FLOAT)).astype(LOW)

    theirs = normed_got_t[pl.ds(pl.multiple_of(z * 192, 32), 192), :]
    outer = dot(att_t[:, 0:OWN], branch[...]) + dot(att_t[:, OWN:], misc[0:OWN, 0:HALF])
    for side, inner, got, sums, pair in ((0, inner0, got0, sums0, feed_got), (1, inner1, got1, sums1, misc)):
        grad = dot(normed_t[...], inner[...]) + dot(theirs, got[...])
        vectors = sums[...] + pair[OWN:].astype(FLOAT)[0:8]
        for line in range(2):
            first = line * 96 + side * 48
            rest = jnp.concatenate([outer[first : first + 24], outer[first + 24 : first + 48]], axis=1)
            units[line, side] = jnp.concatenate(
                [grad[line * 96 : line * 96 + 96], rest, vectors], axis=0
            ).astype(LOW)
    half = UP_ROWS // 2
    for index in range(2):
        rows = pl.ds(pl.multiple_of(DOWN_SENT + (z * 2 + index) * half, half), half)
        px[0, index] = units[index, x, 0:half]
        x_send[rows, :] = units[index, 1 - x, 0:half]
        qy[0, index] = units[y, index, half:]
        y_send[rows, :] = units[1 - y, index, half:]


def up_units(place, normed_t, normed_got, inner, got, att_t, branch, misc, sums0, sums1, feed_got, after=()):
    rows = pl.BlockSpec((192, OWN), lambda i, place: (i, 0))
    return call(
        up_kernel,
        "up_units",
        place,
        [
            (normed_t, rows), plain(normed_got), plain(inner[0]), plain(inner[1]), plain(got[0]), plain(got[1]),
            (att_t, pl.BlockSpec((192, 512), lambda i, place: (i, 0))),
            plain(branch), plain(misc), plain(sums0), plain(sums1), plain(feed_got),
        ],
        [made((DOWN_SENT + 4 * UP_ROWS, WIDTH), LOW)] * 2 + unit_outputs(UP_ROWS, WIDTH)[:2],
        scratch=[pltpu.VMEM((2, 2, UP_ROWS, WIDTH), LOW), pltpu.VMEM((WIDTH, OWN), LOW)],
        grid=(4,),
        after=after,
        work=cost(0.9e9, 5e6),
    )


def attention_back_kernel(
    place, own_lengths, peer_lengths, q, k0, k1, v0, v1, log_total, att, back0, misc,
    dq_out, dk_out, dv_out, bias,
):
    bases = first_positions(place)
    ends = pair_ends(place, own_lengths, peer_lengths)
    query_ids = [pairs_along(base, ends, 1)[0:1] for base in bases[:4]]
    for j in range(8):
        key_ids = pairs_along(bases[j], ends, 0)
        for i in range(4):
            bias[pl.ds(j * BLOCK, BLOCK), pl.ds(i * BLOCK, BLOCK)] = jnp.where(
                key_ids == query_ids[i], 0.0, NEGATIVE
            )

    def one_pair(pair, carry):
        lanes = pl.ds(pl.multiple_of(pair * LANES, LANES), LANES)
        keys = jnp.concatenate([k0[:, lanes], k1[:, lanes]], axis=0)
        values = jnp.concatenate([v0[:, lanes], v1[:, lanes]], axis=0)
        keys_t = turned(keys)
        key_grad = jnp.zeros((1024, LANES), FLOAT)
        value_grad = jnp.zeros((1024, LANES), FLOAT)
        far = pl.ds(pl.multiple_of(HALF + pair * LANES, LANES), LANES)
        for part, back in ((0, back0[:, lanes]), (1, misc[0:OWN, far])):
            rows = pl.ds(part * OWN, OWN)
            product = jnp.transpose(back.astype(FLOAT) * att[rows, lanes].astype(FLOAT))
            delta = jnp.concatenate([column_sum(product[0:HEAD_DIM]), column_sum(product[HEAD_DIM:])], axis=1)
            logs = jnp.concatenate(
                [log_total[pl.ds(2 * pair, 1), rows], log_total[pl.ds(2 * pair + 1, 1), rows]], axis=1
            )
            chosen = jnp.concatenate(halves_of(q[rows, lanes]), axis=0)
            grads = jnp.concatenate(halves_of(back), axis=0)
            mask = bias[:, rows]
            weights = jnp.exp(dot_nt(keys, chosen) + jnp.concatenate([mask, mask], axis=1) - logs)
            score_grad = (weights * (dot_nt(values, grads) - delta)).astype(LOW)
            value_grad = value_grad + dot(weights.astype(LOW), grads)
            key_grad = key_grad + dot(score_grad, chosen)
            both = dot(keys_t, score_grad)
            query_grad_t = jnp.concatenate([both[0:HEAD_DIM, 0:OWN], both[HEAD_DIM:, OWN:]], axis=0)
            dq_out[rows, lanes] = (jnp.transpose(query_grad_t) * HEAD_DIM**-0.5).astype(LOW)
        dk_out[:, lanes] = key_grad.astype(LOW)
        dv_out[:, lanes] = value_grad.astype(LOW)
        return carry

    lax.fori_loop(0, PAIRS_OF_HEADS, one_pair, 0)


def attention_back(place, lengths, q, keys, values, log_total, att, back_own, misc, after=()):
    return call(
        attention_back_kernel,
        "attention_back",
        place,
        [plain(array) for array in (q, *keys, *values, log_total, att, back_own, misc)],
        [made((512, HALF), LOW), made((1024, HALF), LOW), made((1024, HALF), LOW)],
        scratch=[pltpu.VMEM((1024, 512), FLOAT)],
        scalars=lengths,
        after=after,
        work=cost(7e9, 6e6, 3e6),
    )


def token_kernel(place, dq, dk, dv, columns, own, own_send, far, far_send):
    for part, target in enumerate((own, own_send, far, far_send)):
        rows = pl.ds(part * OWN, OWN)
        total = dot_nt(dk[rows, :], columns[1]) + dot_nt(dv[rows, :], columns[2])
        if part < 2:
            total = total + dot_nt(dq[rows, :], columns[0])
        target[...] = total.astype(LOW)


def token_parts(place, dq, dk, dv, columns, after=()):
    return call(
        token_kernel,
        "token_parts",
        place,
        [plain(dq), plain(dk), plain(dv), plain(columns)],
        [made((OWN, WIDTH), LOW)] * 4,
        after=after,
        work=cost(1.5e9, 5e6),
    )


def token_last_kernel(place, own, own_got, across, first_grad, token0, token1):
    total = own[...].astype(FLOAT) + own_got[...].astype(FLOAT) + across[8 * JOINT_SECOND :].astype(FLOAT) + first_grad[...]
    total = total.astype(LOW)
    token0[...] = total[0:BLOCK]
    token1[...] = total[BLOCK:]


def token_last(place, arrays, after=()):
    return call(
        token_last_kernel,
        "token_last",
        place,
        [plain(array) for array in arrays],
        [made((BLOCK, WIDTH), LOW)] * 2,
        after=after,
        work=cost(1e6, 2e6),
    )


def back_rows_kernel(place, done0, done1, back0, back1, outputs, token_grad):
    odd = place[0] % 2
    outputs[odd] = done0[...]
    outputs[1 - odd] = done1[...]
    token_grad[odd] = back0[...].astype(FLOAT)
    token_grad[1 - odd] = back1[...].astype(FLOAT)


def back_rows(place, done, back, after=()):
    return call(
        back_rows_kernel,
        "back_rows",
        place,
        [plain(array) for array in (*done, *back)],
        [made((2, BLOCK, WIDTH), LOW), made((2, BLOCK, WIDTH), FLOAT)],
        after=after,
        work=cost(1e6, 2e6),
    )


def joint_kernel(
    place, t0, t1, t2, t3, t4, t5, t6, t7, dq, dk, dv, far, far_got, px_send, px, qy_send, qy, tokens_t, units
):
    y, x = place[1], place[2]
    qy_send[pl.ds(8 * JOINT_SECOND, OWN), :] = added(far[...], far_got[...])
    for index, block in enumerate((t0, t1, t2, t3, t4, t5, t6, t7)):
        tokens_t[:, pl.ds(index * BLOCK, BLOCK)] = jnp.transpose(block[...].astype(FLOAT)).astype(LOW)
    biases = jnp.concatenate([column_sum(dq[...].astype(FLOAT)), column_sum(dv[...].astype(FLOAT))], axis=1)
    biases = jnp.concatenate([biases, jnp.zeros((7, WIDTH), FLOAT)], axis=0)
    for z in range(4):
        rows = pl.ds(z * 192, 192)
        query = dot(tokens_t[rows, 0:512], dq[...])
        key = dot(tokens_t[rows, :], dk[...])
        value = dot(tokens_t[rows, :], dv[...])
        for line in range(2):
            for side in range(2):
                at = line * 96 + side * 48
                units[line, side, 0:JOINT_FIRST] = jnp.concatenate(
                    [query[at : at + 48], key[at : at + 48]], axis=1
                ).astype(LOW)
                rest = jnp.concatenate([value[at : at + 24], value[at + 24 : at + 48]], axis=1)
                units[line, side, JOINT_FIRST:] = jnp.concatenate([rest, biases], axis=0).astype(LOW)
        for line in range(2):
            px[z, line] = units[line, x, 0:JOINT_FIRST]
            px_send[z, line] = units[line, 1 - x, 0:JOINT_FIRST]
        for side in range(2):
            qy[z, side] = units[y, side, JOINT_FIRST:]
            qy_send[pl.ds((z * 2 + side) * JOINT_SECOND, JOINT_SECOND), :] = units[1 - y, side, JOINT_FIRST:]


def joint_units(place, blocks, dq, dk, dv, far, far_got, after=()):
    first, second = made((4, 2, JOINT_FIRST, WIDTH), LOW), made((4, 2, JOINT_SECOND, WIDTH), LOW)
    return call(
        joint_kernel,
        "joint_units",
        place,
        [plain(array) for array in (*blocks, dq, dk, dv, far, far_got)],
        [first, first, made((8 * JOINT_SECOND + OWN, WIDTH), LOW), second],
        scratch=[pltpu.VMEM((WIDTH, 1024), LOW), pltpu.VMEM((2, 2, JOINT_ROWS, WIDTH), LOW)],
        after=after,
        work=cost(1.5e9, 6e6),
    )


def added(left, right):
    return (left.astype(FLOAT) + right.astype(FLOAT)).astype(LOW)


def down_pair_kernel(place, px, px_got, qy, qy_got, x_in, y_in, x_send, y_send, p, q):
    y, x = place[1], place[2]
    p[0] = added(px[0, y], px_got[0, y])
    y_send[...] = added(px[0, 1 - y], px_got[0, 1 - y])
    q[0] = added(qy[0, x], qy_got[0, x])
    x_send[...] = added(qy[0, 1 - x], qy_got[0, 1 - x])


def down_pair_stage(place, arrays, x_send, y_send, after=()):
    half = DOWN_ROWS // 2
    block = pl.BlockSpec((1, 2, half, WIDTH), lambda i, place: (i, 0, 0, 0))
    sent = (x_send.shape, LOW, pl.BlockSpec((half, WIDTH), lambda i, place: (i, 0)))
    kept = ((4, half, WIDTH), LOW, pl.BlockSpec((1, half, WIDTH), lambda i, place: (i, 0, 0)))
    anywhere = pl.BlockSpec(memory_space=pl.ANY)
    return call(
        down_pair_kernel,
        "down_pair_stage",
        place,
        [(array, block) for array in arrays] + [(x_send, anywhere), (y_send, anywhere)],
        [sent, sent, kept, kept],
        grid=(4,),
        after=after,
        work=cost(1e6, 1e7),
        aliases=((4, 0), (5, 1)),
    )


def second_kernel(
    place, x_got, y_got, px, qy, down_p, down_q, x_send, y_send, p, q, down_send, down_keep
):
    z_here, y, x = place[0], place[1], place[2]
    half = UP_ROWS // 2
    for z in range(4):
        for got, have, own, keep, send in ((x_got, px, y, p, y_send), (y_got, qy, x, q, x_send)):
            at = DOWN_SENT + z * UP_ROWS
            mine = pl.ds(pl.multiple_of(at + own * half, half), half)
            other = pl.ds(pl.multiple_of(at + (1 - own) * half, half), half)
            keep[z] = added(have[z, own], got[mine, :])
            send[pl.ds(z * half, half), :] = added(have[z, 1 - own], got[other, :])
    low = z_here % 2
    small = DOWN_ROWS // 2
    for target, parity in ((down_keep, low), (down_send, 1 - low)):
        for high in range(2):
            index = 2 * high + parity
            rows = pl.ds(pl.multiple_of(index * small, small), small)
            target[high, 0:small] = added(down_p[index], y_got[rows, :])
            target[high, small:] = added(down_q[index], x_got[rows, :])


def second_stage(place, arrays, after=()):
    kept = made((4, UP_ROWS // 2, WIDTH), LOW)
    down = made((2, DOWN_ROWS, WIDTH), LOW)
    return call(
        second_kernel,
        "second_stage",
        place,
        [plain(array) for array in arrays],
        [made((OWN, WIDTH), LOW), made((OWN, WIDTH), LOW), kept, kept, down, down],
        after=after,
        work=cost(1e6, 1e7),
    )


def joint_pair_kernel(place, px, px_got, qy, qy_got, x_send, y_send, p, q):
    y, x = place[1], place[2]
    for z in range(4):
        p[z] = added(px[z, y], px_got[z, y])
        y_send[z] = added(px[z, 1 - y], px_got[z, 1 - y])


        def from_y(side):
            return qy_got[pl.ds(pl.multiple_of((z * 2 + side) * JOINT_SECOND, 32), JOINT_SECOND), :]

        q[z] = added(qy[z, x], from_y(x))
        x_send[z] = added(qy[z, 1 - x], from_y(1 - x))


def joint_pair_stage(place, arrays, after=()):
    first, second = made((4, JOINT_FIRST, WIDTH), LOW), made((4, JOINT_SECOND, WIDTH), LOW)
    return call(
        joint_pair_kernel,
        "joint_pair_stage",
        place,
        [plain(array) for array in arrays],
        [second, first, first, second],
        after=after,
        work=cost(1e6, 1e7),
    )


def up_line_kernel(place, x_got, y_got, p, q, down_two, down_got, send, keep, down_send, down_keep):
    low, high_here = place[0] % 2, place[0] // 2
    half = UP_ROWS // 2
    for target, parity in ((keep, low), (send, 1 - low)):
        for high in range(2):
            index = 2 * high + parity
            rows = pl.ds(pl.multiple_of(index * half, half), half)
            target[high, 0:half] = added(p[index], y_got[rows, :])
            target[high, half:] = added(q[index], x_got[rows, :])
    down_keep[...] = added(down_two[high_here], down_got[high_here])
    down_send[...] = added(down_two[1 - high_here], down_got[1 - high_here])


def up_line_stage(place, arrays, after=()):
    return call(
        up_line_kernel,
        "up_line_stage",
        place,
        [plain(array) for array in arrays],
        [made((2, UP_ROWS, WIDTH), LOW)] * 2 + [made((DOWN_ROWS, WIDTH), LOW)] * 2,
        after=after,
        work=cost(1e6, 1e7),
    )


def joint_line_kernel(place, x_got, y_got, p, q, keep, one, two, three):
    low, high = place[0] % 2, place[0] // 2
    for target, index in (
        (keep, 2 * high + low), (one, 2 * high + 1 - low), (two, 2 * (1 - high) + low), (three, 2 * (1 - high) + 1 - low)
    ):
        target[0:JOINT_FIRST] = added(p[index], y_got[index])
        target[JOINT_FIRST:] = added(q[index], x_got[index])


def joint_line_stage(place, arrays, after=()):
    return call(
        joint_line_kernel,
        "joint_line_stage",
        place,
        [plain(array) for array in arrays],
        [made((JOINT_ROWS, WIDTH), LOW)] * 4,
        after=after,
        work=cost(1e6, 1e6),
    )


def end_stage_kernel(place, keep_two, got, send, keep):
    high = place[0] // 2
    keep[...] = added(keep_two[high], got[high])
    send[...] = added(keep_two[1 - high], got[1 - high])


def end_stage(place, keep_two, got, after=()):
    return call(
        end_stage_kernel,
        "end_stage",
        place,
        [plain(keep_two), plain(got)],
        [made(keep_two.shape[1:], LOW)] * 2,
        after=after,
        work=cost(1e6, 1e6),
    )


def joint_sum_kernel(place, first, second, third, fourth, out):
    total = (first[...].astype(FLOAT) + second[...].astype(FLOAT)) + (third[...].astype(FLOAT) + fourth[...].astype(FLOAT))
    out[...] = total.astype(LOW)


def joint_sum(place, arrays, after=()):
    results, mark = call(
        joint_sum_kernel,
        "joint_sum",
        place,
        [plain(array) for array in arrays],
        [made((JOINT_ROWS, WIDTH), LOW)],
        after=after,
        work=cost(1e6, 1e6),
    )
    return results[0], mark


def last_sum_kernel(place, *refs):
    count = len(refs) // 3
    for index in range(count):
        refs[2 * count + index][...] = added(refs[2 * index][...], refs[2 * index + 1][...])


def last_sum(place, pairs, after=()):
    return call(
        last_sum_kernel,
        "last_sum",
        place,
        [plain(array) for pair in pairs for array in pair],
        [made(pair[0].shape, LOW) for pair in pairs],
        after=after,
        work=cost(1e6, 1e6),
    )


def gathered(unit, mark=None):
    across = x_swap(unit)
    if mark is not None:
        across, mark = lax.optimization_barrier((across, mark))
    return unit, core_swap(unit), across, core_swap(across)


def quarters(place):
    x, c = place[2], place[3]
    return (x, c), (x, 1 - c), (1 - x, c), (1 - x, 1 - c)


def line_shift(place):
    seq = place[0] * 2 + place[1]
    return lax.rem(WIDTH - seq * 96, WIDTH)


def dense_out_kernel(
    place, d0, d1, d2, d3, u0, u1, u2, u3,
    down, up, out, gain2, shift2, down_bias, gain1, shift1, out_bias, up_bias, heads, tails,
):
    for down_unit, unit, (x, c) in zip((d0, d1, d2, d3), (u0, u1, u2, u3), quarters(place)):
        quarter = 2 * x + c
        down[pl.ds(pl.multiple_of(quarter * DOWN_ROWS, 32), DOWN_ROWS), :] = down_unit[...].astype(FLOAT)
        up[:, pl.ds(pl.multiple_of(quarter * WIDTH, LANES), WIDTH)] = unit[0:96, :].astype(FLOAT)
        rest = unit[96:128, :].astype(FLOAT)
        lanes = pl.ds(pl.multiple_of(c * HALF, LANES), HALF)
        out[pl.ds(pl.multiple_of(x * 48, 8), 24), lanes] = rest[0:24, 0:HALF]
        out[pl.ds(pl.multiple_of(x * 48 + 24, 8), 24), lanes] = rest[0:24, HALF:]

        @pl.when(x == 0)
        def _(rest=rest):
            heads[...] = rest[24:32]

        @pl.when(x == 1)
        def _(rest=rest):
            tails[...] = rest[24:32]

    seq = place[0] * 2 + place[1]
    shift = line_shift(place)
    head = pltpu.roll(heads[...], shift, 1)
    gain2[...] = head[0:1, 0:96]
    shift2[...] = head[1:2, 0:96]
    down_bias[...] = head[2:3, 0:96]
    tail = pltpu.roll(tails[...], shift, 1)
    gain1[...] = tail[0:1, 0:96]
    shift1[...] = tail[1:2, 0:96]
    out_bias[...] = tail[2:3, 0:96]
    wide = tails[pl.ds(4 + seq // 2, 1), :]
    up_bias[...] = jnp.where(seq % 2 == 0, wide[:, 0:HALF], wide[:, HALF:])


def dense_outputs(place, units, after=()):
    results, mark = call(
        dense_out_kernel,
        "dense_outputs",
        place,
        [plain(unit) for unit in units],
        [made((4 * DOWN_ROWS, WIDTH), FLOAT), made((96, FF), FLOAT), made((96, WIDTH), FLOAT)]
        + [made((1, 96), FLOAT)] * 6
        + [made((1, HALF), FLOAT)],
        scratch=[pltpu.VMEM((8, WIDTH), FLOAT)] * 2,
        after=after,
        work=cost(1e6, 3e6),
    )
    return (*results[:3], *(vector.reshape(-1) for vector in results[3:])), mark


def joint_out_kernel(place, u0, u1, u2, u3, joint, query_bias, value_bias, sums):
    for unit, (x, c) in zip((u0, u1, u2, u3), quarters(place)):

        def lanes(kind):
            return pl.ds(pl.multiple_of(kind * WIDTH + c * HALF, LANES), HALF)

        first = unit[0:JOINT_FIRST].astype(FLOAT)
        rest = unit[JOINT_FIRST:].astype(FLOAT)
        rows = pl.ds(pl.multiple_of(x * 48, 16), 48)
        joint[rows, lanes(0)] = first[:, 0:HALF]
        joint[rows, lanes(1)] = first[:, HALF:]
        joint[pl.ds(pl.multiple_of(x * 48, 8), 24), lanes(2)] = rest[0:24, 0:HALF]
        joint[pl.ds(pl.multiple_of(x * 48 + 24, 8), 24), lanes(2)] = rest[0:24, HALF:]

        @pl.when(x == 0)
        def _(rest=rest, c=c):
            half = pl.ds(pl.multiple_of(c * HALF, LANES), HALF)
            sums[0:1, half] = rest[24:25, 0:HALF]
            sums[1:2, half] = rest[24:25, HALF:]

    turned = pltpu.roll(sums[...], line_shift(place), 1)
    query_bias[...] = turned[0:1, 0:96]
    value_bias[...] = turned[1:2, 0:96]


def joint_outputs(place, units, after=()):
    results, mark = call(
        joint_out_kernel,
        "joint_outputs",
        place,
        [plain(unit) for unit in units],
        [made((96, 3 * WIDTH), FLOAT), made((1, 96), FLOAT), made((1, 96), FLOAT)],
        scratch=[pltpu.VMEM((8, WIDTH), FLOAT)],
        after=after,
        work=cost(1e6, 2e6),
    )
    return (results[0], results[1].reshape(-1), results[2].reshape(-1)), mark


def row_body(
    tokens,
    pair_lengths,
    joint_weight,
    query_bias,
    value_bias,
    out_weight,
    out_bias,
    first_gain,
    first_shift,
    up_weight,
    up_bias,
    down_weight,
    down_bias,
    second_gain,
    second_shift,
    cotangent,
):
    seq, rows = lax.axis_index("seq"), lax.axis_index("rows")
    z, y, x, c = seq // 2, seq % 2, rows // 2, rows % 2
    place = jnp.stack([z, y, x, c]).astype(jnp.int32)
    odd = z % 2
    weights = {
        "out": out_weight, "out_bias": out_bias, "gain1": first_gain, "shift1": first_shift,
        "up": up_weight, "up_bias": up_bias, "down": down_weight, "down_bias": down_bias,
        "gain2": second_gain, "shift2": second_shift,
    }

    def local_row(array, index):
        return lax.dynamic_index_in_dim(array, index, 0, keepdims=False)

    columns, query_row, value_row = own_columns(place, joint_weight, query_bias, value_bias)
    lengths = (pair_lengths, core_swap(pair_lengths))
    own = [row_swap(local_row(tokens, odd), 0), row_swap(local_row(tokens, 1 - odd), 1)]
    *own, columns, lengths = lax.optimization_barrier((*own, columns, lengths))
    across = [y_swap(block) for block in own]
    here = own + [core_swap(block) for block in own]
    (q, k_here, v_here, summed, stats), mark = first_attention(
        place, lengths, here, columns, query_row, value_row
    )
    padding = jnp.zeros((16, WIDTH), LOW)
    cotangents = [
        row_swap(jnp.concatenate([local_row(cotangent, index), padding], axis=0), second)
        for second, index in ((0, odd), (1, 1 - odd))
    ]
    across[0], across[1], mark, cotangents[0] = lax.optimization_barrier((across[0], across[1], mark, cotangents[0]))
    there = across + [core_swap(block) for block in across]
    blocks = here + there
    (att, k_there, v_there, log_total), mark = attention(
        place, lengths, there, columns, value_row, q, summed, stats, (mark,)
    )
    att, cotangents[1] = lax.optimization_barrier((att, cotangents[1]))
    att_got = core_swap(att)
    results, mark = forward(place, att, att_got, own, cotangents, weights, (mark,))
    (
        result0, result1, feed, second_grad, act, act_send, slope, unit1, inverse1, normed, normed_t, att_t, sums0
    ) = results
    act_got, feed_got, normed_got = core_swap(act_send), core_swap(feed), core_swap(normed)
    done = (row_swap(result0, 0), row_swap(result1, 1))
    (px_send, px, qy_send, qy), mark = down_units(place, act, act_got, feed, feed_got, (mark,))
    down_pair = (px, x_swap(px_send), qy, y_swap(qy_send))
    results, mark = backward(place, feed, slope, second_grad, unit1, inverse1, weights, (mark, normed_got))
    inner0, inner1, send0, send1, first_grad, branch_own, back_own, misc_send, sums1 = results
    got, misc = (core_swap(send0), core_swap(send1)), core_swap(misc_send)
    (x_send, y_send, px, qy), mark = up_units(
        place, normed_t, normed_got, (inner0, inner1), got, att_t, branch_own, misc, sums0, sums1, feed_got, (mark,)
    )
    (x_send, y_send, down_p, down_q), mark = down_pair_stage(place, down_pair, x_send, y_send, (mark,))
    x_got, y_got = x_swap(x_send), y_swap(y_send)
    (dq, dk, dv), mark = attention_back(
        place, lengths, q, (k_here, k_there), (v_here, v_there), log_total, att, back_own, misc, (mark,)
    )
    (token_own, own_send, token_far, far_send), mark = token_parts(place, dq, dk, dv, columns, (mark, *done))
    own_got, far_got = core_swap(own_send), core_swap(far_send)
    (px_send, joint_px, qy_send, joint_qy), mark = joint_units(
        place, blocks, dq, dk, dv, token_far, far_got, (mark,)
    )
    (x_send, y_send, p, q_, down_send, down_two), mark = second_stage(
        place, (x_got, y_got, px, qy, down_p, down_q), (mark,)
    )
    x_got, y_got, down_got = x_swap(x_send), y_swap(y_send), z_swap(down_send, 1)
    px_send, qy_send, mark = lax.optimization_barrier((px_send, qy_send, mark))
    across = y_swap(qy_send)
    joint_pair = (joint_px, x_swap(px_send), joint_qy, across)
    (up_send, up_two, down_send, down_keep), mark = up_line_stage(
        place, (x_got, y_got, p, q_, down_two, down_got), (mark,)
    )
    up_got, down_got = z_swap(up_send, 1), z_swap(down_send, 2)
    (up_send, up_keep), mark = end_stage(place, up_two, up_got, (mark, down_got))
    up_got = z_swap(up_send, 2)
    (down_unit,), mark = last_sum(place, ((down_keep, down_got),), (mark,))
    down_all = gathered(down_unit)
    (x_send, y_send, joint_p, joint_q), mark = joint_pair_stage(place, joint_pair, (mark,))
    joint_x_got, joint_y_got = x_swap(x_send), y_swap(y_send)
    (token0, token1), mark = token_last(place, (token_own, own_got, across, first_grad), (mark,))
    back = (row_swap(token0, 0), row_swap(token1, 1))
    (keep, one, two, three), mark = joint_line_stage(
        place, (joint_x_got, joint_y_got, joint_p, joint_q), (mark,)
    )
    joint_last = (keep, z_swap(one, 1), z_swap(two, 2), z_swap(three, 3))
    (up_unit,), mark = last_sum(place, ((up_keep, up_got),), (mark, *down_all[1:]))
    up_all = gathered(up_unit)
    joint_unit, mark = joint_sum(place, joint_last, (mark,))
    (
        down_grad, up_grad, out_grad, second_gain_grad, second_shift_grad, down_bias_grad, first_gain_grad,
        first_shift_grad, out_bias_grad, up_bias_grad,
    ), mark = dense_outputs(place, (*down_all, *up_all), (mark,))
    joint_all = gathered(joint_unit, mark)
    (joint_grad, query_bias_grad, value_bias_grad), mark = joint_outputs(place, joint_all, (mark,))
    (outputs, token_grad), mark = back_rows(place, done, back, (mark,))
    return (
        outputs,
        token_grad,
        joint_grad,
        query_bias_grad,
        value_bias_grad,
        out_grad,
        out_bias_grad,
        first_gain_grad,
        first_shift_grad,
        up_grad,
        up_bias_grad,
        down_grad,
        down_bias_grad,
        second_gain_grad,
        second_shift_grad,
    )


def body(tokens, *others):
    if (lax.axis_size("seq"), lax.axis_size("rows")) == (8, 4) and tokens.shape == (2, BLOCK, WIDTH):
        return row_body(tokens, *others)
    return general_body(tokens, *others)


def solution(mesh):
    placed = (
        P("rows", "seq", None),
        P("rows", None),
        P(),
        P(),
        P(),
        P(),
        P(),
        P(),
        P(),
        P(),
        P(),
        P(),
        P(),
        P(),
        P(),
        P("rows", "seq", None),
    )
    return jax.shard_map(
        body,
        mesh=mesh,
        in_specs=placed,
        out_specs=(
            P("rows", "seq", None),
            P("rows", "seq", None),
            P("seq", None),
            P("seq"),
            P("seq"),
            P("seq", None),
            P("seq"),
            P("seq"),
            P("seq"),
            P("seq", None),
            P("seq"),
            P("seq", None),
            P("seq"),
            P("seq"),
            P("seq"),
        ),
        check_vma=False,
    )
```

profile of v0, /device:TPU:0, one launch (start us, length us, event | category | flops | bytes accessed | tf_op | source)
XLA Modules:
  0.0 159.9 jit_solution(11355911949154525908)
XLA Ops:
  2.2 2.7 %collective-permute-start.1 = (bf16[128,768]{1,0:T(8,128)(2,1)S(1)}, bf16[128,768]{1,0:T(8,128)(2,1)S(1)}, u32[]{:S(2)}, u32[]{:S(2)}) collective-permute-start(bf16[128,768]{1,0:T(8,128)(2,1)S(1)} %get-tuple-element.283), channel_id=1, source_target_pairs={{0,8},{1,24},{2,10},{3,26},{4,12},{5,28},{6,14},{7,30},{8,0},{9,16... | collective-permute-start | bytes 589832 | tf_op jit(solution)/shard_map/ppermute | solution.py:406
  7.5 2.0 %copy-done.3 = bf16[768,2304]{1,0:T(8,128)(2,1)S(1)} copy-done((bf16[768,2304]{1,0:T(8,128)(2,1)S(1)}, bf16[768,2304]{1,0:T(8,128)(2,1)}, u32[]{:S(2)}) %copy-start.3) | copy-done | bytes 3538968
  9.5 1.5 own_columns.1
  11.0 8.0 %collective-permute-start.5 = (bf16[128,768]{1,0:T(8,128)(2,1)S(1)}, bf16[128,768]{1,0:T(8,128)(2,1)S(1)}, u32[]{:S(2)}, u32[]{:S(2)}) collective-permute-start(bf16[128,768]{1,0:T(8,128)(2,1)S(1)} %collective-permute-done.refs_3_.refs_6_.refs_1_), channel_id=1, source_target_pairs={{0,1},{1,0},{2,3},{3,2},{4,5},{5,4},{6,7},{7,6},{8,9},{9,8},{10,11... | collective-permute-start | bytes 589832 | tf_op jit(solution)/shard_map/ppermute | solution.py:406
  19.0 1.5 collective-permute-start.3
  21.2 5.0 %first_attention.1 = (bf16[512,384]{1,0:T(8,128)(2,1)S(1)}, bf16[512,384]{1,0:T(8,128)(2,1)S(1)}, bf16[512,384]{1,0:T(8,128)(2,1)S(1)}, f32[3,128,1024]{2,1,0:T(...) custom-call(s32[4]{0:T(128)S(1)} %pad_add_fusion.refs_0_, s32[2,16]{1,0:T(2,128)S(1)} %copy-done.5, ...), custom_call_target="tpu_custom_call" | custom-call | flops 1024 | bytes 1024 | tf_op jit(solution)/shard_map/first_attention/pallas_call | solution.py:369
  26.7 3.8 %collective-permute-done.4.refs_4_.refs_6_ = bf16[128,768]{1,0:T(8,128)(2,1)S(1)} collective-permute-done((bf16[128,768]{1,0:T(8,128)(2,1)S(1)}, bf16[128,768]{1,0:T(8,128)(2,1)S(1)}, u32[]{:S(2)}, u32[]{:S(2)}) %collective-permute-start.4) | collective-permute-done | bytes 196640 | tf_op jit(solution)/shard_map/ppermute | solution.py:406
  32.4 5.0 %attention.1 = (bf16[512,384]{1,0:T(8,128)(2,1)S(1)}, bf16[512,384]{1,0:T(8,128)(2,1)S(1)}, bf16[512,384]{1,0:T(8,128)(2,1)S(1)}, f32[8,512]{1,0:T(8,128)S(1)}, f32[8,128]{1,0:T(8,128)S(1)}) custom-call(s32[4]{0:T(128)S(1)} %pad_add_fusion.refs_0_, s32[2,16]{1,0:T(2,128)S(1)} %copy-done.5, s32[2,16]{1,0:T(2,128)S(1)} %collective-permute-done.2.refs_2_, ...), custom_call_target="tpu_custom_call" | custom-call | flops 1024 | bytes 1024 | tf_op jit(solution)/shard_map/attention/pallas_call | solution.py:369
  37.8 1.4 collective-permute-done.11.refs_2_
  39.2 6.4 %forward.1 = (bf16[128,768]{1,0:T(8,128)(2,1)S(1)}, bf16[128,768]{1,0:T(8,128)(2,1)S(1)}, bf16[272,768]{1,0:T(8,128)(2,1)S(1)}, f32[256,768]{1,0:T(8,128)S(1)}, ...) custom-call(s32[4]{0:T(128)S(1)} %pad_add_fusion.refs_0_, ...), custom_call_target="tpu_custom_call" | custom-call | flops 1024 | bytes 1024 | tf_op jit(solution)/shard_map/forward/pallas_call | solution.py:369
  46.3 2.1 %collective-permute-done.15.refs_4_.refs_12_ = bf16[272,768]{1,0:T(8,128)(2,1)S(1)} collective-permute-done((bf16[272,768]{1,0:T(8,128)(2,1)S(1)}, bf16[272,768]{1,0:T(8,128)(2,1)S(1)}, u32[]{:S(2)}, u32[]{:S(2)}) %collective-permute-start.15) | collective-permute-done | bytes 417824 | tf_op jit(solution)/shard_map/ppermute | solution.py:406
  48.5 2.6 %down_units.1 = (bf16[4,2,48,768]{3,2,1,0:T(8,128)(2,1)S(1)}, bf16[4,2,48,768]{3,2,1,0:T(8,128)(2,1)S(1)}, bf16[4,2,48,768]{3,2,1,0:T(8,128)(2,1)S(1)}, bf16[4,2,48,768]{3,2,1,0:T(8,128)(2,1)S(1)}, f32[8,128]{1,0:T(8,128)S(1)}) custom-call(s32[4]{0:T(128)S(1)} %pad_add_fusion.refs_0_, bf16[16,96,256]{2,1,0:T(8,128)(2,1)S(1)} %get-tuple-element.180.refs_1_, ...), custom_call_target="tpu_custom_call" | custom-call | flops 1024 | bytes 1024 | tf_op jit(solution)/shard_map/down_units/pallas_call | solution.py:369
  51.1 1.6 collective-permute-start.18
  52.7 1.5 collective-permute-start.19
  54.2 5.0 %backward.1 = (bf16[256,768]{1,0:T(8,128)(2,1)S(1)}, bf16[256,768]{1,0:T(8,128)(2,1)S(1)}, bf16[256,768]{1,0:T(8,128)(2,1)S(1)}, bf16[256,768]{1,0:T(8,128)(2,1)...) custom-call(s32[4]{0:T(128)S(1)} %pad_add_fusion.refs_0_, ...), custom_call_target="tpu_custom_call" | custom-call | flops 1024 | bytes 1024 | tf_op jit(solution)/shard_map/backward/pallas_call | solution.py:369
  59.9 1.7 %collective-permute-done.20.refs_5_ = bf16[256,768]{1,0:T(8,128)(2,1)S(1)} collective-permute-done((bf16[256,768]{1,0:T(8,128)(2,1)S(1)}, bf16[256,768]{1,0:T(8,128)(2,1)S(1)}, u32[]{:S(2)}, u32[]{:S(2)}) %collective-permute-start.20) | collective-permute-done | bytes 393248 | tf_op jit(solution)/shard_map/ppermute | solution.py:406
  62.2 3.3 %up_units.1 = (bf16[704,768]{1,0:T(8,128)(2,1)S(1)}, bf16[704,768]{1,0:T(8,128)(2,1)S(1)}, bf16[4,2,64,768]{3,2,1,0:T(8,128)(2,1)S(1)}, bf16[4,2,64,768]{3,2,1,0:T(8,128)(2,1)S(1)}, f32[8,128]{1,0:T(8,128)S(1)}) custom-call(s32[4]{0:T(128)S(1)} %pad_add_fusion.refs_0_, bf16[768,256]{1,0:T(8,128)(2,1)S(1)} %get-tuple-element.191.refs_1_, ...), custom_call_target="tpu_custom_call" | custom-call | flops 1024 | bytes 1024 | tf_op jit(solution)/shard_map/up_units/pallas_call | solution.py:369
  65.5 1.1 collective-permute-done.18.refs_2_
  66.7 1.2 collective-permute-done.19.refs_4_
  69.6 1.5 collective-permute-start.25
  71.9 10.3 %attention_back.1 = (bf16[512,384]{1,0:T(8,128)(2,1)S(1)}, bf16[1024,384]{1,0:T(8,128)(2,1)S(1)}, bf16[1024,384]{1,0:T(8,128)(2,1)S(1)}, f32[8,128]{1,0:T(8,128)S(1)}) custom-call(s32[4]{0:T(128)S(1)} %pad_add_fusion.refs_0_, s32[2,16]{1,0:T(2,128)S(1)} %copy-done.5, s32[2,16]{1,0:T(2,128)S(1)} %collective-permute-done.2.refs_2_, ...), custom_call_target="tpu_custom_call" | custom-call | flops 1024 | bytes 1024 | tf_op jit(solution)/shard_map/attention_back/pallas_call | solution.py:369
  82.2 2.7 %token_parts.1 = (bf16[256,768]{1,0:T(8,128)(2,1)S(1)}, bf16[256,768]{1,0:T(8,128)(2,1)S(1)}, bf16[256,768]{1,0:T(8,128)(2,1)S(1)}, bf16[256,768]{1,0:T(8,128)(2,1)S(1)}, f32[8,128]{1,0:T(8,128)S(1)}) custom-call(s32[4]{0:T(128)S(1)} %pad_add_fusion.refs_0_, bf16[512,384]{1,0:T(8,128)(2,1)S(1)} %get-tuple-element.205.refs_1_.refs_9_, ...), custom_call_target="tpu_custom_call" | custom-call | flops 1024 | bytes 1024 | tf_op jit(solution)/shard_map/token_parts/pallas_call | solution.py:369
  85.0 1.2 collective-permute-start.23
  86.2 1.3 collective-permute-done.23.refs_13_
  87.5 3.2 %joint_units.1 = (bf16[4,2,48,768]{3,2,1,0:T(8,128)(2,1)S(1)}, bf16[4,2,48,768]{3,2,1,0:T(8,128)(2,1)S(1)}, bf16[512,768]{1,0:T(8,128)(2,1)S(1)}, bf16[4,2,32,768]{3,2,1,0:T(8,128)(2,1)S(1)}, f32[8,128]{1,0:T(8,128)S(1)}) custom-call(s32[4]{0:T(128)S(1)} %pad_add_fusion.refs_0_, bf16[128,768]{1,0:T(8,128)(2,1)S(1)} %collective-permute-done.refs_3_.refs_6_.refs_1_, ...), custom_call_target="tpu_custom_call" | custom-call | flops 1024 | bytes 1024 | tf_op jit(solution)/shard_map/joint_units/pallas_call | solution.py:369
  90.7 3.2 %collective-permute-done.24.refs_1_ = bf16[704,768]{1,0:T(8,128)(2,1)S(1)} collective-permute-done((bf16[704,768]{1,0:T(8,128)(2,1)S(1)}, bf16[704,768]{1,0:T(8,128)(2,1)S(1)}, u32[]{:S(2)}, u32[]{:S(2)}) %collective-permute-start.24) | collective-permute-done | bytes 1081376 | tf_op jit(solution)/shard_map/ppermute | solution.py:406
  95.3 1.5 collective-permute-start.28
  96.8 1.5 collective-permute-start.29
  99.4 6.1 %collective-permute-done.30.refs_6_ = bf16[2,96,768]{2,1,0:T(8,128)(2,1)S(1)} collective-permute-done((bf16[2,96,768]{2,1,0:T(8,128)(2,1)S(1)}, bf16[2,96,768]{2,1,0:T(8,128)(2,1)S(1)}, u32[]{:S(2)}, u32[]{:S(2)}) %collective-permute-start.30) | collective-permute-done | bytes 294944 | tf_op jit(solution)/shard_map/ppermute | solution.py:406
  105.5 1.9 %collective-permute-done.28.refs_1_ = bf16[256,768]{1,0:T(8,128)(2,1)S(1)} collective-permute-done((bf16[256,768]{1,0:T(8,128)(2,1)S(1)}, bf16[256,768]{1,0:T(8,128)(2,1)S(1)}, u32[]{:S(2)}, u32[]{:S(2)}) %collective-permute-start.28) | collective-permute-done | bytes 393248 | tf_op jit(solution)/shard_map/ppermute | solution.py:406
  107.4 1.4 collective-permute-done.29.refs_2_
  110.6 8.0 %collective-permute-done.31.refs_4_.refs_2_ = bf16[96,768]{1,0:T(8,128)(2,1)S(1)} collective-permute-done((bf16[96,768]{1,0:T(8,128)(2,1)S(1)}, bf16[96,768]{1,0:T(8,128)(2,1)S(1)}, u32[]{:S(2)}, u32[]{:S(2)}) %collective-permute-start.31) | collective-permute-done | bytes 147488 | tf_op jit(solution)/shard_map/ppermute | solution.py:406
  118.6 2.0 %collective-permute-done.32.refs_2_ = bf16[2,128,768]{2,1,0:T(8,128)(2,1)S(1)} collective-permute-done((bf16[2,128,768]{2,1,0:T(8,128)(2,1)S(1)}, bf16[2,128,768]{2,1,0:T(8,128)(2,1)S(1)}, u32[]{:S(2)}, u32[]{:S(2)}) %collective-permute-start.32) | collective-permute-done | bytes 393248 | tf_op jit(solution)/shard_map/ppermute | solution.py:406
  123.0 1.6 %collective-permute-start.36 = (bf16[4,48,768]{2,1,0:T(8,128)(2,1)S(1)}, bf16[4,48,768]{2,1,0:T(8,128)(2,1)S(1)}, u32[]{:S(2)}, u32[]{:S(2)}) collective-permute-start(bf16[4,48,768]{2,1,0:T(8,128)(2,1)S(1)} %get-tuple-element.247), channel_id=1, source_target_pairs={{0,4},{1,5},{2,6},{3,7},{4,0},{5,1},{6,2},{7,3},{8,12},{9,13},{10,... | collective-permute-start | bytes 884744 | tf_op jit(solution)/shard_map/ppermute | solution.py:406
  125.3 1.4 collective-permute-start.35
  127.1 2.7 %collective-permute-done.42.refs_5_.refs_3_ = bf16[96,768]{1,0:T(8,128)(2,1)S(1)} collective-permute-done((bf16[96,768]{1,0:T(8,128)(2,1)S(1)}, bf16[96,768]{1,0:T(8,128)(2,1)S(1)}, u32[]{:S(2)}, u32[]{:S(2)}) %collective-permute-start.42) | collective-permute-done | bytes 147488 | tf_op jit(solution)/shard_map/ppermute | solution.py:406
  130.5 1.4 collective-permute-done.35.refs_1_
  132.6 2.2 %collective-permute-done.40.refs_2_ = bf16[128,768]{1,0:T(8,128)(2,1)S(1)} collective-permute-done((bf16[128,768]{1,0:T(8,128)(2,1)S(1)}, bf16[128,768]{1,0:T(8,128)(2,1)S(1)}, u32[]{:S(2)}, u32[]{:S(2)}) %collective-permute-start.40) | collective-permute-done | bytes 196640 | tf_op jit(solution)/shard_map/ppermute | solution.py:406
  136.0 2.5 %collective-permute-start.38 = (bf16[80,768]{1,0:T(8,128)(2,1)S(1)}, bf16[80,768]{1,0:T(8,128)(2,1)S(1)}, u32[]{:S(2)}, u32[]{:S(2)}) collective-permute-start(bf16[80,768]{1,0:T(8,128)(2,1)S(1)} %get-tuple-element.253), channel_id=1, source_target_pairs={{0,16},{1,17},{2,18},{3,19},{4,20},{5,21},{6,22},{7,23},{8,24},{9,... | collective-permute-start | bytes 368648 | tf_op jit(solution)/shard_map/ppermute | solution.py:406
  138.5 1.9 %collective-permute-start.39 = (bf16[80,768]{1,0:T(8,128)(2,1)S(1)}, bf16[80,768]{1,0:T(8,128)(2,1)S(1)}, u32[]{:S(2)}, u32[]{:S(2)}) collective-permute-start(bf16[80,768]{1,0:T(8,128)(2,1)S(1)} %get-tuple-element.254), channel_id=1, source_target_pairs={{0,24},{1,25},{2,26},{3,27},{4,28},{5,29},{6,30},{7,31},{8,16},{9,... | collective-permute-start | bytes 368648 | tf_op jit(solution)/shard_map/ppermute | solution.py:406
  141.1 1.4 collective-permute-done.37.refs_2_
  142.5 3.6 %collective-permute-done.38.refs_3_ = bf16[80,768]{1,0:T(8,128)(2,1)S(1)} collective-permute-done((bf16[80,768]{1,0:T(8,128)(2,1)S(1)}, bf16[80,768]{1,0:T(8,128)(2,1)S(1)}, u32[]{:S(2)}, u32[]{:S(2)}) %collective-permute-start.38) | collective-permute-done | bytes 122912 | tf_op jit(solution)/shard_map/ppermute | solution.py:406
  146.7 1.5 collective-permute-start.45
  148.8 1.9 %collective-permute-start.34 = (bf16[128,768]{1,0:T(8,128)(2,1)S(1)}, bf16[128,768]{1,0:T(8,128)(2,1)S(1)}, u32[]{:S(2)}, u32[]{:S(2)}) collective-permute-start(bf16[128,768]{1,0:T(8,128)(2,1)S(1)} %get-tuple-element.245), channel_id=1, source_target_pairs={{0,8},{1,24},{2,10},{3,26},{4,12},{5,28},{6,14},{7,30},{8,0},{9,16... | collective-permute-start | bytes 589832 | tf_op jit(solution)/shard_map/ppermute | solution.py:406
  150.8 2.3 %collective-permute-start.44 = (bf16[80,768]{1,0:T(8,128)(2,1)S(1)}, bf16[80,768]{1,0:T(8,128)(2,1)S(1)}, u32[]{:S(2)}, u32[]{:S(2)}) collective-permute-start(bf16[80,768]{1,0:T(8,128)(2,1)S(1)} %get-tuple-element.260.refs_1_), channel_id=1, source_target_pairs={{0,1},{1,0},{2,3},{3,2},{4,5},{5,4},{6,7},{7,6},{8,9},{9,8},{10,11... | collective-permute-start | bytes 368648 | tf_op jit(solution)/shard_map/ppermute | solution.py:406
  153.0 2.3 %dense_outputs.1 = (f32[384,768]{1,0:T(8,128)}, f32[96,3072]{1,0:T(8,128)}, f32[96,768]{1,0:T(8,128)}, f32[1,96]{1,0:T(1,128)}, f32[1,96]{1,0:T(1,128)}, /*index...) custom-call(s32[4]{0:T(128)S(1)} %pad_add_fusion.refs_0_, ...), custom_call_target="tpu_custom_call" | custom-call | flops 1024 | bytes 1024 | tf_op jit(solution)/shard_map/dense_outputs/pallas_call | solution.py:369
  156.7 1.5 joint_outputs.1
  158.3 1.6 %back_rows.1 = (bf16[2,128,768]{2,1,0:T(8,128)(2,1)}, f32[2,128,768]{2,1,0:T(8,128)}, f32[8,128]{1,0:T(8,128)}) custom-call(s32[4]{0:T(128)S(1)} %pad_add_fusion.refs_0_, bf16[128,768]{1,0:T(8,128)(2,1)S(1)} %collective-permute-done.12.refs_6_.refs_1_, bf16[128,768]{1,0:T(8,128)(2,1)S(1)} %collective-permute-done.13.refs_7_.refs_2_, ...), custom_call_target="tpu_custom_call" | custom-call | flops 1024 | bytes 1024 | tf_op jit(solution)/shard_map/back_rows/pallas_call | solution.py:369
  (117 shorter events, 25.5 us)
Async XLA Ops:
  0.7 10.4 %collective-permute-start.2 = (s32[2,16]{1,0:T(2,128)}, s32[2,16]{1,0:T(2,128)S(1)}, u32[]{:S(2)}, u32[]{:S(2)}) collective-permute-start(s32[2,16]{1,0:T(2,128)} %refs_1_.4), channel_id=1, source_target_pairs={{0,1},{1,0},{2,3},{3,2},{4,5},{5,4},{6,7},{7,6},{8,9},{9,8},{10,11... | collective-permute-start | bytes 392 | tf_op jit(solution)/shard_map/ppermute | solution.py:406
  2.2 8.8 %collective-permute-start.1 = (bf16[128,768]{1,0:T(8,128)(2,1)S(1)}, bf16[128,768]{1,0:T(8,128)(2,1)S(1)}, u32[]{:S(2)}, u32[]{:S(2)}) collective-permute-start(bf16[128,768]{1,0:T(8,128)(2,1)S(1)} %get-tuple-element.283), channel_id=1, source_target_pairs={{0,8},{1,24},{2,10},{3,26},{4,12},{5,28},{6,14},{7,30},{8,0},{9,16... | collective-permute-start | bytes 589832 | tf_op jit(solution)/shard_map/ppermute | solution.py:406
  4.9 6.1 %collective-permute-start = (bf16[128,768]{1,0:T(8,128)(2,1)S(1)}, bf16[128,768]{1,0:T(8,128)(2,1)S(1)}, u32[]{:S(2)}, u32[]{:S(2)}) collective-permute-start(bf16[128,768]{1,0:T(8,128)(2,1)S(1)} %get-tuple-element.284), channel_id=1, source_target_pairs={{0,0},{1,16},{2,2},{3,18},{4,4},{5,20},{6,6},{7,22},{8,8},{9,24},{... | collective-permute-start | bytes 589832 | tf_op jit(solution)/shard_map/ppermute | solution.py:406
  6.7 19.5 %collective-permute-start.7 = (bf16[144,768]{1,0:T(8,128)(2,1)S(1)}, bf16[144,768]{1,0:T(8,128)(2,1)S(1)}, u32[]{:S(2)}, u32[]{:S(2)}) collective-permute-start(bf16[144,768]{1,0:T(8,128)(2,1)S(1)} %concatenate.6), channel_id=1, source_target_pairs={{0,0},{1,16},{2,2},{3,18},{4,4},{5,20},{6,6},{7,22},{8,8},{9,24},{... | collective-permute-start | bytes 663560 | tf_op jit(solution)/shard_map/ppermute | solution.py:406
  11.0 10.1 %collective-permute-start.5 = (bf16[128,768]{1,0:T(8,128)(2,1)S(1)}, bf16[128,768]{1,0:T(8,128)(2,1)S(1)}, u32[]{:S(2)}, u32[]{:S(2)}) collective-permute-start(bf16[128,768]{1,0:T(8,128)(2,1)S(1)} %collective-permute-done.refs_3_.refs_6_.refs_1_), channel_id=1, source_target_pairs={{0,1},{1,0},{2,3},{3,2},{4,5},{5,4},{6,7},{7,6},{8,9},{9,8},{10,11... | collective-permute-start | bytes 589832 | tf_op jit(solution)/shard_map/ppermute | solution.py:406
  19.0 2.1 %collective-permute-start.6 = (bf16[128,768]{1,0:T(8,128)(2,1)S(1)}, bf16[128,768]{1,0:T(8,128)(2,1)S(1)}, u32[]{:S(2)}, u32[]{:S(2)}) collective-permute-start(bf16[128,768]{1,0:T(8,128)(2,1)S(1)} %collective-permute-done.1.refs_4_.refs_7_.refs_2_), channel_id=1, source_target_pairs={{0,1},{1,0},{2,3},{3,2},{4,5},{5,4},{6,7},{7,6},{8,9},{9,8},{10,11... | collective-permute-start | bytes 589832 | tf_op jit(solution)/shard_map/ppermute | solution.py:406
  19.0 7.7 %collective-permute-start.3 = (bf16[128,768]{1,0:T(8,128)(2,1)S(1)}, bf16[128,768]{1,0:T(8,128)(2,1)S(1)}, u32[]{:S(2)}, u32[]{:S(2)}) collective-permute-start(bf16[128,768]{1,0:T(8,128)(2,1)S(1)} %collective-permute-done.refs_3_.refs_6_.refs_1_), channel_id=1, source_target_pairs={{0,4},{1,5},{2,6},{3,7},{4,0},{5,1},{6,2},{7,3},{8,12},{9,13},{10,... | collective-permute-start | bytes 589832 | tf_op jit(solution)/shard_map/ppermute | solution.py:406
  20.6 10.0 %collective-permute-start.4 = (bf16[128,768]{1,0:T(8,128)(2,1)S(1)}, bf16[128,768]{1,0:T(8,128)(2,1)S(1)}, u32[]{:S(2)}, u32[]{:S(2)}) collective-permute-start(bf16[128,768]{1,0:T(8,128)(2,1)S(1)} %collective-permute-done.1.refs_4_.refs_7_.refs_2_), channel_id=1, source_target_pairs={{0,4},{1,5},{2,6},{3,7},{4,0},{5,1},{6,2},{7,3},{8,12},{9,13},{10,... | collective-permute-start | bytes 589832 | tf_op jit(solution)/shard_map/ppermute | solution.py:406
  21.1 16.2 %collective-permute-start.10 = (bf16[144,768]{1,0:T(8,128)(2,1)S(1)}, bf16[144,768]{1,0:T(8,128)(2,1)S(1)}, u32[]{:S(2)}, u32[]{:S(2)}) collective-permute-start(bf16[144,768]{1,0:T(8,128)(2,1)S(1)} %concatenate.7), channel_id=1, source_target_pairs={{0,8},{1,24},{2,10},{3,26},{4,12},{5,28},{6,14},{7,30},{8,0},{9,16... | collective-permute-start | bytes 663560 | tf_op jit(solution)/shard_map/ppermute | solution.py:406
  30.6 1.7 %collective-permute-start.9 = (bf16[128,768]{1,0:T(8,128)(2,1)S(1)}, bf16[128,768]{1,0:T(8,128)(2,1)S(1)}, u32[]{:S(2)}, u32[]{:S(2)}) collective-permute-start(bf16[128,768]{1,0:T(8,128)(2,1)S(1)} %collective-permute-done.4.refs_4_.refs_6_), channel_id=1, source_target_pairs={{0,1},{1,0},{2,3},{3,2},{4,5},{5,4},{6,7},{7,6},{8,9},{9,8},{10,11... | collective-permute-start | bytes 589832 | tf_op jit(solution)/shard_map/ppermute | solution.py:406
  37.4 1.8 %collective-permute-start.11 = (bf16[512,384]{1,0:T(8,128)(2,1)S(1)}, bf16[512,384]{1,0:T(8,128)(2,1)S(1)}, u32[]{:S(2)}, u32[]{:S(2)}) collective-permute-start(bf16[512,384]{1,0:T(8,128)(2,1)S(1)} %get-tuple-element.164.refs_1_.refs_9_), channel_id=1, source_target_pairs={{0,1},{1,0},{2,3},{3,2},{4,5},{5,4},{6,7},{7,6},{8,9},{9,8},{10,11... | collective-permute-start | bytes 1179656 | tf_op jit(solution)/shard_map/ppermute | solution.py:406
  45.5 3.0 %collective-permute-start.14 = (bf16[16,96,256]{2,1,0:T(8,128)(2,1)S(1)}, bf16[16,96,256]{2,1,0:T(8,128)(2,1)S(1)}, u32[]{:S(2)}, u32[]{:S(2)}) collective-permute-start(bf16[16,96,256]{2,1,0:T(8,128)(2,1)S(1)} %get-tuple-element.181), channel_id=1, source_target_pairs={{0,1},{1,0},{2,3},{3,2},{4,5},{5,4},{6,7},{7,6},{8,9},{9,8},{10,11... | collective-permute-start | bytes 2359304 | tf_op jit(solution)/shard_map/ppermute | solution.py:406
  45.8 2.7 %collective-permute-start.15 = (bf16[272,768]{1,0:T(8,128)(2,1)S(1)}, bf16[272,768]{1,0:T(8,128)(2,1)S(1)}, u32[]{:S(2)}, u32[]{:S(2)}) collective-permute-start(bf16[272,768]{1,0:T(8,128)(2,1)S(1)} %get-tuple-element.175.refs_3_.refs_1_), channel_id=1, source_target_pairs={{0,1},{1,0},{2,3},{3,2},{4,5},{5,4},{6,7},{7,6},{8,9},{9,8},{10,11... | collective-permute-start | bytes 1253384 | tf_op jit(solution)/shard_map/ppermute | solution.py:406
  46.1 8.1 %collective-permute-start.16 = (bf16[256,768]{1,0:T(8,128)(2,1)S(1)}, bf16[256,768]{1,0:T(8,128)(2,1)S(1)}, u32[]{:S(2)}, u32[]{:S(2)}) collective-permute-start(bf16[256,768]{1,0:T(8,128)(2,1)S(1)} %get-tuple-element.184), channel_id=1, source_target_pairs={{0,1},{1,0},{2,3},{3,2},{4,5},{5,4},{6,7},{7,6},{8,9},{9,8},{10,11... | collective-permute-start | bytes 1179656 | tf_op jit(solution)/shard_map/ppermute | solution.py:406
  51.1 15.5 %collective-permute-start.18 = (bf16[4,2,48,768]{3,2,1,0:T(8,128)(2,1)S(1)}, bf16[4,2,48,768]{3,2,1,0:T(8,128)(2,1)S(1)}, u32[]{:S(2)}, u32[]{:S(2)}) collective-permute-start(bf16[4,2,48,768]{3,2,1,0:T(8,128)(2,1)S(1)} %get-tuple-element.188), channel_id=1, source_target_pairs={{0,2},{1,3},{2,0},{3,1},{4,6},{5,7},{6,4},{7,5},{8,10},{9,11},{10,... | collective-permute-start | bytes 1769480 | tf_op jit(solution)/shard_map/ppermute | solution.py:406
  52.7 15.2 %collective-permute-start.19 = (bf16[4,2,48,768]{3,2,1,0:T(8,128)(2,1)S(1)}, bf16[4,2,48,768]{3,2,1,0:T(8,128)(2,1)S(1)}, u32[]{:S(2)}, u32[]{:S(2)}) collective-permute-start(bf16[4,2,48,768]{3,2,1,0:T(8,128)(2,1)S(1)} %get-tuple-element.190), channel_id=1, source_target_pairs={{0,4},{1,5},{2,6},{3,7},{4,0},{5,1},{6,2},{7,3},{8,12},{9,13},{10,... | collective-permute-start | bytes 1769480 | tf_op jit(solution)/shard_map/ppermute | solution.py:406
  59.3 3.0 %collective-permute-start.17 = (bf16[272,768]{1,0:T(8,128)(2,1)S(1)}, bf16[272,768]{1,0:T(8,128)(2,1)S(1)}, u32[]{:S(2)}, u32[]{:S(2)}) collective-permute-start(bf16[272,768]{1,0:T(8,128)(2,1)S(1)} %get-tuple-element.186), channel_id=1, source_target_pairs={{0,1},{1,0},{2,3},{3,2},{4,5},{5,4},{6,7},{7,6},{8,9},{9,8},{10,11... | collective-permute-start | bytes 1253384 | tf_op jit(solution)/shard_map/ppermute | solution.py:406
  59.3 2.3 %collective-permute-start.20 = (bf16[256,768]{1,0:T(8,128)(2,1)S(1)}, bf16[256,768]{1,0:T(8,128)(2,1)S(1)}, u32[]{:S(2)}, u32[]{:S(2)}) collective-permute-start(bf16[256,768]{1,0:T(8,128)(2,1)S(1)} %get-tuple-element.194), channel_id=1, source_target_pairs={{0,1},{1,0},{2,3},{3,2},{4,5},{5,4},{6,7},{7,6},{8,9},{9,8},{10,11... | collective-permute-start | bytes 1179656 | tf_op jit(solution)/shard_map/ppermute | solution.py:406
  59.8 2.4 %collective-permute-start.21 = (bf16[256,768]{1,0:T(8,128)(2,1)S(1)}, bf16[256,768]{1,0:T(8,128)(2,1)S(1)}, u32[]{:S(2)}, u32[]{:S(2)}) collective-permute-start(bf16[256,768]{1,0:T(8,128)(2,1)S(1)} %get-tuple-element.195), channel_id=1, source_target_pairs={{0,1},{1,0},{2,3},{3,2},{4,5},{5,4},{6,7},{7,6},{8,9},{9,8},{10,11... | collective-permute-start | bytes 1179656 | tf_op jit(solution)/shard_map/ppermute | solution.py:406
  69.0 24.9 %collective-permute-start.24 = (bf16[704,768]{1,0:T(8,128)(2,1)S(1)}, bf16[704,768]{1,0:T(8,128)(2,1)S(1)}, u32[]{:S(2)}, u32[]{:S(2)}) collective-permute-start(bf16[704,768]{1,0:T(8,128)(2,1)S(1)} %get-tuple-element.216), channel_id=1, source_target_pairs={{0,2},{1,3},{2,0},{3,1},{4,6},{5,7},{6,4},{7,5},{8,10},{9,11},{10,... | collective-permute-start | bytes 3244040 | tf_op jit(solution)/shard_map/ppermute | solution.py:406
  69.6 24.6 %collective-permute-start.25 = (bf16[704,768]{1,0:T(8,128)(2,1)S(1)}, bf16[704,768]{1,0:T(8,128)(2,1)S(1)}, u32[]{:S(2)}, u32[]{:S(2)}) collective-permute-start(bf16[704,768]{1,0:T(8,128)(2,1)S(1)} %get-tuple-element.217), channel_id=1, source_target_pairs={{0,4},{1,5},{2,6},{3,7},{4,0},{5,1},{6,2},{7,3},{8,12},{9,13},{10,... | collective-permute-start | bytes 3244040 | tf_op jit(solution)/shard_map/ppermute | solution.py:406
  71.1 11.1 %collective-permute-start.12 = (bf16[128,768]{1,0:T(8,128)(2,1)S(1)}, bf16[128,768]{1,0:T(8,128)(2,1)S(1)}, u32[]{:S(2)}, u32[]{:S(2)}) collective-permute-start(bf16[128,768]{1,0:T(8,128)(2,1)S(1)} %get-tuple-element.168), channel_id=1, source_target_pairs={{0,0},{1,16},{2,2},{3,18},{4,4},{5,20},{6,6},{7,22},{8,8},{9,24},{... | collective-permute-start | bytes 589832 | tf_op jit(solution)/shard_map/ppermute | solution.py:406
  71.8 10.4 %collective-permute-start.13 = (bf16[128,768]{1,0:T(8,128)(2,1)S(1)}, bf16[128,768]{1,0:T(8,128)(2,1)S(1)}, u32[]{:S(2)}, u32[]{:S(2)}) collective-permute-start(bf16[128,768]{1,0:T(8,128)(2,1)S(1)} %get-tuple-element.169), channel_id=1, source_target_pairs={{0,8},{1,24},{2,10},{3,26},{4,12},{5,28},{6,14},{7,30},{8,0},{9,16... | collective-permute-start | bytes 589832 | tf_op jit(solution)/shard_map/ppermute | solution.py:406
  85.0 2.5 %collective-permute-start.23 = (bf16[256,768]{1,0:T(8,128)(2,1)S(1)}, bf16[256,768]{1,0:T(8,128)(2,1)S(1)}, u32[]{:S(2)}, u32[]{:S(2)}) collective-permute-start(bf16[256,768]{1,0:T(8,128)(2,1)S(1)} %get-tuple-element.212), channel_id=1, source_target_pairs={{0,1},{1,0},{2,3},{3,2},{4,5},{5,4},{6,7},{7,6},{8,9},{9,8},{10,11... | collective-permute-start | bytes 1179656 | tf_op jit(solution)/shard_map/ppermute | solution.py:406
  95.3 12.1 %collective-permute-start.28 = (bf16[256,768]{1,0:T(8,128)(2,1)S(1)}, bf16[256,768]{1,0:T(8,128)(2,1)S(1)}, u32[]{:S(2)}, u32[]{:S(2)}) collective-permute-start(bf16[256,768]{1,0:T(8,128)(2,1)S(1)} %get-tuple-element.229), channel_id=1, source_target_pairs={{0,2},{1,3},{2,0},{3,1},{4,6},{5,7},{6,4},{7,5},{8,10},{9,11},{10,... | collective-permute-start | bytes 1179656 | tf_op jit(solution)/shard_map/ppermute | solution.py:406
  96.8 12.1 %collective-permute-start.29 = (bf16[256,768]{1,0:T(8,128)(2,1)S(1)}, bf16[256,768]{1,0:T(8,128)(2,1)S(1)}, u32[]{:S(2)}, u32[]{:S(2)}) collective-permute-start(bf16[256,768]{1,0:T(8,128)(2,1)S(1)} %get-tuple-element.230), channel_id=1, source_target_pairs={{0,4},{1,5},{2,6},{3,7},{4,0},{5,1},{6,2},{7,3},{8,12},{9,13},{10,... | collective-permute-start | bytes 1179656 | tf_op jit(solution)/shard_map/ppermute | solution.py:406
  98.3 23.9 %collective-permute-start.26 = (bf16[512,768]{1,0:T(8,128)(2,1)S(1)}, bf16[512,768]{1,0:T(8,128)(2,1)S(1)}, u32[]{:S(2)}, u32[]{:S(2)}) collective-permute-start(bf16[512,768]{1,0:T(8,128)(2,1)S(1)} %get-tuple-element.224), channel_id=1, source_target_pairs={{0,4},{1,5},{2,6},{3,7},{4,0},{5,1},{6,2},{7,3},{8,12},{9,13},{10,... | collective-permute-start | bytes 2359304 | tf_op jit(solution)/shard_map/ppermute | solution.py:406
  98.8 6.7 %collective-permute-start.30 = (bf16[2,96,768]{2,1,0:T(8,128)(2,1)S(1)}, bf16[2,96,768]{2,1,0:T(8,128)(2,1)S(1)}, u32[]{:S(2)}, u32[]{:S(2)}) collective-permute-start(bf16[2,96,768]{2,1,0:T(8,128)(2,1)S(1)} %get-tuple-element.234), channel_id=1, source_target_pairs={{0,8},{1,9},{2,10},{3,11},{4,12},{5,13},{6,14},{7,15},{8,0},{9,1},... | collective-permute-start | bytes 884744 | tf_op jit(solution)/shard_map/ppermute | solution.py:406
  98.8 23.1 %collective-permute-start.27 = (bf16[4,2,48,768]{3,2,1,0:T(8,128)(2,1)S(1)}, bf16[4,2,48,768]{3,2,1,0:T(8,128)(2,1)S(1)}, u32[]{:S(2)}, u32[]{:S(2)}) collective-permute-start(bf16[4,2,48,768]{3,2,1,0:T(8,128)(2,1)S(1)} %get-tuple-element.227), channel_id=1, source_target_pairs={{0,2},{1,3},{2,0},{3,1},{4,6},{5,7},{6,4},{7,5},{8,10},{9,11},{10,... | collective-permute-start | bytes 1769480 | tf_op jit(solution)/shard_map/ppermute | solution.py:406
  109.6 11.0 %collective-permute-start.32 = (bf16[2,128,768]{2,1,0:T(8,128)(2,1)S(1)}, bf16[2,128,768]{2,1,0:T(8,128)(2,1)S(1)}, u32[]{:S(2)}, u32[]{:S(2)}) collective-permute-start(bf16[2,128,768]{2,1,0:T(8,128)(2,1)S(1)} %get-tuple-element.239), channel_id=1, source_target_pairs={{0,8},{1,9},{2,10},{3,11},{4,12},{5,13},{6,14},{7,15},{8,0},{9,1},... | collective-permute-start | bytes 1179656 | tf_op jit(solution)/shard_map/ppermute | solution.py:406
  109.7 17.4 %collective-permute-start.22 = (bf16[256,768]{1,0:T(8,128)(2,1)S(1)}, bf16[256,768]{1,0:T(8,128)(2,1)S(1)}, u32[]{:S(2)}, u32[]{:S(2)}) collective-permute-start(bf16[256,768]{1,0:T(8,128)(2,1)S(1)} %get-tuple-element.210), channel_id=1, source_target_pairs={{0,1},{1,0},{2,3},{3,2},{4,5},{5,4},{6,7},{7,6},{8,9},{9,8},{10,11... | collective-permute-start | bytes 1179656 | tf_op jit(solution)/shard_map/ppermute | solution.py:406
  109.8 8.8 %collective-permute-start.31 = (bf16[96,768]{1,0:T(8,128)(2,1)S(1)}, bf16[96,768]{1,0:T(8,128)(2,1)S(1)}, u32[]{:S(2)}, u32[]{:S(2)}) collective-permute-start(bf16[96,768]{1,0:T(8,128)(2,1)S(1)} %get-tuple-element.237), channel_id=1, source_target_pairs={{0,16},{1,17},{2,18},{3,19},{4,20},{5,21},{6,22},{7,23},{8,24},{9,... | collective-permute-start | bytes 442376 | tf_op jit(solution)/shard_map/ppermute | solution.py:406
  123.0 8.9 %collective-permute-start.36 = (bf16[4,48,768]{2,1,0:T(8,128)(2,1)S(1)}, bf16[4,48,768]{2,1,0:T(8,128)(2,1)S(1)}, u32[]{:S(2)}, u32[]{:S(2)}) collective-permute-start(bf16[4,48,768]{2,1,0:T(8,128)(2,1)S(1)} %get-tuple-element.247), channel_id=1, source_target_pairs={{0,4},{1,5},{2,6},{3,7},{4,0},{5,1},{6,2},{7,3},{8,12},{9,13},{10,... | collective-permute-start | bytes 884744 | tf_op jit(solution)/shard_map/ppermute | solution.py:406
  124.6 5.1 %collective-permute-start.42 = (bf16[96,768]{1,0:T(8,128)(2,1)S(1)}, bf16[96,768]{1,0:T(8,128)(2,1)S(1)}, u32[]{:S(2)}, u32[]{:S(2)}) collective-permute-start(bf16[96,768]{1,0:T(8,128)(2,1)S(1)} %get-tuple-element.258.refs_1_), channel_id=1, source_target_pairs={{0,2},{1,3},{2,0},{3,1},{4,6},{5,7},{6,4},{7,5},{8,10},{9,11},{10,... | collective-permute-start | bytes 442376 | tf_op jit(solution)/shard_map/ppermute | solution.py:406
  125.3 6.6 %collective-permute-start.35 = (bf16[4,32,768]{2,1,0:T(8,128)(2,1)S(1)}, bf16[4,32,768]{2,1,0:T(8,128)(2,1)S(1)}, u32[]{:S(2)}, u32[]{:S(2)}) collective-permute-start(bf16[4,32,768]{2,1,0:T(8,128)(2,1)S(1)} %get-tuple-element.246), channel_id=1, source_target_pairs={{0,2},{1,3},{2,0},{3,1},{4,6},{5,7},{6,4},{7,5},{8,10},{9,11},{10,... | collective-permute-start | bytes 589832 | tf_op jit(solution)/shard_map/ppermute | solution.py:406
  126.7 8.1 %collective-permute-start.40 = (bf16[128,768]{1,0:T(8,128)(2,1)S(1)}, bf16[128,768]{1,0:T(8,128)(2,1)S(1)}, u32[]{:S(2)}, u32[]{:S(2)}) collective-permute-start(bf16[128,768]{1,0:T(8,128)(2,1)S(1)} %get-tuple-element.256), channel_id=1, source_target_pairs={{0,16},{1,17},{2,18},{3,19},{4,20},{5,21},{6,22},{7,23},{8,24},{9,... | collective-permute-start | bytes 589832 | tf_op jit(solution)/shard_map/ppermute | solution.py:406
  127.1 5.4 %collective-permute-start.41 = (bf16[96,768]{1,0:T(8,128)(2,1)S(1)}, bf16[96,768]{1,0:T(8,128)(2,1)S(1)}, u32[]{:S(2)}, u32[]{:S(2)}) collective-permute-start(bf16[96,768]{1,0:T(8,128)(2,1)S(1)} %get-tuple-element.258.refs_1_), channel_id=1, source_target_pairs={{0,1},{1,0},{2,3},{3,2},{4,5},{5,4},{6,7},{7,6},{8,9},{9,8},{10,11... | collective-permute-start | bytes 442376 | tf_op jit(solution)/shard_map/ppermute | solution.py:406
  129.8 5.0 %collective-permute-start.43 = (bf16[96,768]{1,0:T(8,128)(2,1)S(1)}, bf16[96,768]{1,0:T(8,128)(2,1)S(1)}, u32[]{:S(2)}, u32[]{:S(2)}) collective-permute-start(bf16[96,768]{1,0:T(8,128)(2,1)S(1)} %collective-permute-done.42.refs_5_.refs_3_), channel_id=1, source_target_pairs={{0,1},{1,0},{2,3},{3,2},{4,5},{5,4},{6,7},{7,6},{8,9},{9,8},{10,11... | collective-permute-start | bytes 442376 | tf_op jit(solution)/shard_map/ppermute | solution.py:406
  135.3 5.7 %collective-permute-start.47 = (bf16[128,768]{1,0:T(8,128)(2,1)S(1)}, bf16[128,768]{1,0:T(8,128)(2,1)S(1)}, u32[]{:S(2)}, u32[]{:S(2)}) collective-permute-start(bf16[128,768]{1,0:T(8,128)(2,1)S(1)} %get-tuple-element.261.refs_5_), channel_id=1, source_target_pairs={{0,2},{1,3},{2,0},{3,1},{4,6},{5,7},{6,4},{7,5},{8,10},{9,11},{10,... | collective-permute-start | bytes 589832 | tf_op jit(solution)/shard_map/ppermute | solution.py:406
  136.0 6.5 %collective-permute-start.37 = (bf16[80,768]{1,0:T(8,128)(2,1)S(1)}, bf16[80,768]{1,0:T(8,128)(2,1)S(1)}, u32[]{:S(2)}, u32[]{:S(2)}) collective-permute-start(bf16[80,768]{1,0:T(8,128)(2,1)S(1)} %get-tuple-element.252), channel_id=1, source_target_pairs={{0,8},{1,9},{2,10},{3,11},{4,12},{5,13},{6,14},{7,15},{8,0},{9,1},... | collective-permute-start | bytes 368648 | tf_op jit(solution)/shard_map/ppermute | solution.py:406
  136.0 10.1 %collective-permute-start.38 = (bf16[80,768]{1,0:T(8,128)(2,1)S(1)}, bf16[80,768]{1,0:T(8,128)(2,1)S(1)}, u32[]{:S(2)}, u32[]{:S(2)}) collective-permute-start(bf16[80,768]{1,0:T(8,128)(2,1)S(1)} %get-tuple-element.253), channel_id=1, source_target_pairs={{0,16},{1,17},{2,18},{3,19},{4,20},{5,21},{6,22},{7,23},{8,24},{9,... | collective-permute-start | bytes 368648 | tf_op jit(solution)/shard_map/ppermute | solution.py:406
  138.5 7.6 %collective-permute-start.39 = (bf16[80,768]{1,0:T(8,128)(2,1)S(1)}, bf16[80,768]{1,0:T(8,128)(2,1)S(1)}, u32[]{:S(2)}, u32[]{:S(2)}) collective-permute-start(bf16[80,768]{1,0:T(8,128)(2,1)S(1)} %get-tuple-element.254), channel_id=1, source_target_pairs={{0,24},{1,25},{2,26},{3,27},{4,28},{5,29},{6,30},{7,31},{8,16},{9,... | collective-permute-start | bytes 368648 | tf_op jit(solution)/shard_map/ppermute | solution.py:406
  140.4 10.4 %collective-permute-start.46 = (bf16[128,768]{1,0:T(8,128)(2,1)S(1)}, bf16[128,768]{1,0:T(8,128)(2,1)S(1)}, u32[]{:S(2)}, u32[]{:S(2)}) collective-permute-start(bf16[128,768]{1,0:T(8,128)(2,1)S(1)} %get-tuple-element.261.refs_5_), channel_id=1, source_target_pairs={{0,1},{1,0},{2,3},{3,2},{4,5},{5,4},{6,7},{7,6},{8,9},{9,8},{10,11... | collective-permute-start | bytes 589832 | tf_op jit(solution)/shard_map/ppermute | solution.py:406
  141.1 12.0 %collective-permute-start.48 = (bf16[128,768]{1,0:T(8,128)(2,1)S(1)}, bf16[128,768]{1,0:T(8,128)(2,1)S(1)}, u32[]{:S(2)}, u32[]{:S(2)}) collective-permute-start(bf16[128,768]{1,0:T(8,128)(2,1)S(1)} %collective-permute-done.47.refs_7_), channel_id=1, source_target_pairs={{0,1},{1,0},{2,3},{3,2},{4,5},{5,4},{6,7},{7,6},{8,9},{9,8},{10,11... | collective-permute-start | bytes 589832 | tf_op jit(solution)/shard_map/ppermute | solution.py:406
  146.7 8.6 %collective-permute-start.45 = (bf16[80,768]{1,0:T(8,128)(2,1)S(1)}, bf16[80,768]{1,0:T(8,128)(2,1)S(1)}, u32[]{:S(2)}, u32[]{:S(2)}) collective-permute-start(bf16[80,768]{1,0:T(8,128)(2,1)S(1)} %get-tuple-element.260.refs_1_), channel_id=1, source_target_pairs={{0,2},{1,3},{2,0},{3,1},{4,6},{5,7},{6,4},{7,5},{8,10},{9,11},{10,... | collective-permute-start | bytes 368648 | tf_op jit(solution)/shard_map/ppermute | solution.py:406
  148.2 10.1 %collective-permute-start.33 = (bf16[128,768]{1,0:T(8,128)(2,1)S(1)}, bf16[128,768]{1,0:T(8,128)(2,1)S(1)}, u32[]{:S(2)}, u32[]{:S(2)}) collective-permute-start(bf16[128,768]{1,0:T(8,128)(2,1)S(1)} %get-tuple-element.244), channel_id=1, source_target_pairs={{0,0},{1,16},{2,2},{3,18},{4,4},{5,20},{6,6},{7,22},{8,8},{9,24},{... | collective-permute-start | bytes 589832 | tf_op jit(solution)/shard_map/ppermute | solution.py:406
  148.8 9.4 %collective-permute-start.34 = (bf16[128,768]{1,0:T(8,128)(2,1)S(1)}, bf16[128,768]{1,0:T(8,128)(2,1)S(1)}, u32[]{:S(2)}, u32[]{:S(2)}) collective-permute-start(bf16[128,768]{1,0:T(8,128)(2,1)S(1)} %get-tuple-element.245), channel_id=1, source_target_pairs={{0,8},{1,24},{2,10},{3,26},{4,12},{5,28},{6,14},{7,30},{8,0},{9,16... | collective-permute-start | bytes 589832 | tf_op jit(solution)/shard_map/ppermute | solution.py:406
  150.8 5.2 %collective-permute-start.44 = (bf16[80,768]{1,0:T(8,128)(2,1)S(1)}, bf16[80,768]{1,0:T(8,128)(2,1)S(1)}, u32[]{:S(2)}, u32[]{:S(2)}) collective-permute-start(bf16[80,768]{1,0:T(8,128)(2,1)S(1)} %get-tuple-element.260.refs_1_), channel_id=1, source_target_pairs={{0,1},{1,0},{2,3},{3,2},{4,5},{5,4},{6,7},{7,6},{8,9},{9,8},{10,11... | collective-permute-start | bytes 368648 | tf_op jit(solution)/shard_map/ppermute | solution.py:406
  (16 other events, 125.9 us)
where the time goes:
time: 162 us; the launch traced here: 160 us
  Pallas kernels  58.1 us (36%)
  waiting for transfers between devices  51.1 us (32%)
  starting transfers between devices  44.6 us (28%)
  local copies, waits for them, and re-layouts  4.23 us (3%)
    pallas_call x23, Pallas kernels, call(): pl.pallas_call(ordered, grid_spec=pltpu.PrefetchScalarGridSpec(num_scalar...  58.1 us
    ppermute x50, waiting for transfers between devices, permute(): return lax.ppermute(value, AXES, pairs)  51.1 us
    ppermute x50, starting transfers between devices, permute(): return lax.ppermute(value, AXES, pairs)  44.6 us
  transfers between devices with their start and end apart: 50, of which 26 were waited for; matrix products, arithmetic and copies ran while one was open for 2% of the time, Pallas kernels for 30%

commit v1 on v0

--- a/solution.py
+++ b/solution.py
@@ -1356,13 +1356,13 @@
         row_swap(jnp.concatenate([local_row(cotangent, index), padding], axis=0), second)
         for second, index in ((0, odd), (1, 1 - odd))
     ]
-    across[0], across[1], mark, cotangents[0] = lax.optimization_barrier((across[0], across[1], mark, cotangents[0]))
+    across[0], across[1], mark = lax.optimization_barrier((across[0], across[1], mark))
     there = across + [core_swap(block) for block in across]
     blocks = here + there
     (att, k_there, v_there, log_total), mark = attention(
         place, lengths, there, columns, value_row, q, summed, stats, (mark,)
     )
-    att, cotangents[1] = lax.optimization_barrier((att, cotangents[1]))
+    att, *cotangents = lax.optimization_barrier((att, *cotangents))
     att_got = core_swap(att)
     results, mark = forward(place, att, att_got, own, cotangents, weights, (mark,))
     (
@@ -1389,7 +1389,7 @@
         place, blocks, dq, dk, dv, token_far, far_got, (mark,)
     )
     (x_send, y_send, p, q_, down_send, down_two), mark = second_stage(
-        place, (x_got, y_got, px, qy, down_p, down_q), (mark,)
+        place, (x_got, y_got, px, qy, down_p, down_q), (mark, own_got)
     )
     x_got, y_got, down_got = x_swap(x_send), y_swap(y_send), z_swap(down_send, 1)
     px_send, qy_send, mark = lax.optimization_barrier((px_send, qy_send, mark))
@@ -1402,25 +1402,29 @@
     (up_send, up_keep), mark = end_stage(place, up_two, up_got, (mark, down_got))
     up_got = z_swap(up_send, 2)
     (down_unit,), mark = last_sum(place, ((down_keep, down_got),), (mark,))
-    down_all = gathered(down_unit)
+    down_across = x_swap(down_unit)
     (x_send, y_send, joint_p, joint_q), mark = joint_pair_stage(place, joint_pair, (mark,))
     joint_x_got, joint_y_got = x_swap(x_send), y_swap(y_send)
+    down_own, up_got = lax.optimization_barrier((down_unit, up_got))
+    down_all = (down_unit, core_swap(down_own), down_across, core_swap(down_across))
     (token0, token1), mark = token_last(place, (token_own, own_got, across, first_grad), (mark,))
     back = (row_swap(token0, 0), row_swap(token1, 1))
+    (up_unit,), mark = last_sum(place, ((up_keep, up_got),), (mark,))
+    up_all = gathered(up_unit)
     (keep, one, two, three), mark = joint_line_stage(
-        place, (joint_x_got, joint_y_got, joint_p, joint_q), (mark,)
+        place, (joint_x_got, joint_y_got, joint_p, joint_q), (mark, *down_all[1:])
     )
     joint_last = (keep, z_swap(one, 1), z_swap(two, 2), z_swap(three, 3))
-    (up_unit,), mark = last_sum(place, ((up_keep, up_got),), (mark, *down_all[1:]))
-    up_all = gathered(up_unit)
     joint_unit, mark = joint_sum(place, joint_last, (mark,))
+    joint_across = x_swap(joint_unit)
+    joint_across, first_back = lax.optimization_barrier((joint_across, back[0]))
+    joint_all = (joint_unit, core_swap(joint_unit), joint_across, core_swap(joint_across))
     (
         down_grad, up_grad, out_grad, second_gain_grad, second_shift_grad, down_bias_grad, first_gain_grad,
         first_shift_grad, out_bias_grad, up_bias_grad,
     ), mark = dense_outputs(place, (*down_all, *up_all), (mark,))
-    joint_all = gathered(joint_unit, mark)
     (joint_grad, query_bias_grad, value_bias_grad), mark = joint_outputs(place, joint_all, (mark,))
-    (outputs, token_grad), mark = back_rows(place, done, back, (mark,))
+    (outputs, token_grad), mark = back_rows(place, done, (first_back, back[1]), (mark,))
     return (
         outputs,
         token_grad,

time: 162 us -> 159 us (0.981); the launches traced: 160 us -> 159 us
  waiting for transfers between devices: 51.1 us -> 47.6 us
  starting transfers between devices: 44.6 us -> 46.9 us
    ppermute x50, waiting for transfers between devices: 51.1 us -> 47.6 us  [permute(): return lax.ppermute(value, AXES, pairs)]
    ppermute x50, starting transfers between devices: 44.6 us -> 46.9 us  [permute(): return lax.ppermute(value, AXES, pairs)]
  transfers between devices with their start and end apart: 50 -> 50, of which waited for: 26 -> 22; matrix products, arithmetic and copies ran while one was open for 2% -> 1% of each run, Pallas kernels for 30% -> 30%
where the time goes in v1:
time: 159 us
  Pallas kernels  57.8 us (36%)
  waiting for transfers between devices  47.6 us (30%)
  starting transfers between devices  46.9 us (29%)
  local copies, waits for them, and re-layouts  4.62 us (3%)
    pallas_call x23, Pallas kernels, call(): pl.pallas_call(ordered, grid_spec=pltpu.PrefetchScalarGridSpec(num_scalar...  57.8 us
    ppermute x50, waiting for transfers between devices, permute(): return lax.ppermute(value, AXES, pairs)  47.6 us
    ppermute x50, starting transfers between devices, permute(): return lax.ppermute(value, AXES, pairs)  46.9 us
  transfers between devices with their start and end apart: 50, of which 22 were waited for; matrix products, arithmetic and copies ran while one was open for 1% of the time, Pallas kernels for 30%

profile of v1, /device:TPU:0, one launch (start us, length us, event | category | flops | bytes accessed | tf_op | source)
XLA Modules:
  0.0 158.8 jit_solution(3101976606880070832)
XLA Ops:
  1.8 3.1 %collective-permute-start.1 = (bf16[128,768]{1,0:T(8,128)(2,1)S(1)}, bf16[128,768]{1,0:T(8,128)(2,1)S(1)}, u32[]{:S(2)}, u32[]{:S(2)}) collective-permute-start(bf16[128,768]{1,0:T(8,128)(2,1)S(1)} %get-tuple-element.289), channel_id=1, source_target_pairs={{0,8},{1,24},{2,10},{3,26},{4,12},{5,28},{6,14},{7,30},{8,0},{9,16... | collective-permute-start | bytes 589832 | tf_op jit(solution)/shard_map/ppermute | solution.py:406
  5.6 3.5 %collective-permute-start.2 = (s32[2,16]{1,0:T(2,128)}, s32[2,16]{1,0:T(2,128)S(1)}, u32[]{:S(2)}, u32[]{:S(2)}) collective-permute-start(s32[2,16]{1,0:T(2,128)} %refs_1_.4), channel_id=1, source_target_pairs={{0,1},{1,0},{2,3},{3,2},{4,5},{5,4},{6,7},{7,6},{8,9},{9,8},{10,11... | collective-permute-start | bytes 392 | tf_op jit(solution)/shard_map/ppermute | solution.py:406
  10.5 2.0 %copy-done.3 = bf16[768,2304]{1,0:T(8,128)(2,1)S(1)} copy-done((bf16[768,2304]{1,0:T(8,128)(2,1)S(1)}, bf16[768,2304]{1,0:T(8,128)(2,1)}, u32[]{:S(2)}) %copy-start.3) | copy-done | bytes 3538968
  12.5 1.5 own_columns.1
  14.0 2.0 %collective-permute-start.5 = (bf16[128,768]{1,0:T(8,128)(2,1)S(1)}, bf16[128,768]{1,0:T(8,128)(2,1)S(1)}, u32[]{:S(2)}, u32[]{:S(2)}) collective-permute-start(bf16[128,768]{1,0:T(8,128)(2,1)S(1)} %collective-permute-done.refs_3_.refs_6_.refs_1_), channel_id=1, source_target_pairs={{0,1},{1,0},{2,3},{3,2},{4,5},{5,4},{6,7},{7,6},{8,9},{9,8},{10,11... | collective-permute-start | bytes 589832 | tf_op jit(solution)/shard_map/ppermute | solution.py:406
  16.0 1.5 collective-permute-start.3
  18.9 5.0 %first_attention.1 = (bf16[512,384]{1,0:T(8,128)(2,1)S(1)}, bf16[512,384]{1,0:T(8,128)(2,1)S(1)}, bf16[512,384]{1,0:T(8,128)(2,1)S(1)}, f32[3,128,1024]{2,1,0:T(...) custom-call(s32[4]{0:T(128)S(1)} %pad_add_fusion.refs_0_, s32[2,16]{1,0:T(2,128)S(1)} %copy-done.5, ...), custom_call_target="tpu_custom_call" | custom-call | flops 1024 | bytes 1024 | tf_op jit(solution)/shard_map/first_attention/pallas_call | solution.py:369
  23.9 3.6 %collective-permute-done.4.refs_4_.refs_6_ = bf16[128,768]{1,0:T(8,128)(2,1)S(1)} collective-permute-done((bf16[128,768]{1,0:T(8,128)(2,1)S(1)}, bf16[128,768]{1,0:T(8,128)(2,1)S(1)}, u32[]{:S(2)}, u32[]{:S(2)}) %collective-permute-start.4) | collective-permute-done | bytes 196640 | tf_op jit(solution)/shard_map/ppermute | solution.py:406
  29.9 5.0 %attention.1 = (bf16[512,384]{1,0:T(8,128)(2,1)S(1)}, bf16[512,384]{1,0:T(8,128)(2,1)S(1)}, bf16[512,384]{1,0:T(8,128)(2,1)S(1)}, f32[8,512]{1,0:T(8,128)S(1)}, f32[8,128]{1,0:T(8,128)S(1)}) custom-call(s32[4]{0:T(128)S(1)} %pad_add_fusion.refs_0_, s32[2,16]{1,0:T(2,128)S(1)} %copy-done.5, s32[2,16]{1,0:T(2,128)S(1)} %collective-permute-done.2.refs_2_, ...), custom_call_target="tpu_custom_call" | custom-call | flops 1024 | bytes 1024 | tf_op jit(solution)/shard_map/attention/pallas_call | solution.py:369
  35.4 1.3 collective-permute-done.11.refs_2_
  36.7 6.4 %forward.1 = (bf16[128,768]{1,0:T(8,128)(2,1)S(1)}, bf16[128,768]{1,0:T(8,128)(2,1)S(1)}, bf16[272,768]{1,0:T(8,128)(2,1)S(1)}, f32[256,768]{1,0:T(8,128)S(1)}, ...) custom-call(s32[4]{0:T(128)S(1)} %pad_add_fusion.refs_0_, ...), custom_call_target="tpu_custom_call" | custom-call | flops 1024 | bytes 1024 | tf_op jit(solution)/shard_map/forward/pallas_call | solution.py:369
  43.9 2.1 %collective-permute-done.15.refs_4_.refs_12_ = bf16[272,768]{1,0:T(8,128)(2,1)S(1)} collective-permute-done((bf16[272,768]{1,0:T(8,128)(2,1)S(1)}, bf16[272,768]{1,0:T(8,128)(2,1)S(1)}, u32[]{:S(2)}, u32[]{:S(2)}) %collective-permute-start.15) | collective-permute-done | bytes 417824 | tf_op jit(solution)/shard_map/ppermute | solution.py:406
  46.0 2.6 %down_units.1 = (bf16[4,2,48,768]{3,2,1,0:T(8,128)(2,1)S(1)}, bf16[4,2,48,768]{3,2,1,0:T(8,128)(2,1)S(1)}, bf16[4,2,48,768]{3,2,1,0:T(8,128)(2,1)S(1)}, bf16[4,2,48,768]{3,2,1,0:T(8,128)(2,1)S(1)}, f32[8,128]{1,0:T(8,128)S(1)}) custom-call(s32[4]{0:T(128)S(1)} %pad_add_fusion.refs_0_, bf16[16,96,256]{2,1,0:T(8,128)(2,1)S(1)} %get-tuple-element.183.refs_1_, ...), custom_call_target="tpu_custom_call" | custom-call | flops 1024 | bytes 1024 | tf_op jit(solution)/shard_map/down_units/pallas_call | solution.py:369
  48.7 1.6 collective-permute-start.18
  50.2 1.5 collective-permute-start.19
  51.7 5.0 %backward.1 = (bf16[256,768]{1,0:T(8,128)(2,1)S(1)}, bf16[256,768]{1,0:T(8,128)(2,1)S(1)}, bf16[256,768]{1,0:T(8,128)(2,1)S(1)}, bf16[256,768]{1,0:T(8,128)(2,1)...) custom-call(s32[4]{0:T(128)S(1)} %pad_add_fusion.refs_0_, ...), custom_call_target="tpu_custom_call" | custom-call | flops 1024 | bytes 1024 | tf_op jit(solution)/shard_map/backward/pallas_call | solution.py:369
  57.4 1.7 %collective-permute-done.20.refs_5_ = bf16[256,768]{1,0:T(8,128)(2,1)S(1)} collective-permute-done((bf16[256,768]{1,0:T(8,128)(2,1)S(1)}, bf16[256,768]{1,0:T(8,128)(2,1)S(1)}, u32[]{:S(2)}, u32[]{:S(2)}) %collective-permute-start.20) | collective-permute-done | bytes 393248 | tf_op jit(solution)/shard_map/ppermute | solution.py:406
  59.7 3.3 %up_units.1 = (bf16[704,768]{1,0:T(8,128)(2,1)S(1)}, bf16[704,768]{1,0:T(8,128)(2,1)S(1)}, bf16[4,2,64,768]{3,2,1,0:T(8,128)(2,1)S(1)}, bf16[4,2,64,768]{3,2,1,0:T(8,128)(2,1)S(1)}, f32[8,128]{1,0:T(8,128)S(1)}) custom-call(s32[4]{0:T(128)S(1)} %pad_add_fusion.refs_0_, bf16[768,256]{1,0:T(8,128)(2,1)S(1)} %get-tuple-element.194.refs_1_, ...), custom_call_target="tpu_custom_call" | custom-call | flops 1024 | bytes 1024 | tf_op jit(solution)/shard_map/up_units/pallas_call | solution.py:369
  63.0 1.2 collective-permute-done.18.refs_2_
  64.2 1.2 collective-permute-done.19.refs_4_
  67.2 1.5 collective-permute-start.24
  70.0 10.1 %attention_back.1 = (bf16[512,384]{1,0:T(8,128)(2,1)S(1)}, bf16[1024,384]{1,0:T(8,128)(2,1)S(1)}, bf16[1024,384]{1,0:T(8,128)(2,1)S(1)}, f32[8,128]{1,0:T(8,128)S(1)}) custom-call(s32[4]{0:T(128)S(1)} %pad_add_fusion.refs_0_, s32[2,16]{1,0:T(2,128)S(1)} %copy-done.5, s32[2,16]{1,0:T(2,128)S(1)} %collective-permute-done.2.refs_2_, ...), custom_call_target="tpu_custom_call" | custom-call | flops 1024 | bytes 1024 | tf_op jit(solution)/shard_map/attention_back/pallas_call | solution.py:369
  80.1 2.8 %token_parts.1 = (bf16[256,768]{1,0:T(8,128)(2,1)S(1)}, bf16[256,768]{1,0:T(8,128)(2,1)S(1)}, bf16[256,768]{1,0:T(8,128)(2,1)S(1)}, bf16[256,768]{1,0:T(8,128)(2,1)S(1)}, f32[8,128]{1,0:T(8,128)S(1)}) custom-call(s32[4]{0:T(128)S(1)} %pad_add_fusion.refs_0_, bf16[512,384]{1,0:T(8,128)(2,1)S(1)} %get-tuple-element.208.refs_1_.refs_9_, ...), custom_call_target="tpu_custom_call" | custom-call | flops 1024 | bytes 1024 | tf_op jit(solution)/shard_map/token_parts/pallas_call | solution.py:369
  82.9 2.8 %collective-permute-start.22 = (bf16[256,768]{1,0:T(8,128)(2,1)S(1)}, bf16[256,768]{1,0:T(8,128)(2,1)S(1)}, u32[]{:S(2)}, u32[]{:S(2)}) collective-permute-start(bf16[256,768]{1,0:T(8,128)(2,1)S(1)} %get-tuple-element.213), channel_id=1, source_target_pairs={{0,1},{1,0},{2,3},{3,2},{4,5},{5,4},{6,7},{7,6},{8,9},{9,8},{10,11... | collective-permute-start | bytes 1179656 | tf_op jit(solution)/shard_map/ppermute | solution.py:406
  85.8 1.3 collective-permute-done.22.refs_13_
  87.0 3.2 %joint_units.1 = (bf16[4,2,48,768]{3,2,1,0:T(8,128)(2,1)S(1)}, bf16[4,2,48,768]{3,2,1,0:T(8,128)(2,1)S(1)}, bf16[512,768]{1,0:T(8,128)(2,1)S(1)}, bf16[4,2,32,768]{3,2,1,0:T(8,128)(2,1)S(1)}, f32[8,128]{1,0:T(8,128)S(1)}) custom-call(s32[4]{0:T(128)S(1)} %pad_add_fusion.refs_0_, bf16[128,768]{1,0:T(8,128)(2,1)S(1)} %collective-permute-done.refs_3_.refs_6_.refs_1_, ...), custom_call_target="tpu_custom_call" | custom-call | flops 1024 | bytes 1024 | tf_op jit(solution)/shard_map/joint_units/pallas_call | solution.py:369
  90.3 1.3 collective-permute-done.23.refs_1_
  92.9 1.5 collective-permute-start.28
  94.4 1.5 collective-permute-start.29
  97.6 5.7 %collective-permute-done.30.refs_6_ = bf16[2,96,768]{2,1,0:T(8,128)(2,1)S(1)} collective-permute-done((bf16[2,96,768]{2,1,0:T(8,128)(2,1)S(1)}, bf16[2,96,768]{2,1,0:T(8,128)(2,1)S(1)}, u32[]{:S(2)}, u32[]{:S(2)}) %collective-permute-start.30) | collective-permute-done | bytes 294944 | tf_op jit(solution)/shard_map/ppermute | solution.py:406
  103.4 1.7 %collective-permute-done.28.refs_1_ = bf16[256,768]{1,0:T(8,128)(2,1)S(1)} collective-permute-done((bf16[256,768]{1,0:T(8,128)(2,1)S(1)}, bf16[256,768]{1,0:T(8,128)(2,1)S(1)}, u32[]{:S(2)}, u32[]{:S(2)}) %collective-permute-start.28) | collective-permute-done | bytes 393248 | tf_op jit(solution)/shard_map/ppermute | solution.py:406
  105.0 1.4 collective-permute-done.29.refs_2_
  107.9 2.1 %collective-permute-start.31 = (bf16[96,768]{1,0:T(8,128)(2,1)S(1)}, bf16[96,768]{1,0:T(8,128)(2,1)S(1)}, u32[]{:S(2)}, u32[]{:S(2)}) collective-permute-start(bf16[96,768]{1,0:T(8,128)(2,1)S(1)} %get-tuple-element.238), channel_id=1, source_target_pairs={{0,16},{1,17},{2,18},{3,19},{4,20},{5,21},{6,22},{7,23},{8,24},{9,... | collective-permute-start | bytes 442376 | tf_op jit(solution)/shard_map/ppermute | solution.py:406
  110.0 5.4 %collective-permute-done.31.refs_4_.refs_2_ = bf16[96,768]{1,0:T(8,128)(2,1)S(1)} collective-permute-done((bf16[96,768]{1,0:T(8,128)(2,1)S(1)}, bf16[96,768]{1,0:T(8,128)(2,1)S(1)}, u32[]{:S(2)}, u32[]{:S(2)}) %collective-permute-start.31) | collective-permute-done | bytes 147488 | tf_op jit(solution)/shard_map/ppermute | solution.py:406
  115.4 1.3 collective-permute-done.32.refs_2_
  117.4 2.9 %collective-permute-start.35 = (bf16[128,768]{1,0:T(8,128)(2,1)S(1)}, bf16[128,768]{1,0:T(8,128)(2,1)S(1)}, u32[]{:S(2)}, u32[]{:S(2)}) collective-permute-start(bf16[128,768]{1,0:T(8,128)(2,1)S(1)} %get-tuple-element.250), channel_id=1, source_target_pairs={{0,16},{1,17},{2,18},{3,19},{4,20},{5,21},{6,22},{7,23},{8,24},{9,... | collective-permute-start | bytes 589832 | tf_op jit(solution)/shard_map/ppermute | solution.py:406
  123.4 1.4 collective-permute-start.33
  124.7 1.9 %collective-permute-done.37.refs_7_.refs_3_ = bf16[96,768]{1,0:T(8,128)(2,1)S(1)} collective-permute-done((bf16[96,768]{1,0:T(8,128)(2,1)S(1)}, bf16[96,768]{1,0:T(8,128)(2,1)S(1)}, u32[]{:S(2)}, u32[]{:S(2)}) %collective-permute-start.37) | collective-permute-done | bytes 147488 | tf_op jit(solution)/shard_map/ppermute | solution.py:406
  126.6 1.6 collective-permute-done.35.refs_2_
  130.9 2.0 %collective-permute-start.39 = (bf16[80,768]{1,0:T(8,128)(2,1)S(1)}, bf16[80,768]{1,0:T(8,128)(2,1)S(1)}, u32[]{:S(2)}, u32[]{:S(2)}) collective-permute-start(bf16[80,768]{1,0:T(8,128)(2,1)S(1)} %get-tuple-element.259), channel_id=1, source_target_pairs={{0,8},{1,9},{2,10},{3,11},{4,12},{5,13},{6,14},{7,15},{8,0},{9,1},... | collective-permute-start | bytes 368648 | tf_op jit(solution)/shard_map/ppermute | solution.py:406
  132.9 1.7 %collective-permute-start.40 = (bf16[80,768]{1,0:T(8,128)(2,1)S(1)}, bf16[80,768]{1,0:T(8,128)(2,1)S(1)}, u32[]{:S(2)}, u32[]{:S(2)}) collective-permute-start(bf16[80,768]{1,0:T(8,128)(2,1)S(1)} %get-tuple-element.260), channel_id=1, source_target_pairs={{0,16},{1,17},{2,18},{3,19},{4,20},{5,21},{6,22},{7,23},{8,24},{9,... | collective-permute-start | bytes 368648 | tf_op jit(solution)/shard_map/ppermute | solution.py:406
  136.0 1.8 %collective-permute-done.39.refs_2_ = bf16[80,768]{1,0:T(8,128)(2,1)S(1)} collective-permute-done((bf16[80,768]{1,0:T(8,128)(2,1)S(1)}, bf16[80,768]{1,0:T(8,128)(2,1)S(1)}, u32[]{:S(2)}, u32[]{:S(2)}) %collective-permute-start.39) | collective-permute-done | bytes 122912 | tf_op jit(solution)/shard_map/ppermute | solution.py:406
  137.8 9.3 %collective-permute-done.40.refs_3_ = bf16[80,768]{1,0:T(8,128)(2,1)S(1)} collective-permute-done((bf16[80,768]{1,0:T(8,128)(2,1)S(1)}, bf16[80,768]{1,0:T(8,128)(2,1)S(1)}, u32[]{:S(2)}, u32[]{:S(2)}) %collective-permute-start.40) | collective-permute-done | bytes 122912 | tf_op jit(solution)/shard_map/ppermute | solution.py:406
  149.3 1.9 %collective-permute-start.44 = (bf16[128,768]{1,0:T(8,128)(2,1)S(1)}, bf16[128,768]{1,0:T(8,128)(2,1)S(1)}, u32[]{:S(2)}, u32[]{:S(2)}) collective-permute-start(bf16[128,768]{1,0:T(8,128)(2,1)S(1)} %get-tuple-element.266), channel_id=1, source_target_pairs={{0,8},{1,24},{2,10},{3,26},{4,12},{5,28},{6,14},{7,30},{8,0},{9,16... | collective-permute-start | bytes 589832 | tf_op jit(solution)/shard_map/ppermute | solution.py:406
  151.3 1.5 collective-permute-done.42.refs_3_
  152.7 2.3 %dense_outputs.1 = (f32[384,768]{1,0:T(8,128)}, f32[96,3072]{1,0:T(8,128)}, f32[96,768]{1,0:T(8,128)}, f32[1,96]{1,0:T(1,128)}, f32[1,96]{1,0:T(1,128)}, /*index...) custom-call(s32[4]{0:T(128)S(1)} %pad_add_fusion.refs_0_, ...), custom_call_target="tpu_custom_call" | custom-call | flops 1024 | bytes 1024 | tf_op jit(solution)/shard_map/dense_outputs/pallas_call | solution.py:369
  155.6 1.5 joint_outputs.1
  157.2 1.6 %back_rows.1 = (bf16[2,128,768]{2,1,0:T(8,128)(2,1)}, f32[2,128,768]{2,1,0:T(8,128)}, f32[8,128]{1,0:T(8,128)}) custom-call(s32[4]{0:T(128)S(1)} %pad_add_fusion.refs_0_, bf16[128,768]{1,0:T(8,128)(2,1)S(1)} %collective-permute-done.12.refs_6_.refs_1_, bf16[128,768]{1,0:T(8,128)(2,1)S(1)} %collective-permute-done.13.refs_7_.refs_2_, ...), custom_call_target="tpu_custom_call" | custom-call | flops 1024 | bytes 1024 | tf_op jit(solution)/shard_map/back_rows/pallas_call | solution.py:369
  (115 shorter events, 27.6 us)
Async XLA Ops:
  1.8 12.2 %collective-permute-start.1 = (bf16[128,768]{1,0:T(8,128)(2,1)S(1)}, bf16[128,768]{1,0:T(8,128)(2,1)S(1)}, u32[]{:S(2)}, u32[]{:S(2)}) collective-permute-start(bf16[128,768]{1,0:T(8,128)(2,1)S(1)} %get-tuple-element.289), channel_id=1, source_target_pairs={{0,8},{1,24},{2,10},{3,26},{4,12},{5,28},{6,14},{7,30},{8,0},{9,16... | collective-permute-start | bytes 589832 | tf_op jit(solution)/shard_map/ppermute | solution.py:406
  4.9 9.1 %collective-permute-start = (bf16[128,768]{1,0:T(8,128)(2,1)S(1)}, bf16[128,768]{1,0:T(8,128)(2,1)S(1)}, u32[]{:S(2)}, u32[]{:S(2)}) collective-permute-start(bf16[128,768]{1,0:T(8,128)(2,1)S(1)} %get-tuple-element.290), channel_id=1, source_target_pairs={{0,0},{1,16},{2,2},{3,18},{4,4},{5,20},{6,6},{7,22},{8,8},{9,24},{... | collective-permute-start | bytes 589832 | tf_op jit(solution)/shard_map/ppermute | solution.py:406
  5.6 8.4 %collective-permute-start.2 = (s32[2,16]{1,0:T(2,128)}, s32[2,16]{1,0:T(2,128)S(1)}, u32[]{:S(2)}, u32[]{:S(2)}) collective-permute-start(s32[2,16]{1,0:T(2,128)} %refs_1_.4), channel_id=1, source_target_pairs={{0,1},{1,0},{2,3},{3,2},{4,5},{5,4},{6,7},{7,6},{8,9},{9,8},{10,11... | collective-permute-start | bytes 392 | tf_op jit(solution)/shard_map/ppermute | solution.py:406
  14.0 4.8 %collective-permute-start.5 = (bf16[128,768]{1,0:T(8,128)(2,1)S(1)}, bf16[128,768]{1,0:T(8,128)(2,1)S(1)}, u32[]{:S(2)}, u32[]{:S(2)}) collective-permute-start(bf16[128,768]{1,0:T(8,128)(2,1)S(1)} %collective-permute-done.refs_3_.refs_6_.refs_1_), channel_id=1, source_target_pairs={{0,1},{1,0},{2,3},{3,2},{4,5},{5,4},{6,7},{7,6},{8,9},{9,8},{10,11... | collective-permute-start | bytes 589832 | tf_op jit(solution)/shard_map/ppermute | solution.py:406
  16.0 2.9 %collective-permute-start.6 = (bf16[128,768]{1,0:T(8,128)(2,1)S(1)}, bf16[128,768]{1,0:T(8,128)(2,1)S(1)}, u32[]{:S(2)}, u32[]{:S(2)}) collective-permute-start(bf16[128,768]{1,0:T(8,128)(2,1)S(1)} %collective-permute-done.1.refs_4_.refs_7_.refs_2_), channel_id=1, source_target_pairs={{0,1},{1,0},{2,3},{3,2},{4,5},{5,4},{6,7},{7,6},{8,9},{9,8},{10,11... | collective-permute-start | bytes 589832 | tf_op jit(solution)/shard_map/ppermute | solution.py:406
  16.0 7.9 %collective-permute-start.3 = (bf16[128,768]{1,0:T(8,128)(2,1)S(1)}, bf16[128,768]{1,0:T(8,128)(2,1)S(1)}, u32[]{:S(2)}, u32[]{:S(2)}) collective-permute-start(bf16[128,768]{1,0:T(8,128)(2,1)S(1)} %collective-permute-done.refs_3_.refs_6_.refs_1_), channel_id=1, source_target_pairs={{0,4},{1,5},{2,6},{3,7},{4,0},{5,1},{6,2},{7,3},{8,12},{9,13},{10,... | collective-permute-start | bytes 589832 | tf_op jit(solution)/shard_map/ppermute | solution.py:406
  17.5 10.0 %collective-permute-start.4 = (bf16[128,768]{1,0:T(8,128)(2,1)S(1)}, bf16[128,768]{1,0:T(8,128)(2,1)S(1)}, u32[]{:S(2)}, u32[]{:S(2)}) collective-permute-start(bf16[128,768]{1,0:T(8,128)(2,1)S(1)} %collective-permute-done.1.refs_4_.refs_7_.refs_2_), channel_id=1, source_target_pairs={{0,4},{1,5},{2,6},{3,7},{4,0},{5,1},{6,2},{7,3},{8,12},{9,13},{10,... | collective-permute-start | bytes 589832 | tf_op jit(solution)/shard_map/ppermute | solution.py:406
  18.1 16.8 %collective-permute-start.9 = (bf16[144,768]{1,0:T(8,128)(2,1)S(1)}, bf16[144,768]{1,0:T(8,128)(2,1)S(1)}, u32[]{:S(2)}, u32[]{:S(2)}) collective-permute-start(bf16[144,768]{1,0:T(8,128)(2,1)S(1)} %concatenate.6), channel_id=1, source_target_pairs={{0,0},{1,16},{2,2},{3,18},{4,4},{5,20},{6,6},{7,22},{8,8},{9,24},{... | collective-permute-start | bytes 663560 | tf_op jit(solution)/shard_map/ppermute | solution.py:406
  18.8 16.1 %collective-permute-start.10 = (bf16[144,768]{1,0:T(8,128)(2,1)S(1)}, bf16[144,768]{1,0:T(8,128)(2,1)S(1)}, u32[]{:S(2)}, u32[]{:S(2)}) collective-permute-start(bf16[144,768]{1,0:T(8,128)(2,1)S(1)} %concatenate.7), channel_id=1, source_target_pairs={{0,8},{1,24},{2,10},{3,26},{4,12},{5,28},{6,14},{7,30},{8,0},{9,16... | collective-permute-start | bytes 663560 | tf_op jit(solution)/shard_map/ppermute | solution.py:406
  27.5 1.9 %collective-permute-start.7 = (bf16[128,768]{1,0:T(8,128)(2,1)S(1)}, bf16[128,768]{1,0:T(8,128)(2,1)S(1)}, u32[]{:S(2)}, u32[]{:S(2)}) collective-permute-start(bf16[128,768]{1,0:T(8,128)(2,1)S(1)} %collective-permute-done.3.refs_3_.refs_5_), channel_id=1, source_target_pairs={{0,1},{1,0},{2,3},{3,2},{4,5},{5,4},{6,7},{7,6},{8,9},{9,8},{10,11... | collective-permute-start | bytes 589832 | tf_op jit(solution)/shard_map/ppermute | solution.py:406
  43.1 3.0 %collective-permute-start.14 = (bf16[16,96,256]{2,1,0:T(8,128)(2,1)S(1)}, bf16[16,96,256]{2,1,0:T(8,128)(2,1)S(1)}, u32[]{:S(2)}, u32[]{:S(2)}) collective-permute-start(bf16[16,96,256]{2,1,0:T(8,128)(2,1)S(1)} %get-tuple-element.184), channel_id=1, source_target_pairs={{0,1},{1,0},{2,3},{3,2},{4,5},{5,4},{6,7},{7,6},{8,9},{9,8},{10,11... | collective-permute-start | bytes 2359304 | tf_op jit(solution)/shard_map/ppermute | solution.py:406
  43.4 2.6 %collective-permute-start.15 = (bf16[272,768]{1,0:T(8,128)(2,1)S(1)}, bf16[272,768]{1,0:T(8,128)(2,1)S(1)}, u32[]{:S(2)}, u32[]{:S(2)}) collective-permute-start(bf16[272,768]{1,0:T(8,128)(2,1)S(1)} %get-tuple-element.178.refs_3_.refs_1_), channel_id=1, source_target_pairs={{0,1},{1,0},{2,3},{3,2},{4,5},{5,4},{6,7},{7,6},{8,9},{9,8},{10,11... | collective-permute-start | bytes 1253384 | tf_op jit(solution)/shard_map/ppermute | solution.py:406
  43.6 8.1 %collective-permute-start.16 = (bf16[256,768]{1,0:T(8,128)(2,1)S(1)}, bf16[256,768]{1,0:T(8,128)(2,1)S(1)}, u32[]{:S(2)}, u32[]{:S(2)}) collective-permute-start(bf16[256,768]{1,0:T(8,128)(2,1)S(1)} %get-tuple-element.187), channel_id=1, source_target_pairs={{0,1},{1,0},{2,3},{3,2},{4,5},{5,4},{6,7},{7,6},{8,9},{9,8},{10,11... | collective-permute-start | bytes 1179656 | tf_op jit(solution)/shard_map/ppermute | solution.py:406
  48.7 15.6 %collective-permute-start.18 = (bf16[4,2,48,768]{3,2,1,0:T(8,128)(2,1)S(1)}, bf16[4,2,48,768]{3,2,1,0:T(8,128)(2,1)S(1)}, u32[]{:S(2)}, u32[]{:S(2)}) collective-permute-start(bf16[4,2,48,768]{3,2,1,0:T(8,128)(2,1)S(1)} %get-tuple-element.191), channel_id=1, source_target_pairs={{0,2},{1,3},{2,0},{3,1},{4,6},{5,7},{6,4},{7,5},{8,10},{9,11},{10,... | collective-permute-start | bytes 1769480 | tf_op jit(solution)/shard_map/ppermute | solution.py:406
  50.2 15.2 %collective-permute-start.19 = (bf16[4,2,48,768]{3,2,1,0:T(8,128)(2,1)S(1)}, bf16[4,2,48,768]{3,2,1,0:T(8,128)(2,1)S(1)}, u32[]{:S(2)}, u32[]{:S(2)}) collective-permute-start(bf16[4,2,48,768]{3,2,1,0:T(8,128)(2,1)S(1)} %get-tuple-element.193), channel_id=1, source_target_pairs={{0,4},{1,5},{2,6},{3,7},{4,0},{5,1},{6,2},{7,3},{8,12},{9,13},{10,... | collective-permute-start | bytes 1769480 | tf_op jit(solution)/shard_map/ppermute | solution.py:406
  56.8 3.0 %collective-permute-start.17 = (bf16[272,768]{1,0:T(8,128)(2,1)S(1)}, bf16[272,768]{1,0:T(8,128)(2,1)S(1)}, u32[]{:S(2)}, u32[]{:S(2)}) collective-permute-start(bf16[272,768]{1,0:T(8,128)(2,1)S(1)} %get-tuple-element.189), channel_id=1, source_target_pairs={{0,1},{1,0},{2,3},{3,2},{4,5},{5,4},{6,7},{7,6},{8,9},{9,8},{10,11... | collective-permute-start | bytes 1253384 | tf_op jit(solution)/shard_map/ppermute | solution.py:406
  56.9 2.3 %collective-permute-start.20 = (bf16[256,768]{1,0:T(8,128)(2,1)S(1)}, bf16[256,768]{1,0:T(8,128)(2,1)S(1)}, u32[]{:S(2)}, u32[]{:S(2)}) collective-permute-start(bf16[256,768]{1,0:T(8,128)(2,1)S(1)} %get-tuple-element.197), channel_id=1, source_target_pairs={{0,1},{1,0},{2,3},{3,2},{4,5},{5,4},{6,7},{7,6},{8,9},{9,8},{10,11... | collective-permute-start | bytes 1179656 | tf_op jit(solution)/shard_map/ppermute | solution.py:406
  57.4 2.4 %collective-permute-start.21 = (bf16[256,768]{1,0:T(8,128)(2,1)S(1)}, bf16[256,768]{1,0:T(8,128)(2,1)S(1)}, u32[]{:S(2)}, u32[]{:S(2)}) collective-permute-start(bf16[256,768]{1,0:T(8,128)(2,1)S(1)} %get-tuple-element.198), channel_id=1, source_target_pairs={{0,1},{1,0},{2,3},{3,2},{4,5},{5,4},{6,7},{7,6},{8,9},{9,8},{10,11... | collective-permute-start | bytes 1179656 | tf_op jit(solution)/shard_map/ppermute | solution.py:406
  66.6 25.0 %collective-permute-start.23 = (bf16[704,768]{1,0:T(8,128)(2,1)S(1)}, bf16[704,768]{1,0:T(8,128)(2,1)S(1)}, u32[]{:S(2)}, u32[]{:S(2)}) collective-permute-start(bf16[704,768]{1,0:T(8,128)(2,1)S(1)} %get-tuple-element.218), channel_id=1, source_target_pairs={{0,2},{1,3},{2,0},{3,1},{4,6},{5,7},{6,4},{7,5},{8,10},{9,11},{10,... | collective-permute-start | bytes 3244040 | tf_op jit(solution)/shard_map/ppermute | solution.py:406
  67.2 24.7 %collective-permute-start.24 = (bf16[704,768]{1,0:T(8,128)(2,1)S(1)}, bf16[704,768]{1,0:T(8,128)(2,1)S(1)}, u32[]{:S(2)}, u32[]{:S(2)}) collective-permute-start(bf16[704,768]{1,0:T(8,128)(2,1)S(1)} %get-tuple-element.219), channel_id=1, source_target_pairs={{0,4},{1,5},{2,6},{3,7},{4,0},{5,1},{6,2},{7,3},{8,12},{9,13},{10,... | collective-permute-start | bytes 3244040 | tf_op jit(solution)/shard_map/ppermute | solution.py:406
  68.7 11.4 %collective-permute-start.12 = (bf16[128,768]{1,0:T(8,128)(2,1)S(1)}, bf16[128,768]{1,0:T(8,128)(2,1)S(1)}, u32[]{:S(2)}, u32[]{:S(2)}) collective-permute-start(bf16[128,768]{1,0:T(8,128)(2,1)S(1)} %get-tuple-element.171), channel_id=1, source_target_pairs={{0,0},{1,16},{2,2},{3,18},{4,4},{5,20},{6,6},{7,22},{8,8},{9,24},{... | collective-permute-start | bytes 589832 | tf_op jit(solution)/shard_map/ppermute | solution.py:406
  69.4 10.8 %collective-permute-start.13 = (bf16[128,768]{1,0:T(8,128)(2,1)S(1)}, bf16[128,768]{1,0:T(8,128)(2,1)S(1)}, u32[]{:S(2)}, u32[]{:S(2)}) collective-permute-start(bf16[128,768]{1,0:T(8,128)(2,1)S(1)} %get-tuple-element.172), channel_id=1, source_target_pairs={{0,8},{1,24},{2,10},{3,26},{4,12},{5,28},{6,14},{7,30},{8,0},{9,16... | collective-permute-start | bytes 589832 | tf_op jit(solution)/shard_map/ppermute | solution.py:406
  82.9 4.1 %collective-permute-start.22 = (bf16[256,768]{1,0:T(8,128)(2,1)S(1)}, bf16[256,768]{1,0:T(8,128)(2,1)S(1)}, u32[]{:S(2)}, u32[]{:S(2)}) collective-permute-start(bf16[256,768]{1,0:T(8,128)(2,1)S(1)} %get-tuple-element.213), channel_id=1, source_target_pairs={{0,1},{1,0},{2,3},{3,2},{4,5},{5,4},{6,7},{7,6},{8,9},{9,8},{10,11... | collective-permute-start | bytes 1179656 | tf_op jit(solution)/shard_map/ppermute | solution.py:406
  85.7 4.6 %collective-permute-start.25 = (bf16[256,768]{1,0:T(8,128)(2,1)S(1)}, bf16[256,768]{1,0:T(8,128)(2,1)S(1)}, u32[]{:S(2)}, u32[]{:S(2)}) collective-permute-start(bf16[256,768]{1,0:T(8,128)(2,1)S(1)} %get-tuple-element.225), channel_id=1, source_target_pairs={{0,1},{1,0},{2,3},{3,2},{4,5},{5,4},{6,7},{7,6},{8,9},{9,8},{10,11... | collective-permute-start | bytes 1179656 | tf_op jit(solution)/shard_map/ppermute | solution.py:406
  92.9 12.1 %collective-permute-start.28 = (bf16[256,768]{1,0:T(8,128)(2,1)S(1)}, bf16[256,768]{1,0:T(8,128)(2,1)S(1)}, u32[]{:S(2)}, u32[]{:S(2)}) collective-permute-start(bf16[256,768]{1,0:T(8,128)(2,1)S(1)} %get-tuple-element.230), channel_id=1, source_target_pairs={{0,2},{1,3},{2,0},{3,1},{4,6},{5,7},{6,4},{7,5},{8,10},{9,11},{10,... | collective-permute-start | bytes 1179656 | tf_op jit(solution)/shard_map/ppermute | solution.py:406
  94.4 12.1 %collective-permute-start.29 = (bf16[256,768]{1,0:T(8,128)(2,1)S(1)}, bf16[256,768]{1,0:T(8,128)(2,1)S(1)}, u32[]{:S(2)}, u32[]{:S(2)}) collective-permute-start(bf16[256,768]{1,0:T(8,128)(2,1)S(1)} %get-tuple-element.231), channel_id=1, source_target_pairs={{0,4},{1,5},{2,6},{3,7},{4,0},{5,1},{6,2},{7,3},{8,12},{9,13},{10,... | collective-permute-start | bytes 1179656 | tf_op jit(solution)/shard_map/ppermute | solution.py:406
  95.9 25.6 %collective-permute-start.27 = (bf16[512,768]{1,0:T(8,128)(2,1)S(1)}, bf16[512,768]{1,0:T(8,128)(2,1)S(1)}, u32[]{:S(2)}, u32[]{:S(2)}) collective-permute-start(bf16[512,768]{1,0:T(8,128)(2,1)S(1)} %get-tuple-element.229), channel_id=1, source_target_pairs={{0,4},{1,5},{2,6},{3,7},{4,0},{5,1},{6,2},{7,3},{8,12},{9,13},{10,... | collective-permute-start | bytes 2359304 | tf_op jit(solution)/shard_map/ppermute | solution.py:406
  96.4 6.9 %collective-permute-start.30 = (bf16[2,96,768]{2,1,0:T(8,128)(2,1)S(1)}, bf16[2,96,768]{2,1,0:T(8,128)(2,1)S(1)}, u32[]{:S(2)}, u32[]{:S(2)}) collective-permute-start(bf16[2,96,768]{2,1,0:T(8,128)(2,1)S(1)} %get-tuple-element.235), channel_id=1, source_target_pairs={{0,8},{1,9},{2,10},{3,11},{4,12},{5,13},{6,14},{7,15},{8,0},{9,1},... | collective-permute-start | bytes 884744 | tf_op jit(solution)/shard_map/ppermute | solution.py:406
  97.0 24.5 %collective-permute-start.26 = (bf16[4,2,48,768]{3,2,1,0:T(8,128)(2,1)S(1)}, bf16[4,2,48,768]{3,2,1,0:T(8,128)(2,1)S(1)}, u32[]{:S(2)}, u32[]{:S(2)}) collective-permute-start(bf16[4,2,48,768]{3,2,1,0:T(8,128)(2,1)S(1)} %get-tuple-element.227), channel_id=1, source_target_pairs={{0,2},{1,3},{2,0},{3,1},{4,6},{5,7},{6,4},{7,5},{8,10},{9,11},{10,... | collective-permute-start | bytes 1769480 | tf_op jit(solution)/shard_map/ppermute | solution.py:406
  107.3 9.5 %collective-permute-start.32 = (bf16[2,128,768]{2,1,0:T(8,128)(2,1)S(1)}, bf16[2,128,768]{2,1,0:T(8,128)(2,1)S(1)}, u32[]{:S(2)}, u32[]{:S(2)}) collective-permute-start(bf16[2,128,768]{2,1,0:T(8,128)(2,1)S(1)} %get-tuple-element.240), channel_id=1, source_target_pairs={{0,8},{1,9},{2,10},{3,11},{4,12},{5,13},{6,14},{7,15},{8,0},{9,1},... | collective-permute-start | bytes 1179656 | tf_op jit(solution)/shard_map/ppermute | solution.py:406
  107.9 7.5 %collective-permute-start.31 = (bf16[96,768]{1,0:T(8,128)(2,1)S(1)}, bf16[96,768]{1,0:T(8,128)(2,1)S(1)}, u32[]{:S(2)}, u32[]{:S(2)}) collective-permute-start(bf16[96,768]{1,0:T(8,128)(2,1)S(1)} %get-tuple-element.238), channel_id=1, source_target_pairs={{0,16},{1,17},{2,18},{3,19},{4,20},{5,21},{6,22},{7,23},{8,24},{9,... | collective-permute-start | bytes 442376 | tf_op jit(solution)/shard_map/ppermute | solution.py:406
  117.4 10.8 %collective-permute-start.35 = (bf16[128,768]{1,0:T(8,128)(2,1)S(1)}, bf16[128,768]{1,0:T(8,128)(2,1)S(1)}, u32[]{:S(2)}, u32[]{:S(2)}) collective-permute-start(bf16[128,768]{1,0:T(8,128)(2,1)S(1)} %get-tuple-element.250), channel_id=1, source_target_pairs={{0,16},{1,17},{2,18},{3,19},{4,20},{5,21},{6,22},{7,23},{8,24},{9,... | collective-permute-start | bytes 589832 | tf_op jit(solution)/shard_map/ppermute | solution.py:406
  120.9 5.7 %collective-permute-start.37 = (bf16[96,768]{1,0:T(8,128)(2,1)S(1)}, bf16[96,768]{1,0:T(8,128)(2,1)S(1)}, u32[]{:S(2)}, u32[]{:S(2)}) collective-permute-start(bf16[96,768]{1,0:T(8,128)(2,1)S(1)} %get-tuple-element.257.refs_1_), channel_id=1, source_target_pairs={{0,2},{1,3},{2,0},{3,1},{4,6},{5,7},{6,4},{7,5},{8,10},{9,11},{10,... | collective-permute-start | bytes 442376 | tf_op jit(solution)/shard_map/ppermute | solution.py:406
  122.3 7.9 %collective-permute-start.34 = (bf16[4,48,768]{2,1,0:T(8,128)(2,1)S(1)}, bf16[4,48,768]{2,1,0:T(8,128)(2,1)S(1)}, u32[]{:S(2)}, u32[]{:S(2)}) collective-permute-start(bf16[4,48,768]{2,1,0:T(8,128)(2,1)S(1)} %get-tuple-element.245), channel_id=1, source_target_pairs={{0,4},{1,5},{2,6},{3,7},{4,0},{5,1},{6,2},{7,3},{8,12},{9,13},{10,... | collective-permute-start | bytes 884744 | tf_op jit(solution)/shard_map/ppermute | solution.py:406
  123.4 6.8 %collective-permute-start.33 = (bf16[4,32,768]{2,1,0:T(8,128)(2,1)S(1)}, bf16[4,32,768]{2,1,0:T(8,128)(2,1)S(1)}, u32[]{:S(2)}, u32[]{:S(2)}) collective-permute-start(bf16[4,32,768]{2,1,0:T(8,128)(2,1)S(1)} %get-tuple-element.244), channel_id=1, source_target_pairs={{0,2},{1,3},{2,0},{3,1},{4,6},{5,7},{6,4},{7,5},{8,10},{9,11},{10,... | collective-permute-start | bytes 589832 | tf_op jit(solution)/shard_map/ppermute | solution.py:406
  126.6 3.6 %collective-permute-start.38 = (bf16[96,768]{1,0:T(8,128)(2,1)S(1)}, bf16[96,768]{1,0:T(8,128)(2,1)S(1)}, u32[]{:S(2)}, u32[]{:S(2)}) collective-permute-start(bf16[96,768]{1,0:T(8,128)(2,1)S(1)} %collective-permute-done.37.refs_7_.refs_3_), channel_id=1, source_target_pairs={{0,1},{1,0},{2,3},{3,2},{4,5},{5,4},{6,7},{7,6},{8,9},{9,8},{10,11... | collective-permute-start | bytes 442376 | tf_op jit(solution)/shard_map/ppermute | solution.py:406
  128.2 2.0 %collective-permute-start.36 = (bf16[96,768]{1,0:T(8,128)(2,1)S(1)}, bf16[96,768]{1,0:T(8,128)(2,1)S(1)}, u32[]{:S(2)}, u32[]{:S(2)}) collective-permute-start(bf16[96,768]{1,0:T(8,128)(2,1)S(1)} %get-tuple-element.257.refs_1_), channel_id=1, source_target_pairs={{0,1},{1,0},{2,3},{3,2},{4,5},{5,4},{6,7},{7,6},{8,9},{9,8},{10,11... | collective-permute-start | bytes 442376 | tf_op jit(solution)/shard_map/ppermute | solution.py:406
  129.5 19.3 %collective-permute-start.48 = (bf16[128,768]{1,0:T(8,128)(2,1)S(1)}, bf16[128,768]{1,0:T(8,128)(2,1)S(1)}, u32[]{:S(2)}, u32[]{:S(2)}) collective-permute-start(bf16[128,768]{1,0:T(8,128)(2,1)S(1)} %get-tuple-element.268.refs_5_), channel_id=1, source_target_pairs={{0,2},{1,3},{2,0},{3,1},{4,6},{5,7},{6,4},{7,5},{8,10},{9,11},{10,... | collective-permute-start | bytes 589832 | tf_op jit(solution)/shard_map/ppermute | solution.py:406
  130.9 6.9 %collective-permute-start.39 = (bf16[80,768]{1,0:T(8,128)(2,1)S(1)}, bf16[80,768]{1,0:T(8,128)(2,1)S(1)}, u32[]{:S(2)}, u32[]{:S(2)}) collective-permute-start(bf16[80,768]{1,0:T(8,128)(2,1)S(1)} %get-tuple-element.259), channel_id=1, source_target_pairs={{0,8},{1,9},{2,10},{3,11},{4,12},{5,13},{6,14},{7,15},{8,0},{9,1},... | collective-permute-start | bytes 368648 | tf_op jit(solution)/shard_map/ppermute | solution.py:406
  132.9 14.3 %collective-permute-start.40 = (bf16[80,768]{1,0:T(8,128)(2,1)S(1)}, bf16[80,768]{1,0:T(8,128)(2,1)S(1)}, u32[]{:S(2)}, u32[]{:S(2)}) collective-permute-start(bf16[80,768]{1,0:T(8,128)(2,1)S(1)} %get-tuple-element.260), channel_id=1, source_target_pairs={{0,16},{1,17},{2,18},{3,19},{4,20},{5,21},{6,22},{7,23},{8,24},{9,... | collective-permute-start | bytes 368648 | tf_op jit(solution)/shard_map/ppermute | solution.py:406
  134.6 12.6 %collective-permute-start.41 = (bf16[80,768]{1,0:T(8,128)(2,1)S(1)}, bf16[80,768]{1,0:T(8,128)(2,1)S(1)}, u32[]{:S(2)}, u32[]{:S(2)}) collective-permute-start(bf16[80,768]{1,0:T(8,128)(2,1)S(1)} %get-tuple-element.261), channel_id=1, source_target_pairs={{0,24},{1,25},{2,26},{3,27},{4,28},{5,29},{6,30},{7,31},{8,16},{9,... | collective-permute-start | bytes 368648 | tf_op jit(solution)/shard_map/ppermute | solution.py:406
  135.3 15.8 %collective-permute-start.43 = (bf16[128,768]{1,0:T(8,128)(2,1)S(1)}, bf16[128,768]{1,0:T(8,128)(2,1)S(1)}, u32[]{:S(2)}, u32[]{:S(2)}) collective-permute-start(bf16[128,768]{1,0:T(8,128)(2,1)S(1)} %get-tuple-element.264), channel_id=1, source_target_pairs={{0,0},{1,16},{2,2},{3,18},{4,4},{5,20},{6,6},{7,22},{8,8},{9,24},{... | collective-permute-start | bytes 589832 | tf_op jit(solution)/shard_map/ppermute | solution.py:406
  147.8 4.9 %collective-permute-start.42 = (bf16[80,768]{1,0:T(8,128)(2,1)S(1)}, bf16[80,768]{1,0:T(8,128)(2,1)S(1)}, u32[]{:S(2)}, u32[]{:S(2)}) collective-permute-start(bf16[80,768]{1,0:T(8,128)(2,1)S(1)} %get-tuple-element.263.refs_1_), channel_id=1, source_target_pairs={{0,2},{1,3},{2,0},{3,1},{4,6},{5,7},{6,4},{7,5},{8,10},{9,11},{10,... | collective-permute-start | bytes 368648 | tf_op jit(solution)/shard_map/ppermute | solution.py:406
  148.8 3.9 %collective-permute-start.47 = (bf16[128,768]{1,0:T(8,128)(2,1)S(1)}, bf16[128,768]{1,0:T(8,128)(2,1)S(1)}, u32[]{:S(2)}, u32[]{:S(2)}) collective-permute-start(bf16[128,768]{1,0:T(8,128)(2,1)S(1)} %get-tuple-element.268.refs_5_), channel_id=1, source_target_pairs={{0,1},{1,0},{2,3},{3,2},{4,5},{5,4},{6,7},{7,6},{8,9},{9,8},{10,11... | collective-permute-start | bytes 589832 | tf_op jit(solution)/shard_map/ppermute | solution.py:406
  148.8 3.9 %collective-permute-start.49 = (bf16[128,768]{1,0:T(8,128)(2,1)S(1)}, bf16[128,768]{1,0:T(8,128)(2,1)S(1)}, u32[]{:S(2)}, u32[]{:S(2)}) collective-permute-start(bf16[128,768]{1,0:T(8,128)(2,1)S(1)} %collective-permute-done.48.refs_7_), channel_id=1, source_target_pairs={{0,1},{1,0},{2,3},{3,2},{4,5},{5,4},{6,7},{7,6},{8,9},{9,8},{10,11... | collective-permute-start | bytes 589832 | tf_op jit(solution)/shard_map/ppermute | solution.py:406
  149.3 7.8 %collective-permute-start.44 = (bf16[128,768]{1,0:T(8,128)(2,1)S(1)}, bf16[128,768]{1,0:T(8,128)(2,1)S(1)}, u32[]{:S(2)}, u32[]{:S(2)}) collective-permute-start(bf16[128,768]{1,0:T(8,128)(2,1)S(1)} %get-tuple-element.266), channel_id=1, source_target_pairs={{0,8},{1,24},{2,10},{3,26},{4,12},{5,28},{6,14},{7,30},{8,0},{9,16... | collective-permute-start | bytes 589832 | tf_op jit(solution)/shard_map/ppermute | solution.py:406
  151.2 4.4 %collective-permute-start.45 = (bf16[80,768]{1,0:T(8,128)(2,1)S(1)}, bf16[80,768]{1,0:T(8,128)(2,1)S(1)}, u32[]{:S(2)}, u32[]{:S(2)}) collective-permute-start(bf16[80,768]{1,0:T(8,128)(2,1)S(1)} %get-tuple-element.263.refs_1_), channel_id=1, source_target_pairs={{0,1},{1,0},{2,3},{3,2},{4,5},{5,4},{6,7},{7,6},{8,9},{9,8},{10,11... | collective-permute-start | bytes 368648 | tf_op jit(solution)/shard_map/ppermute | solution.py:406
  152.7 2.9 %collective-permute-start.46 = (bf16[80,768]{1,0:T(8,128)(2,1)S(1)}, bf16[80,768]{1,0:T(8,128)(2,1)S(1)}, u32[]{:S(2)}, u32[]{:S(2)}) collective-permute-start(bf16[80,768]{1,0:T(8,128)(2,1)S(1)} %collective-permute-done.42.refs_3_), channel_id=1, source_target_pairs={{0,1},{1,0},{2,3},{3,2},{4,5},{5,4},{6,7},{7,6},{8,9},{9,8},{10,11... | collective-permute-start | bytes 368648 | tf_op jit(solution)/shard_map/ppermute | solution.py:406
  (15 other events, 115.9 us)

commit v2 on v1

--- a/solution.py
+++ b/solution.py
@@ -1253,7 +1253,7 @@
     shift1[...] = tail[1:2, 0:96]
     out_bias[...] = tail[2:3, 0:96]
     wide = tails[pl.ds(4 + seq // 2, 1), :]
-    up_bias[...] = jnp.where(seq % 2 == 0, wide[:, 0:HALF], wide[:, HALF:])
+    up_bias[...] = jnp.where(seq % 2 == 0, wide[:, 0:HALF], wide[:, HALF:]).reshape(HALF)
 
 
 def dense_outputs(place, units, after=()):
@@ -1264,7 +1264,7 @@
         [plain(unit) for unit in units],
         [made((4 * DOWN_ROWS, WIDTH), FLOAT), made((96, FF), FLOAT), made((96, WIDTH), FLOAT)]
         + [made((1, 96), FLOAT)] * 6
-        + [made((1, HALF), FLOAT)],
+        + [made((HALF,), FLOAT)],
         scratch=[pltpu.VMEM((8, WIDTH), FLOAT)] * 2,
         after=after,
         work=cost(1e6, 3e6),
@@ -1414,7 +1414,7 @@
     (keep, one, two, three), mark = joint_line_stage(
         place, (joint_x_got, joint_y_got, joint_p, joint_q), (mark, *down_all[1:])
     )
-    joint_last = (keep, z_swap(one, 1), z_swap(two, 2), z_swap(three, 3))
+    joint_last = (keep, z_swap(two, 2), z_swap(three, 3), z_swap(one, 1))
     joint_unit, mark = joint_sum(place, joint_last, (mark,))
     joint_across = x_swap(joint_unit)
     joint_across, first_back = lax.optimization_barrier((joint_across, back[0]))

time: 159 us -> 158 us (level)
  waiting for transfers between devices: 47.6 us -> 43.9 us
  starting transfers between devices: 46.9 us -> 49.9 us
    ppermute x50, waiting for transfers between devices: 47.6 us -> 43.9 us  [permute(): return lax.ppermute(value, AXES, pairs)]
    ppermute x50, starting transfers between devices: 46.9 us -> 49.9 us  [permute(): return lax.ppermute(value, AXES, pairs)]
where the time goes in v2:
time: 158 us; the launch traced here: 157 us
  Pallas kernels  57.8 us (37%)
  starting transfers between devices  49.9 us (32%)
  waiting for transfers between devices  43.9 us (28%)
  local copies, waits for them, and re-layouts  4.62 us (3%)
    pallas_call x23, Pallas kernels, call(): pl.pallas_call(ordered, grid_spec=pltpu.PrefetchScalarGridSpec(num_scalar...  57.8 us
    ppermute x50, starting transfers between devices, permute(): return lax.ppermute(value, AXES, pairs)  49.9 us
    ppermute x50, waiting for transfers between devices, permute(): return lax.ppermute(value, AXES, pairs)  43.9 us
  transfers between devices with their start and end apart: 50, of which 22 were waited for; matrix products, arithmetic and copies ran while one was open for 1% of the time, Pallas kernels for 30%

profile of v2, /device:TPU:0, one launch (start us, length us, event | category | flops | bytes accessed | tf_op | source)
XLA Modules:
  0.0 157.5 jit_solution(11993772961884548771)
XLA Ops:
  1.8 3.1 %collective-permute-start.1 = (bf16[128,768]{1,0:T(8,128)(2,1)S(1)}, bf16[128,768]{1,0:T(8,128)(2,1)S(1)}, u32[]{:S(2)}, u32[]{:S(2)}) collective-permute-start(bf16[128,768]{1,0:T(8,128)(2,1)S(1)} %get-tuple-element.289), channel_id=1, source_target_pairs={{0,8},{1,24},{2,10},{3,26},{4,12},{5,28},{6,14},{7,30},{8,0},{9,16... | collective-permute-start | bytes 589832 | tf_op jit(solution)/shard_map/ppermute | solution.py:406
  5.6 3.5 %collective-permute-start.2 = (s32[2,16]{1,0:T(2,128)}, s32[2,16]{1,0:T(2,128)S(1)}, u32[]{:S(2)}, u32[]{:S(2)}) collective-permute-start(s32[2,16]{1,0:T(2,128)} %refs_1_.4), channel_id=1, source_target_pairs={{0,1},{1,0},{2,3},{3,2},{4,5},{5,4},{6,7},{7,6},{8,9},{9,8},{10,11... | collective-permute-start | bytes 392 | tf_op jit(solution)/shard_map/ppermute | solution.py:406
  10.5 2.0 %copy-done.3 = bf16[768,2304]{1,0:T(8,128)(2,1)S(1)} copy-done((bf16[768,2304]{1,0:T(8,128)(2,1)S(1)}, bf16[768,2304]{1,0:T(8,128)(2,1)}, u32[]{:S(2)}) %copy-start.3) | copy-done | bytes 3538968
  12.5 1.5 own_columns.1
  14.0 2.0 %collective-permute-start.5 = (bf16[128,768]{1,0:T(8,128)(2,1)S(1)}, bf16[128,768]{1,0:T(8,128)(2,1)S(1)}, u32[]{:S(2)}, u32[]{:S(2)}) collective-permute-start(bf16[128,768]{1,0:T(8,128)(2,1)S(1)} %collective-permute-done.refs_3_.refs_6_.refs_1_), channel_id=1, source_target_pairs={{0,1},{1,0},{2,3},{3,2},{4,5},{5,4},{6,7},{7,6},{8,9},{9,8},{10,11... | collective-permute-start | bytes 589832 | tf_op jit(solution)/shard_map/ppermute | solution.py:406
  16.0 1.5 collective-permute-start.3
  18.9 5.0 %first_attention.1 = (bf16[512,384]{1,0:T(8,128)(2,1)S(1)}, bf16[512,384]{1,0:T(8,128)(2,1)S(1)}, bf16[512,384]{1,0:T(8,128)(2,1)S(1)}, f32[3,128,1024]{2,1,0:T(...) custom-call(s32[4]{0:T(128)S(1)} %pad_add_fusion.refs_0_, s32[2,16]{1,0:T(2,128)S(1)} %copy-done.5, ...), custom_call_target="tpu_custom_call" | custom-call | flops 1024 | bytes 1024 | tf_op jit(solution)/shard_map/first_attention/pallas_call | solution.py:369
  23.9 3.6 %collective-permute-done.4.refs_4_.refs_6_ = bf16[128,768]{1,0:T(8,128)(2,1)S(1)} collective-permute-done((bf16[128,768]{1,0:T(8,128)(2,1)S(1)}, bf16[128,768]{1,0:T(8,128)(2,1)S(1)}, u32[]{:S(2)}, u32[]{:S(2)}) %collective-permute-start.4) | collective-permute-done | bytes 196640 | tf_op jit(solution)/shard_map/ppermute | solution.py:406
  29.9 5.0 %attention.1 = (bf16[512,384]{1,0:T(8,128)(2,1)S(1)}, bf16[512,384]{1,0:T(8,128)(2,1)S(1)}, bf16[512,384]{1,0:T(8,128)(2,1)S(1)}, f32[8,512]{1,0:T(8,128)S(1)}, f32[8,128]{1,0:T(8,128)S(1)}) custom-call(s32[4]{0:T(128)S(1)} %pad_add_fusion.refs_0_, s32[2,16]{1,0:T(2,128)S(1)} %copy-done.5, s32[2,16]{1,0:T(2,128)S(1)} %collective-permute-done.2.refs_2_, ...), custom_call_target="tpu_custom_call" | custom-call | flops 1024 | bytes 1024 | tf_op jit(solution)/shard_map/attention/pallas_call | solution.py:369
  35.4 1.3 collective-permute-done.11.refs_2_
  36.7 6.4 %forward.1 = (bf16[128,768]{1,0:T(8,128)(2,1)S(1)}, bf16[128,768]{1,0:T(8,128)(2,1)S(1)}, bf16[272,768]{1,0:T(8,128)(2,1)S(1)}, f32[256,768]{1,0:T(8,128)S(1)}, ...) custom-call(s32[4]{0:T(128)S(1)} %pad_add_fusion.refs_0_, ...), custom_call_target="tpu_custom_call" | custom-call | flops 1024 | bytes 1024 | tf_op jit(solution)/shard_map/forward/pallas_call | solution.py:369
  44.0 2.1 %collective-permute-done.15.refs_4_.refs_12_ = bf16[272,768]{1,0:T(8,128)(2,1)S(1)} collective-permute-done((bf16[272,768]{1,0:T(8,128)(2,1)S(1)}, bf16[272,768]{1,0:T(8,128)(2,1)S(1)}, u32[]{:S(2)}, u32[]{:S(2)}) %collective-permute-start.15) | collective-permute-done | bytes 417824 | tf_op jit(solution)/shard_map/ppermute | solution.py:406
  46.0 2.6 %down_units.1 = (bf16[4,2,48,768]{3,2,1,0:T(8,128)(2,1)S(1)}, bf16[4,2,48,768]{3,2,1,0:T(8,128)(2,1)S(1)}, bf16[4,2,48,768]{3,2,1,0:T(8,128)(2,1)S(1)}, bf16[4,2,48,768]{3,2,1,0:T(8,128)(2,1)S(1)}, f32[8,128]{1,0:T(8,128)S(1)}) custom-call(s32[4]{0:T(128)S(1)} %pad_add_fusion.refs_0_, bf16[16,96,256]{2,1,0:T(8,128)(2,1)S(1)} %get-tuple-element.183.refs_1_, ...), custom_call_target="tpu_custom_call" | custom-call | flops 1024 | bytes 1024 | tf_op jit(solution)/shard_map/down_units/pallas_call | solution.py:369
  48.7 1.6 collective-permute-start.18
  50.3 1.5 collective-permute-start.19
  51.8 5.0 %backward.1 = (bf16[256,768]{1,0:T(8,128)(2,1)S(1)}, bf16[256,768]{1,0:T(8,128)(2,1)S(1)}, bf16[256,768]{1,0:T(8,128)(2,1)S(1)}, bf16[256,768]{1,0:T(8,128)(2,1)...) custom-call(s32[4]{0:T(128)S(1)} %pad_add_fusion.refs_0_, ...), custom_call_target="tpu_custom_call" | custom-call | flops 1024 | bytes 1024 | tf_op jit(solution)/shard_map/backward/pallas_call | solution.py:369
  57.5 1.7 %collective-permute-done.20.refs_5_ = bf16[256,768]{1,0:T(8,128)(2,1)S(1)} collective-permute-done((bf16[256,768]{1,0:T(8,128)(2,1)S(1)}, bf16[256,768]{1,0:T(8,128)(2,1)S(1)}, u32[]{:S(2)}, u32[]{:S(2)}) %collective-permute-start.20) | collective-permute-done | bytes 393248 | tf_op jit(solution)/shard_map/ppermute | solution.py:406
  59.8 3.3 %up_units.1 = (bf16[704,768]{1,0:T(8,128)(2,1)S(1)}, bf16[704,768]{1,0:T(8,128)(2,1)S(1)}, bf16[4,2,64,768]{3,2,1,0:T(8,128)(2,1)S(1)}, bf16[4,2,64,768]{3,2,1,0:T(8,128)(2,1)S(1)}, f32[8,128]{1,0:T(8,128)S(1)}) custom-call(s32[4]{0:T(128)S(1)} %pad_add_fusion.refs_0_, bf16[768,256]{1,0:T(8,128)(2,1)S(1)} %get-tuple-element.194.refs_1_, ...), custom_call_target="tpu_custom_call" | custom-call | flops 1024 | bytes 1024 | tf_op jit(solution)/shard_map/up_units/pallas_call | solution.py:369
  63.1 1.2 collective-permute-done.18.refs_2_
  64.3 1.2 collective-permute-done.19.refs_4_
  65.5 1.1 down_pair_stage.1
  67.2 1.5 collective-permute-start.24
  70.0 10.1 %attention_back.1 = (bf16[512,384]{1,0:T(8,128)(2,1)S(1)}, bf16[1024,384]{1,0:T(8,128)(2,1)S(1)}, bf16[1024,384]{1,0:T(8,128)(2,1)S(1)}, f32[8,128]{1,0:T(8,128)S(1)}) custom-call(s32[4]{0:T(128)S(1)} %pad_add_fusion.refs_0_, s32[2,16]{1,0:T(2,128)S(1)} %copy-done.5, s32[2,16]{1,0:T(2,128)S(1)} %collective-permute-done.2.refs_2_, ...), custom_call_target="tpu_custom_call" | custom-call | flops 1024 | bytes 1024 | tf_op jit(solution)/shard_map/attention_back/pallas_call | solution.py:369
  80.2 2.8 %token_parts.1 = (bf16[256,768]{1,0:T(8,128)(2,1)S(1)}, bf16[256,768]{1,0:T(8,128)(2,1)S(1)}, bf16[256,768]{1,0:T(8,128)(2,1)S(1)}, bf16[256,768]{1,0:T(8,128)(2,1)S(1)}, f32[8,128]{1,0:T(8,128)S(1)}) custom-call(s32[4]{0:T(128)S(1)} %pad_add_fusion.refs_0_, bf16[512,384]{1,0:T(8,128)(2,1)S(1)} %get-tuple-element.208.refs_1_.refs_9_, ...), custom_call_target="tpu_custom_call" | custom-call | flops 1024 | bytes 1024 | tf_op jit(solution)/shard_map/token_parts/pallas_call | solution.py:369
  82.9 2.8 %collective-permute-start.22 = (bf16[256,768]{1,0:T(8,128)(2,1)S(1)}, bf16[256,768]{1,0:T(8,128)(2,1)S(1)}, u32[]{:S(2)}, u32[]{:S(2)}) collective-permute-start(bf16[256,768]{1,0:T(8,128)(2,1)S(1)} %get-tuple-element.213), channel_id=1, source_target_pairs={{0,1},{1,0},{2,3},{3,2},{4,5},{5,4},{6,7},{7,6},{8,9},{9,8},{10,11... | collective-permute-start | bytes 1179656 | tf_op jit(solution)/shard_map/ppermute | solution.py:406
  85.8 1.3 collective-permute-done.22.refs_13_
  87.1 3.2 %joint_units.1 = (bf16[4,2,48,768]{3,2,1,0:T(8,128)(2,1)S(1)}, bf16[4,2,48,768]{3,2,1,0:T(8,128)(2,1)S(1)}, bf16[512,768]{1,0:T(8,128)(2,1)S(1)}, bf16[4,2,32,768]{3,2,1,0:T(8,128)(2,1)S(1)}, f32[8,128]{1,0:T(8,128)S(1)}) custom-call(s32[4]{0:T(128)S(1)} %pad_add_fusion.refs_0_, bf16[128,768]{1,0:T(8,128)(2,1)S(1)} %collective-permute-done.refs_3_.refs_6_.refs_1_, ...), custom_call_target="tpu_custom_call" | custom-call | flops 1024 | bytes 1024 | tf_op jit(solution)/shard_map/joint_units/pallas_call | solution.py:369
  90.3 1.3 collective-permute-done.23.refs_1_
  92.9 1.5 collective-permute-start.28
  94.4 1.5 collective-permute-start.29
  97.7 5.7 %collective-permute-done.30.refs_6_ = bf16[2,96,768]{2,1,0:T(8,128)(2,1)S(1)} collective-permute-done((bf16[2,96,768]{2,1,0:T(8,128)(2,1)S(1)}, bf16[2,96,768]{2,1,0:T(8,128)(2,1)S(1)}, u32[]{:S(2)}, u32[]{:S(2)}) %collective-permute-start.30) | collective-permute-done | bytes 294944 | tf_op jit(solution)/shard_map/ppermute | solution.py:406
  103.4 1.6 %collective-permute-done.28.refs_1_ = bf16[256,768]{1,0:T(8,128)(2,1)S(1)} collective-permute-done((bf16[256,768]{1,0:T(8,128)(2,1)S(1)}, bf16[256,768]{1,0:T(8,128)(2,1)S(1)}, u32[]{:S(2)}, u32[]{:S(2)}) %collective-permute-start.28) | collective-permute-done | bytes 393248 | tf_op jit(solution)/shard_map/ppermute | solution.py:406
  105.0 1.4 collective-permute-done.29.refs_2_
  108.0 2.1 %collective-permute-start.31 = (bf16[96,768]{1,0:T(8,128)(2,1)S(1)}, bf16[96,768]{1,0:T(8,128)(2,1)S(1)}, u32[]{:S(2)}, u32[]{:S(2)}) collective-permute-start(bf16[96,768]{1,0:T(8,128)(2,1)S(1)} %get-tuple-element.238), channel_id=1, source_target_pairs={{0,16},{1,17},{2,18},{3,19},{4,20},{5,21},{6,22},{7,23},{8,24},{9,... | collective-permute-start | bytes 442376 | tf_op jit(solution)/shard_map/ppermute | solution.py:406
  110.1 5.4 %collective-permute-done.31.refs_4_.refs_2_ = bf16[96,768]{1,0:T(8,128)(2,1)S(1)} collective-permute-done((bf16[96,768]{1,0:T(8,128)(2,1)S(1)}, bf16[96,768]{1,0:T(8,128)(2,1)S(1)}, u32[]{:S(2)}, u32[]{:S(2)}) %collective-permute-start.31) | collective-permute-done | bytes 147488 | tf_op jit(solution)/shard_map/ppermute | solution.py:406
  115.5 1.3 collective-permute-done.32.refs_2_
  117.4 2.9 %collective-permute-start.35 = (bf16[128,768]{1,0:T(8,128)(2,1)S(1)}, bf16[128,768]{1,0:T(8,128)(2,1)S(1)}, u32[]{:S(2)}, u32[]{:S(2)}) collective-permute-start(bf16[128,768]{1,0:T(8,128)(2,1)S(1)} %get-tuple-element.250), channel_id=1, source_target_pairs={{0,16},{1,17},{2,18},{3,19},{4,20},{5,21},{6,22},{7,23},{8,24},{9,... | collective-permute-start | bytes 589832 | tf_op jit(solution)/shard_map/ppermute | solution.py:406
  123.4 1.4 collective-permute-start.33
  124.8 1.8 %collective-permute-done.37.refs_7_.refs_3_ = bf16[96,768]{1,0:T(8,128)(2,1)S(1)} collective-permute-done((bf16[96,768]{1,0:T(8,128)(2,1)S(1)}, bf16[96,768]{1,0:T(8,128)(2,1)S(1)}, u32[]{:S(2)}, u32[]{:S(2)}) %collective-permute-start.37) | collective-permute-done | bytes 147488 | tf_op jit(solution)/shard_map/ppermute | solution.py:406
  126.6 1.6 collective-permute-done.35.refs_2_
  130.9 1.2 collective-permute-start.39
  132.1 3.1 %collective-permute-start.40 = (bf16[80,768]{1,0:T(8,128)(2,1)S(1)}, bf16[80,768]{1,0:T(8,128)(2,1)S(1)}, u32[]{:S(2)}, u32[]{:S(2)}) collective-permute-start(bf16[80,768]{1,0:T(8,128)(2,1)S(1)} %get-tuple-element.260), channel_id=1, source_target_pairs={{0,24},{1,25},{2,26},{3,27},{4,28},{5,29},{6,30},{7,31},{8,16},{9,... | collective-permute-start | bytes 368648 | tf_op jit(solution)/shard_map/ppermute | solution.py:406
  135.9 7.4 %collective-permute-done.39.refs_2_ = bf16[80,768]{1,0:T(8,128)(2,1)S(1)} collective-permute-done((bf16[80,768]{1,0:T(8,128)(2,1)S(1)}, bf16[80,768]{1,0:T(8,128)(2,1)S(1)}, u32[]{:S(2)}, u32[]{:S(2)}) %collective-permute-start.39) | collective-permute-done | bytes 122912 | tf_op jit(solution)/shard_map/ppermute | solution.py:406
  144.6 1.6 collective-permute-start.42
  146.6 3.9 %collective-permute-start.44 = (bf16[128,768]{1,0:T(8,128)(2,1)S(1)}, bf16[128,768]{1,0:T(8,128)(2,1)S(1)}, u32[]{:S(2)}, u32[]{:S(2)}) collective-permute-start(bf16[128,768]{1,0:T(8,128)(2,1)S(1)} %get-tuple-element.266), channel_id=1, source_target_pairs={{0,8},{1,24},{2,10},{3,26},{4,12},{5,28},{6,14},{7,30},{8,0},{9,16... | collective-permute-start | bytes 589832 | tf_op jit(solution)/shard_map/ppermute | solution.py:406
  151.1 2.2 %dense_outputs.1 = (f32[384,768]{1,0:T(8,128)}, f32[96,3072]{1,0:T(8,128)}, f32[96,768]{1,0:T(8,128)}, f32[1,96]{1,0:T(1,128)}, f32[1,96]{1,0:T(1,128)}, /*index...) custom-call(s32[4]{0:T(128)S(1)} %pad_add_fusion.refs_0_, ...), custom_call_target="tpu_custom_call" | custom-call | flops 1024 | bytes 1024 | tf_op jit(solution)/shard_map/dense_outputs/pallas_call | solution.py:369
  153.4 1.5 joint_outputs.1
  155.8 1.6 %back_rows.1 = (bf16[2,128,768]{2,1,0:T(8,128)(2,1)}, f32[2,128,768]{2,1,0:T(8,128)}, f32[8,128]{1,0:T(8,128)}) custom-call(s32[4]{0:T(128)S(1)} %pad_add_fusion.refs_0_, bf16[128,768]{1,0:T(8,128)(2,1)S(1)} %collective-permute-done.12.refs_6_.refs_1_, bf16[128,768]{1,0:T(8,128)(2,1)S(1)} %collective-permute-done.13.refs_7_.refs_2_, ...), custom_call_target="tpu_custom_call" | custom-call | flops 1024 | bytes 1024 | tf_op jit(solution)/shard_map/back_rows/pallas_call | solution.py:369
  (114 shorter events, 26.2 us)
Async XLA Ops:
  1.8 12.2 %collective-permute-start.1 = (bf16[128,768]{1,0:T(8,128)(2,1)S(1)}, bf16[128,768]{1,0:T(8,128)(2,1)S(1)}, u32[]{:S(2)}, u32[]{:S(2)}) collective-permute-start(bf16[128,768]{1,0:T(8,128)(2,1)S(1)} %get-tuple-element.289), channel_id=1, source_target_pairs={{0,8},{1,24},{2,10},{3,26},{4,12},{5,28},{6,14},{7,30},{8,0},{9,16... | collective-permute-start | bytes 589832 | tf_op jit(solution)/shard_map/ppermute | solution.py:406
  4.9 9.1 %collective-permute-start = (bf16[128,768]{1,0:T(8,128)(2,1)S(1)}, bf16[128,768]{1,0:T(8,128)(2,1)S(1)}, u32[]{:S(2)}, u32[]{:S(2)}) collective-permute-start(bf16[128,768]{1,0:T(8,128)(2,1)S(1)} %get-tuple-element.290), channel_id=1, source_target_pairs={{0,0},{1,16},{2,2},{3,18},{4,4},{5,20},{6,6},{7,22},{8,8},{9,24},{... | collective-permute-start | bytes 589832 | tf_op jit(solution)/shard_map/ppermute | solution.py:406
  5.6 8.4 %collective-permute-start.2 = (s32[2,16]{1,0:T(2,128)}, s32[2,16]{1,0:T(2,128)S(1)}, u32[]{:S(2)}, u32[]{:S(2)}) collective-permute-start(s32[2,16]{1,0:T(2,128)} %refs_1_.4), channel_id=1, source_target_pairs={{0,1},{1,0},{2,3},{3,2},{4,5},{5,4},{6,7},{7,6},{8,9},{9,8},{10,11... | collective-permute-start | bytes 392 | tf_op jit(solution)/shard_map/ppermute | solution.py:406
  14.0 4.8 %collective-permute-start.5 = (bf16[128,768]{1,0:T(8,128)(2,1)S(1)}, bf16[128,768]{1,0:T(8,128)(2,1)S(1)}, u32[]{:S(2)}, u32[]{:S(2)}) collective-permute-start(bf16[128,768]{1,0:T(8,128)(2,1)S(1)} %collective-permute-done.refs_3_.refs_6_.refs_1_), channel_id=1, source_target_pairs={{0,1},{1,0},{2,3},{3,2},{4,5},{5,4},{6,7},{7,6},{8,9},{9,8},{10,11... | collective-permute-start | bytes 589832 | tf_op jit(solution)/shard_map/ppermute | solution.py:406
  16.0 2.9 %collective-permute-start.6 = (bf16[128,768]{1,0:T(8,128)(2,1)S(1)}, bf16[128,768]{1,0:T(8,128)(2,1)S(1)}, u32[]{:S(2)}, u32[]{:S(2)}) collective-permute-start(bf16[128,768]{1,0:T(8,128)(2,1)S(1)} %collective-permute-done.1.refs_4_.refs_7_.refs_2_), channel_id=1, source_target_pairs={{0,1},{1,0},{2,3},{3,2},{4,5},{5,4},{6,7},{7,6},{8,9},{9,8},{10,11... | collective-permute-start | bytes 589832 | tf_op jit(solution)/shard_map/ppermute | solution.py:406
  16.0 7.9 %collective-permute-start.3 = (bf16[128,768]{1,0:T(8,128)(2,1)S(1)}, bf16[128,768]{1,0:T(8,128)(2,1)S(1)}, u32[]{:S(2)}, u32[]{:S(2)}) collective-permute-start(bf16[128,768]{1,0:T(8,128)(2,1)S(1)} %collective-permute-done.refs_3_.refs_6_.refs_1_), channel_id=1, source_target_pairs={{0,4},{1,5},{2,6},{3,7},{4,0},{5,1},{6,2},{7,3},{8,12},{9,13},{10,... | collective-permute-start | bytes 589832 | tf_op jit(solution)/shard_map/ppermute | solution.py:406
  17.5 10.0 %collective-permute-start.4 = (bf16[128,768]{1,0:T(8,128)(2,1)S(1)}, bf16[128,768]{1,0:T(8,128)(2,1)S(1)}, u32[]{:S(2)}, u32[]{:S(2)}) collective-permute-start(bf16[128,768]{1,0:T(8,128)(2,1)S(1)} %collective-permute-done.1.refs_4_.refs_7_.refs_2_), channel_id=1, source_target_pairs={{0,4},{1,5},{2,6},{3,7},{4,0},{5,1},{6,2},{7,3},{8,12},{9,13},{10,... | collective-permute-start | bytes 589832 | tf_op jit(solution)/shard_map/ppermute | solution.py:406
  18.1 16.8 %collective-permute-start.9 = (bf16[144,768]{1,0:T(8,128)(2,1)S(1)}, bf16[144,768]{1,0:T(8,128)(2,1)S(1)}, u32[]{:S(2)}, u32[]{:S(2)}) collective-permute-start(bf16[144,768]{1,0:T(8,128)(2,1)S(1)} %concatenate.6), channel_id=1, source_target_pairs={{0,0},{1,16},{2,2},{3,18},{4,4},{5,20},{6,6},{7,22},{8,8},{9,24},{... | collective-permute-start | bytes 663560 | tf_op jit(solution)/shard_map/ppermute | solution.py:406
  18.8 16.1 %collective-permute-start.10 = (bf16[144,768]{1,0:T(8,128)(2,1)S(1)}, bf16[144,768]{1,0:T(8,128)(2,1)S(1)}, u32[]{:S(2)}, u32[]{:S(2)}) collective-permute-start(bf16[144,768]{1,0:T(8,128)(2,1)S(1)} %concatenate.7), channel_id=1, source_target_pairs={{0,8},{1,24},{2,10},{3,26},{4,12},{5,28},{6,14},{7,30},{8,0},{9,16... | collective-permute-start | bytes 663560 | tf_op jit(solution)/shard_map/ppermute | solution.py:406
  27.5 1.9 %collective-permute-start.7 = (bf16[128,768]{1,0:T(8,128)(2,1)S(1)}, bf16[128,768]{1,0:T(8,128)(2,1)S(1)}, u32[]{:S(2)}, u32[]{:S(2)}) collective-permute-start(bf16[128,768]{1,0:T(8,128)(2,1)S(1)} %collective-permute-done.3.refs_3_.refs_5_), channel_id=1, source_target_pairs={{0,1},{1,0},{2,3},{3,2},{4,5},{5,4},{6,7},{7,6},{8,9},{9,8},{10,11... | collective-permute-start | bytes 589832 | tf_op jit(solution)/shard_map/ppermute | solution.py:406
  43.1 3.0 %collective-permute-start.14 = (bf16[16,96,256]{2,1,0:T(8,128)(2,1)S(1)}, bf16[16,96,256]{2,1,0:T(8,128)(2,1)S(1)}, u32[]{:S(2)}, u32[]{:S(2)}) collective-permute-start(bf16[16,96,256]{2,1,0:T(8,128)(2,1)S(1)} %get-tuple-element.184), channel_id=1, source_target_pairs={{0,1},{1,0},{2,3},{3,2},{4,5},{5,4},{6,7},{7,6},{8,9},{9,8},{10,11... | collective-permute-start | bytes 2359304 | tf_op jit(solution)/shard_map/ppermute | solution.py:406
  43.4 2.6 %collective-permute-start.15 = (bf16[272,768]{1,0:T(8,128)(2,1)S(1)}, bf16[272,768]{1,0:T(8,128)(2,1)S(1)}, u32[]{:S(2)}, u32[]{:S(2)}) collective-permute-start(bf16[272,768]{1,0:T(8,128)(2,1)S(1)} %get-tuple-element.178.refs_3_.refs_1_), channel_id=1, source_target_pairs={{0,1},{1,0},{2,3},{3,2},{4,5},{5,4},{6,7},{7,6},{8,9},{9,8},{10,11... | collective-permute-start | bytes 1253384 | tf_op jit(solution)/shard_map/ppermute | solution.py:406
  43.7 8.1 %collective-permute-start.16 = (bf16[256,768]{1,0:T(8,128)(2,1)S(1)}, bf16[256,768]{1,0:T(8,128)(2,1)S(1)}, u32[]{:S(2)}, u32[]{:S(2)}) collective-permute-start(bf16[256,768]{1,0:T(8,128)(2,1)S(1)} %get-tuple-element.187), channel_id=1, source_target_pairs={{0,1},{1,0},{2,3},{3,2},{4,5},{5,4},{6,7},{7,6},{8,9},{9,8},{10,11... | collective-permute-start | bytes 1179656 | tf_op jit(solution)/shard_map/ppermute | solution.py:406
  48.7 15.6 %collective-permute-start.18 = (bf16[4,2,48,768]{3,2,1,0:T(8,128)(2,1)S(1)}, bf16[4,2,48,768]{3,2,1,0:T(8,128)(2,1)S(1)}, u32[]{:S(2)}, u32[]{:S(2)}) collective-permute-start(bf16[4,2,48,768]{3,2,1,0:T(8,128)(2,1)S(1)} %get-tuple-element.191), channel_id=1, source_target_pairs={{0,2},{1,3},{2,0},{3,1},{4,6},{5,7},{6,4},{7,5},{8,10},{9,11},{10,... | collective-permute-start | bytes 1769480 | tf_op jit(solution)/shard_map/ppermute | solution.py:406
  50.3 15.2 %collective-permute-start.19 = (bf16[4,2,48,768]{3,2,1,0:T(8,128)(2,1)S(1)}, bf16[4,2,48,768]{3,2,1,0:T(8,128)(2,1)S(1)}, u32[]{:S(2)}, u32[]{:S(2)}) collective-permute-start(bf16[4,2,48,768]{3,2,1,0:T(8,128)(2,1)S(1)} %get-tuple-element.193), channel_id=1, source_target_pairs={{0,4},{1,5},{2,6},{3,7},{4,0},{5,1},{6,2},{7,3},{8,12},{9,13},{10,... | collective-permute-start | bytes 1769480 | tf_op jit(solution)/shard_map/ppermute | solution.py:406
  56.8 3.0 %collective-permute-start.17 = (bf16[272,768]{1,0:T(8,128)(2,1)S(1)}, bf16[272,768]{1,0:T(8,128)(2,1)S(1)}, u32[]{:S(2)}, u32[]{:S(2)}) collective-permute-start(bf16[272,768]{1,0:T(8,128)(2,1)S(1)} %get-tuple-element.189), channel_id=1, source_target_pairs={{0,1},{1,0},{2,3},{3,2},{4,5},{5,4},{6,7},{7,6},{8,9},{9,8},{10,11... | collective-permute-start | bytes 1253384 | tf_op jit(solution)/shard_map/ppermute | solution.py:406
  56.9 2.3 %collective-permute-start.20 = (bf16[256,768]{1,0:T(8,128)(2,1)S(1)}, bf16[256,768]{1,0:T(8,128)(2,1)S(1)}, u32[]{:S(2)}, u32[]{:S(2)}) collective-permute-start(bf16[256,768]{1,0:T(8,128)(2,1)S(1)} %get-tuple-element.197), channel_id=1, source_target_pairs={{0,1},{1,0},{2,3},{3,2},{4,5},{5,4},{6,7},{7,6},{8,9},{9,8},{10,11... | collective-permute-start | bytes 1179656 | tf_op jit(solution)/shard_map/ppermute | solution.py:406
  57.4 2.4 %collective-permute-start.21 = (bf16[256,768]{1,0:T(8,128)(2,1)S(1)}, bf16[256,768]{1,0:T(8,128)(2,1)S(1)}, u32[]{:S(2)}, u32[]{:S(2)}) collective-permute-start(bf16[256,768]{1,0:T(8,128)(2,1)S(1)} %get-tuple-element.198), channel_id=1, source_target_pairs={{0,1},{1,0},{2,3},{3,2},{4,5},{5,4},{6,7},{7,6},{8,9},{9,8},{10,11... | collective-permute-start | bytes 1179656 | tf_op jit(solution)/shard_map/ppermute | solution.py:406
  66.6 25.0 %collective-permute-start.23 = (bf16[704,768]{1,0:T(8,128)(2,1)S(1)}, bf16[704,768]{1,0:T(8,128)(2,1)S(1)}, u32[]{:S(2)}, u32[]{:S(2)}) collective-permute-start(bf16[704,768]{1,0:T(8,128)(2,1)S(1)} %get-tuple-element.218), channel_id=1, source_target_pairs={{0,2},{1,3},{2,0},{3,1},{4,6},{5,7},{6,4},{7,5},{8,10},{9,11},{10,... | collective-permute-start | bytes 3244040 | tf_op jit(solution)/shard_map/ppermute | solution.py:406
  67.2 24.7 %collective-permute-start.24 = (bf16[704,768]{1,0:T(8,128)(2,1)S(1)}, bf16[704,768]{1,0:T(8,128)(2,1)S(1)}, u32[]{:S(2)}, u32[]{:S(2)}) collective-permute-start(bf16[704,768]{1,0:T(8,128)(2,1)S(1)} %get-tuple-element.219), channel_id=1, source_target_pairs={{0,4},{1,5},{2,6},{3,7},{4,0},{5,1},{6,2},{7,3},{8,12},{9,13},{10,... | collective-permute-start | bytes 3244040 | tf_op jit(solution)/shard_map/ppermute | solution.py:406
  68.7 11.4 %collective-permute-start.12 = (bf16[128,768]{1,0:T(8,128)(2,1)S(1)}, bf16[128,768]{1,0:T(8,128)(2,1)S(1)}, u32[]{:S(2)}, u32[]{:S(2)}) collective-permute-start(bf16[128,768]{1,0:T(8,128)(2,1)S(1)} %get-tuple-element.171), channel_id=1, source_target_pairs={{0,0},{1,16},{2,2},{3,18},{4,4},{5,20},{6,6},{7,22},{8,8},{9,24},{... | collective-permute-start | bytes 589832 | tf_op jit(solution)/shard_map/ppermute | solution.py:406
  69.4 10.8 %collective-permute-start.13 = (bf16[128,768]{1,0:T(8,128)(2,1)S(1)}, bf16[128,768]{1,0:T(8,128)(2,1)S(1)}, u32[]{:S(2)}, u32[]{:S(2)}) collective-permute-start(bf16[128,768]{1,0:T(8,128)(2,1)S(1)} %get-tuple-element.172), channel_id=1, source_target_pairs={{0,8},{1,24},{2,10},{3,26},{4,12},{5,28},{6,14},{7,30},{8,0},{9,16... | collective-permute-start | bytes 589832 | tf_op jit(solution)/shard_map/ppermute | solution.py:406
  82.9 4.1 %collective-permute-start.22 = (bf16[256,768]{1,0:T(8,128)(2,1)S(1)}, bf16[256,768]{1,0:T(8,128)(2,1)S(1)}, u32[]{:S(2)}, u32[]{:S(2)}) collective-permute-start(bf16[256,768]{1,0:T(8,128)(2,1)S(1)} %get-tuple-element.213), channel_id=1, source_target_pairs={{0,1},{1,0},{2,3},{3,2},{4,5},{5,4},{6,7},{7,6},{8,9},{9,8},{10,11... | collective-permute-start | bytes 1179656 | tf_op jit(solution)/shard_map/ppermute | solution.py:406
  85.7 4.6 %collective-permute-start.25 = (bf16[256,768]{1,0:T(8,128)(2,1)S(1)}, bf16[256,768]{1,0:T(8,128)(2,1)S(1)}, u32[]{:S(2)}, u32[]{:S(2)}) collective-permute-start(bf16[256,768]{1,0:T(8,128)(2,1)S(1)} %get-tuple-element.225), channel_id=1, source_target_pairs={{0,1},{1,0},{2,3},{3,2},{4,5},{5,4},{6,7},{7,6},{8,9},{9,8},{10,11... | collective-permute-start | bytes 1179656 | tf_op jit(solution)/shard_map/ppermute | solution.py:406
  92.9 12.1 %collective-permute-start.28 = (bf16[256,768]{1,0:T(8,128)(2,1)S(1)}, bf16[256,768]{1,0:T(8,128)(2,1)S(1)}, u32[]{:S(2)}, u32[]{:S(2)}) collective-permute-start(bf16[256,768]{1,0:T(8,128)(2,1)S(1)} %get-tuple-element.230), channel_id=1, source_target_pairs={{0,2},{1,3},{2,0},{3,1},{4,6},{5,7},{6,4},{7,5},{8,10},{9,11},{10,... | collective-permute-start | bytes 1179656 | tf_op jit(solution)/shard_map/ppermute | solution.py:406
  94.4 12.1 %collective-permute-start.29 = (bf16[256,768]{1,0:T(8,128)(2,1)S(1)}, bf16[256,768]{1,0:T(8,128)(2,1)S(1)}, u32[]{:S(2)}, u32[]{:S(2)}) collective-permute-start(bf16[256,768]{1,0:T(8,128)(2,1)S(1)} %get-tuple-element.231), channel_id=1, source_target_pairs={{0,4},{1,5},{2,6},{3,7},{4,0},{5,1},{6,2},{7,3},{8,12},{9,13},{10,... | collective-permute-start | bytes 1179656 | tf_op jit(solution)/shard_map/ppermute | solution.py:406
  95.9 25.6 %collective-permute-start.27 = (bf16[512,768]{1,0:T(8,128)(2,1)S(1)}, bf16[512,768]{1,0:T(8,128)(2,1)S(1)}, u32[]{:S(2)}, u32[]{:S(2)}) collective-permute-start(bf16[512,768]{1,0:T(8,128)(2,1)S(1)} %get-tuple-element.229), channel_id=1, source_target_pairs={{0,4},{1,5},{2,6},{3,7},{4,0},{5,1},{6,2},{7,3},{8,12},{9,13},{10,... | collective-permute-start | bytes 2359304 | tf_op jit(solution)/shard_map/ppermute | solution.py:406
  96.4 7.0 %collective-permute-start.30 = (bf16[2,96,768]{2,1,0:T(8,128)(2,1)S(1)}, bf16[2,96,768]{2,1,0:T(8,128)(2,1)S(1)}, u32[]{:S(2)}, u32[]{:S(2)}) collective-permute-start(bf16[2,96,768]{2,1,0:T(8,128)(2,1)S(1)} %get-tuple-element.235), channel_id=1, source_target_pairs={{0,8},{1,9},{2,10},{3,11},{4,12},{5,13},{6,14},{7,15},{8,0},{9,1},... | collective-permute-start | bytes 884744 | tf_op jit(solution)/shard_map/ppermute | solution.py:406
  97.1 24.5 %collective-permute-start.26 = (bf16[4,2,48,768]{3,2,1,0:T(8,128)(2,1)S(1)}, bf16[4,2,48,768]{3,2,1,0:T(8,128)(2,1)S(1)}, u32[]{:S(2)}, u32[]{:S(2)}) collective-permute-start(bf16[4,2,48,768]{3,2,1,0:T(8,128)(2,1)S(1)} %get-tuple-element.227), channel_id=1, source_target_pairs={{0,2},{1,3},{2,0},{3,1},{4,6},{5,7},{6,4},{7,5},{8,10},{9,11},{10,... | collective-permute-start | bytes 1769480 | tf_op jit(solution)/shard_map/ppermute | solution.py:406
  107.3 9.5 %collective-permute-start.32 = (bf16[2,128,768]{2,1,0:T(8,128)(2,1)S(1)}, bf16[2,128,768]{2,1,0:T(8,128)(2,1)S(1)}, u32[]{:S(2)}, u32[]{:S(2)}) collective-permute-start(bf16[2,128,768]{2,1,0:T(8,128)(2,1)S(1)} %get-tuple-element.240), channel_id=1, source_target_pairs={{0,8},{1,9},{2,10},{3,11},{4,12},{5,13},{6,14},{7,15},{8,0},{9,1},... | collective-permute-start | bytes 1179656 | tf_op jit(solution)/shard_map/ppermute | solution.py:406
  108.0 7.5 %collective-permute-start.31 = (bf16[96,768]{1,0:T(8,128)(2,1)S(1)}, bf16[96,768]{1,0:T(8,128)(2,1)S(1)}, u32[]{:S(2)}, u32[]{:S(2)}) collective-permute-start(bf16[96,768]{1,0:T(8,128)(2,1)S(1)} %get-tuple-element.238), channel_id=1, source_target_pairs={{0,16},{1,17},{2,18},{3,19},{4,20},{5,21},{6,22},{7,23},{8,24},{9,... | collective-permute-start | bytes 442376 | tf_op jit(solution)/shard_map/ppermute | solution.py:406
  117.4 10.8 %collective-permute-start.35 = (bf16[128,768]{1,0:T(8,128)(2,1)S(1)}, bf16[128,768]{1,0:T(8,128)(2,1)S(1)}, u32[]{:S(2)}, u32[]{:S(2)}) collective-permute-start(bf16[128,768]{1,0:T(8,128)(2,1)S(1)} %get-tuple-element.250), channel_id=1, source_target_pairs={{0,16},{1,17},{2,18},{3,19},{4,20},{5,21},{6,22},{7,23},{8,24},{9,... | collective-permute-start | bytes 589832 | tf_op jit(solution)/shard_map/ppermute | solution.py:406
  120.9 5.7 %collective-permute-start.37 = (bf16[96,768]{1,0:T(8,128)(2,1)S(1)}, bf16[96,768]{1,0:T(8,128)(2,1)S(1)}, u32[]{:S(2)}, u32[]{:S(2)}) collective-permute-start(bf16[96,768]{1,0:T(8,128)(2,1)S(1)} %get-tuple-element.257.refs_1_), channel_id=1, source_target_pairs={{0,2},{1,3},{2,0},{3,1},{4,6},{5,7},{6,4},{7,5},{8,10},{9,11},{10,... | collective-permute-start | bytes 442376 | tf_op jit(solution)/shard_map/ppermute | solution.py:406
  122.4 7.9 %collective-permute-start.34 = (bf16[4,48,768]{2,1,0:T(8,128)(2,1)S(1)}, bf16[4,48,768]{2,1,0:T(8,128)(2,1)S(1)}, u32[]{:S(2)}, u32[]{:S(2)}) collective-permute-start(bf16[4,48,768]{2,1,0:T(8,128)(2,1)S(1)} %get-tuple-element.245), channel_id=1, source_target_pairs={{0,4},{1,5},{2,6},{3,7},{4,0},{5,1},{6,2},{7,3},{8,12},{9,13},{10,... | collective-permute-start | bytes 884744 | tf_op jit(solution)/shard_map/ppermute | solution.py:406
  123.4 6.8 %collective-permute-start.33 = (bf16[4,32,768]{2,1,0:T(8,128)(2,1)S(1)}, bf16[4,32,768]{2,1,0:T(8,128)(2,1)S(1)}, u32[]{:S(2)}, u32[]{:S(2)}) collective-permute-start(bf16[4,32,768]{2,1,0:T(8,128)(2,1)S(1)} %get-tuple-element.244), channel_id=1, source_target_pairs={{0,2},{1,3},{2,0},{3,1},{4,6},{5,7},{6,4},{7,5},{8,10},{9,11},{10,... | collective-permute-start | bytes 589832 | tf_op jit(solution)/shard_map/ppermute | solution.py:406
  126.6 3.6 %collective-permute-start.38 = (bf16[96,768]{1,0:T(8,128)(2,1)S(1)}, bf16[96,768]{1,0:T(8,128)(2,1)S(1)}, u32[]{:S(2)}, u32[]{:S(2)}) collective-permute-start(bf16[96,768]{1,0:T(8,128)(2,1)S(1)} %collective-permute-done.37.refs_7_.refs_3_), channel_id=1, source_target_pairs={{0,1},{1,0},{2,3},{3,2},{4,5},{5,4},{6,7},{7,6},{8,9},{9,8},{10,11... | collective-permute-start | bytes 442376 | tf_op jit(solution)/shard_map/ppermute | solution.py:406
  128.2 2.0 %collective-permute-start.36 = (bf16[96,768]{1,0:T(8,128)(2,1)S(1)}, bf16[96,768]{1,0:T(8,128)(2,1)S(1)}, u32[]{:S(2)}, u32[]{:S(2)}) collective-permute-start(bf16[96,768]{1,0:T(8,128)(2,1)S(1)} %get-tuple-element.257.refs_1_), channel_id=1, source_target_pairs={{0,1},{1,0},{2,3},{3,2},{4,5},{5,4},{6,7},{7,6},{8,9},{9,8},{10,11... | collective-permute-start | bytes 442376 | tf_op jit(solution)/shard_map/ppermute | solution.py:406
  129.5 16.6 %collective-permute-start.48 = (bf16[128,768]{1,0:T(8,128)(2,1)S(1)}, bf16[128,768]{1,0:T(8,128)(2,1)S(1)}, u32[]{:S(2)}, u32[]{:S(2)}) collective-permute-start(bf16[128,768]{1,0:T(8,128)(2,1)S(1)} %get-tuple-element.268.refs_5_), channel_id=1, source_target_pairs={{0,2},{1,3},{2,0},{3,1},{4,6},{5,7},{6,4},{7,5},{8,10},{9,11},{10,... | collective-permute-start | bytes 589832 | tf_op jit(solution)/shard_map/ppermute | solution.py:406
  130.9 12.4 %collective-permute-start.39 = (bf16[80,768]{1,0:T(8,128)(2,1)S(1)}, bf16[80,768]{1,0:T(8,128)(2,1)S(1)}, u32[]{:S(2)}, u32[]{:S(2)}) collective-permute-start(bf16[80,768]{1,0:T(8,128)(2,1)S(1)} %get-tuple-element.259), channel_id=1, source_target_pairs={{0,16},{1,17},{2,18},{3,19},{4,20},{5,21},{6,22},{7,23},{8,24},{9,... | collective-permute-start | bytes 368648 | tf_op jit(solution)/shard_map/ppermute | solution.py:406
  132.1 11.2 %collective-permute-start.40 = (bf16[80,768]{1,0:T(8,128)(2,1)S(1)}, bf16[80,768]{1,0:T(8,128)(2,1)S(1)}, u32[]{:S(2)}, u32[]{:S(2)}) collective-permute-start(bf16[80,768]{1,0:T(8,128)(2,1)S(1)} %get-tuple-element.260), channel_id=1, source_target_pairs={{0,24},{1,25},{2,26},{3,27},{4,28},{5,29},{6,30},{7,31},{8,16},{9,... | collective-permute-start | bytes 368648 | tf_op jit(solution)/shard_map/ppermute | solution.py:406
  135.2 8.7 %collective-permute-start.41 = (bf16[80,768]{1,0:T(8,128)(2,1)S(1)}, bf16[80,768]{1,0:T(8,128)(2,1)S(1)}, u32[]{:S(2)}, u32[]{:S(2)}) collective-permute-start(bf16[80,768]{1,0:T(8,128)(2,1)S(1)} %get-tuple-element.261), channel_id=1, source_target_pairs={{0,8},{1,9},{2,10},{3,11},{4,12},{5,13},{6,14},{7,15},{8,0},{9,1},... | collective-permute-start | bytes 368648 | tf_op jit(solution)/shard_map/ppermute | solution.py:406
  135.2 15.3 %collective-permute-start.43 = (bf16[128,768]{1,0:T(8,128)(2,1)S(1)}, bf16[128,768]{1,0:T(8,128)(2,1)S(1)}, u32[]{:S(2)}, u32[]{:S(2)}) collective-permute-start(bf16[128,768]{1,0:T(8,128)(2,1)S(1)} %get-tuple-element.264), channel_id=1, source_target_pairs={{0,0},{1,16},{2,2},{3,18},{4,4},{5,20},{6,6},{7,22},{8,8},{9,24},{... | collective-permute-start | bytes 589832 | tf_op jit(solution)/shard_map/ppermute | solution.py:406
  144.6 6.0 %collective-permute-start.42 = (bf16[80,768]{1,0:T(8,128)(2,1)S(1)}, bf16[80,768]{1,0:T(8,128)(2,1)S(1)}, u32[]{:S(2)}, u32[]{:S(2)}) collective-permute-start(bf16[80,768]{1,0:T(8,128)(2,1)S(1)} %get-tuple-element.263.refs_1_), channel_id=1, source_target_pairs={{0,2},{1,3},{2,0},{3,1},{4,6},{5,7},{6,4},{7,5},{8,10},{9,11},{10,... | collective-permute-start | bytes 368648 | tf_op jit(solution)/shard_map/ppermute | solution.py:406
  146.1 5.0 %collective-permute-start.47 = (bf16[128,768]{1,0:T(8,128)(2,1)S(1)}, bf16[128,768]{1,0:T(8,128)(2,1)S(1)}, u32[]{:S(2)}, u32[]{:S(2)}) collective-permute-start(bf16[128,768]{1,0:T(8,128)(2,1)S(1)} %get-tuple-element.268.refs_5_), channel_id=1, source_target_pairs={{0,1},{1,0},{2,3},{3,2},{4,5},{5,4},{6,7},{7,6},{8,9},{9,8},{10,11... | collective-permute-start | bytes 589832 | tf_op jit(solution)/shard_map/ppermute | solution.py:406
  146.1 5.0 %collective-permute-start.49 = (bf16[128,768]{1,0:T(8,128)(2,1)S(1)}, bf16[128,768]{1,0:T(8,128)(2,1)S(1)}, u32[]{:S(2)}, u32[]{:S(2)}) collective-permute-start(bf16[128,768]{1,0:T(8,128)(2,1)S(1)} %collective-permute-done.48.refs_7_), channel_id=1, source_target_pairs={{0,1},{1,0},{2,3},{3,2},{4,5},{5,4},{6,7},{7,6},{8,9},{9,8},{10,11... | collective-permute-start | bytes 589832 | tf_op jit(solution)/shard_map/ppermute | solution.py:406
  146.6 9.2 %collective-permute-start.44 = (bf16[128,768]{1,0:T(8,128)(2,1)S(1)}, bf16[128,768]{1,0:T(8,128)(2,1)S(1)}, u32[]{:S(2)}, u32[]{:S(2)}) collective-permute-start(bf16[128,768]{1,0:T(8,128)(2,1)S(1)} %get-tuple-element.266), channel_id=1, source_target_pairs={{0,8},{1,24},{2,10},{3,26},{4,12},{5,28},{6,14},{7,30},{8,0},{9,16... | collective-permute-start | bytes 589832 | tf_op jit(solution)/shard_map/ppermute | solution.py:406
  150.6 2.8 %collective-permute-start.45 = (bf16[80,768]{1,0:T(8,128)(2,1)S(1)}, bf16[80,768]{1,0:T(8,128)(2,1)S(1)}, u32[]{:S(2)}, u32[]{:S(2)}) collective-permute-start(bf16[80,768]{1,0:T(8,128)(2,1)S(1)} %get-tuple-element.263.refs_1_), channel_id=1, source_target_pairs={{0,1},{1,0},{2,3},{3,2},{4,5},{5,4},{6,7},{7,6},{8,9},{9,8},{10,11... | collective-permute-start | bytes 368648 | tf_op jit(solution)/shard_map/ppermute | solution.py:406
  150.6 2.8 %collective-permute-start.46 = (bf16[80,768]{1,0:T(8,128)(2,1)S(1)}, bf16[80,768]{1,0:T(8,128)(2,1)S(1)}, u32[]{:S(2)}, u32[]{:S(2)}) collective-permute-start(bf16[80,768]{1,0:T(8,128)(2,1)S(1)} %collective-permute-done.42.refs_3_), channel_id=1, source_target_pairs={{0,1},{1,0},{2,3},{3,2},{4,5},{5,4},{6,7},{7,6},{8,9},{9,8},{10,11... | collective-permute-start | bytes 368648 | tf_op jit(solution)/shard_map/ppermute | solution.py:406
  (15 other events, 115.9 us)

commit v3 on v2

--- a/solution.py
+++ b/solution.py
@@ -1104,7 +1104,7 @@
     )
 
 
-def up_line_kernel(place, x_got, y_got, p, q, down_two, down_got, send, keep, down_send, down_keep):
+def up_line_kernel(place, y_got, x_got, p, q, down_two, down_got, send, keep, down_send, down_keep):
     low, high_here = place[0] % 2, place[0] // 2
     half = UP_ROWS // 2
     for target, parity in ((keep, low), (send, 1 - low)):
@@ -1396,7 +1396,7 @@
     across = y_swap(qy_send)
     joint_pair = (joint_px, x_swap(px_send), joint_qy, across)
     (up_send, up_two, down_send, down_keep), mark = up_line_stage(
-        place, (x_got, y_got, p, q_, down_two, down_got), (mark,)
+        place, (y_got, x_got, p, q_, down_two, down_got), (mark,)
     )
     up_got, down_got = z_swap(up_send, 1), z_swap(down_send, 2)
     (up_send, up_keep), mark = end_stage(place, up_two, up_got, (mark, down_got))

time: 158 us -> 157 us (level)
  no operation moved by 1% of the time
where the time goes in v3:
time: 157 us
  Pallas kernels  57.8 us (37%)
  starting transfers between devices  49.3 us (31%)
  waiting for transfers between devices  43.5 us (28%)
  local copies, waits for them, and re-layouts  4.62 us (3%)
    pallas_call x23, Pallas kernels, call(): pl.pallas_call(ordered, grid_spec=pltpu.PrefetchScalarGridSpec(num_scalar...  57.8 us
    ppermute x50, starting transfers between devices, permute(): return lax.ppermute(value, AXES, pairs)  49.3 us
    ppermute x50, waiting for transfers between devices, permute(): return lax.ppermute(value, AXES, pairs)  43.5 us
  transfers between devices with their start and end apart: 50, of which 22 were waited for; matrix products, arithmetic and copies ran while one was open for 1% of the time, Pallas kernels for 30%

profile of v3, /device:TPU:0, one launch (start us, length us, event | category | flops | bytes accessed | tf_op | source)
XLA Modules:
  0.0 156.5 jit_solution(18423928647308923406)
XLA Ops:
  0.7 1.1 dynamic-slice_bitcast_fusion.2
  1.8 3.1 %collective-permute-start.1 = (bf16[128,768]{1,0:T(8,128)(2,1)S(1)}, bf16[128,768]{1,0:T(8,128)(2,1)S(1)}, u32[]{:S(2)}, u32[]{:S(2)}) collective-permute-start(bf16[128,768]{1,0:T(8,128)(2,1)S(1)} %get-tuple-element.289), channel_id=1, source_target_pairs={{0,8},{1,24},{2,10},{3,26},{4,12},{5,28},{6,14},{7,30},{8,0},{9,16... | collective-permute-start | bytes 589832 | tf_op jit(solution)/shard_map/ppermute | solution.py:406
  5.6 3.5 %collective-permute-start.2 = (s32[2,16]{1,0:T(2,128)}, s32[2,16]{1,0:T(2,128)S(1)}, u32[]{:S(2)}, u32[]{:S(2)}) collective-permute-start(s32[2,16]{1,0:T(2,128)} %refs_1_.4), channel_id=1, source_target_pairs={{0,1},{1,0},{2,3},{3,2},{4,5},{5,4},{6,7},{7,6},{8,9},{9,8},{10,11... | collective-permute-start | bytes 392 | tf_op jit(solution)/shard_map/ppermute | solution.py:406
  10.5 2.0 %copy-done.3 = bf16[768,2304]{1,0:T(8,128)(2,1)S(1)} copy-done((bf16[768,2304]{1,0:T(8,128)(2,1)S(1)}, bf16[768,2304]{1,0:T(8,128)(2,1)}, u32[]{:S(2)}) %copy-start.3) | copy-done | bytes 3538968
  12.5 1.5 own_columns.1
  14.0 2.0 %collective-permute-start.5 = (bf16[128,768]{1,0:T(8,128)(2,1)S(1)}, bf16[128,768]{1,0:T(8,128)(2,1)S(1)}, u32[]{:S(2)}, u32[]{:S(2)}) collective-permute-start(bf16[128,768]{1,0:T(8,128)(2,1)S(1)} %collective-permute-done.refs_3_.refs_6_.refs_1_), channel_id=1, source_target_pairs={{0,1},{1,0},{2,3},{3,2},{4,5},{5,4},{6,7},{7,6},{8,9},{9,8},{10,11... | collective-permute-start | bytes 589832 | tf_op jit(solution)/shard_map/ppermute | solution.py:406
  16.0 1.5 collective-permute-start.3
  18.9 5.0 %first_attention.1 = (bf16[512,384]{1,0:T(8,128)(2,1)S(1)}, bf16[512,384]{1,0:T(8,128)(2,1)S(1)}, bf16[512,384]{1,0:T(8,128)(2,1)S(1)}, f32[3,128,1024]{2,1,0:T(...) custom-call(s32[4]{0:T(128)S(1)} %pad_add_fusion.refs_0_, s32[2,16]{1,0:T(2,128)S(1)} %copy-done.5, ...), custom_call_target="tpu_custom_call" | custom-call | flops 1024 | bytes 1024 | tf_op jit(solution)/shard_map/first_attention/pallas_call | solution.py:369
  23.9 3.6 %collective-permute-done.4.refs_4_.refs_6_ = bf16[128,768]{1,0:T(8,128)(2,1)S(1)} collective-permute-done((bf16[128,768]{1,0:T(8,128)(2,1)S(1)}, bf16[128,768]{1,0:T(8,128)(2,1)S(1)}, u32[]{:S(2)}, u32[]{:S(2)}) %collective-permute-start.4) | collective-permute-done | bytes 196640 | tf_op jit(solution)/shard_map/ppermute | solution.py:406
  29.9 5.0 %attention.1 = (bf16[512,384]{1,0:T(8,128)(2,1)S(1)}, bf16[512,384]{1,0:T(8,128)(2,1)S(1)}, bf16[512,384]{1,0:T(8,128)(2,1)S(1)}, f32[8,512]{1,0:T(8,128)S(1)}, f32[8,128]{1,0:T(8,128)S(1)}) custom-call(s32[4]{0:T(128)S(1)} %pad_add_fusion.refs_0_, s32[2,16]{1,0:T(2,128)S(1)} %copy-done.5, s32[2,16]{1,0:T(2,128)S(1)} %collective-permute-done.2.refs_2_, ...), custom_call_target="tpu_custom_call" | custom-call | flops 1024 | bytes 1024 | tf_op jit(solution)/shard_map/attention/pallas_call | solution.py:369
  35.4 1.3 collective-permute-done.11.refs_2_
  36.7 6.4 %forward.1 = (bf16[128,768]{1,0:T(8,128)(2,1)S(1)}, bf16[128,768]{1,0:T(8,128)(2,1)S(1)}, bf16[272,768]{1,0:T(8,128)(2,1)S(1)}, f32[256,768]{1,0:T(8,128)S(1)}, ...) custom-call(s32[4]{0:T(128)S(1)} %pad_add_fusion.refs_0_, ...), custom_call_target="tpu_custom_call" | custom-call | flops 1024 | bytes 1024 | tf_op jit(solution)/shard_map/forward/pallas_call | solution.py:369
  44.0 2.1 %collective-permute-done.15.refs_4_.refs_12_ = bf16[272,768]{1,0:T(8,128)(2,1)S(1)} collective-permute-done((bf16[272,768]{1,0:T(8,128)(2,1)S(1)}, bf16[272,768]{1,0:T(8,128)(2,1)S(1)}, u32[]{:S(2)}, u32[]{:S(2)}) %collective-permute-start.15) | collective-permute-done | bytes 417824 | tf_op jit(solution)/shard_map/ppermute | solution.py:406
  46.0 2.6 %down_units.1 = (bf16[4,2,48,768]{3,2,1,0:T(8,128)(2,1)S(1)}, bf16[4,2,48,768]{3,2,1,0:T(8,128)(2,1)S(1)}, bf16[4,2,48,768]{3,2,1,0:T(8,128)(2,1)S(1)}, bf16[4,2,48,768]{3,2,1,0:T(8,128)(2,1)S(1)}, f32[8,128]{1,0:T(8,128)S(1)}) custom-call(s32[4]{0:T(128)S(1)} %pad_add_fusion.refs_0_, bf16[16,96,256]{2,1,0:T(8,128)(2,1)S(1)} %get-tuple-element.183.refs_1_, ...), custom_call_target="tpu_custom_call" | custom-call | flops 1024 | bytes 1024 | tf_op jit(solution)/shard_map/down_units/pallas_call | solution.py:369
  48.7 1.6 %collective-permute-start.18 = (bf16[4,2,48,768]{3,2,1,0:T(8,128)(2,1)S(1)}, bf16[4,2,48,768]{3,2,1,0:T(8,128)(2,1)S(1)}, u32[]{:S(2)}, u32[]{:S(2)}) collective-permute-start(bf16[4,2,48,768]{3,2,1,0:T(8,128)(2,1)S(1)} %get-tuple-element.191), channel_id=1, source_target_pairs={{0,2},{1,3},{2,0},{3,1},{4,6},{5,7},{6,4},{7,5},{8,10},{9,11},{10,... | collective-permute-start | bytes 1769480 | tf_op jit(solution)/shard_map/ppermute | solution.py:406
  50.3 1.5 collective-permute-start.19
  51.8 5.0 %backward.1 = (bf16[256,768]{1,0:T(8,128)(2,1)S(1)}, bf16[256,768]{1,0:T(8,128)(2,1)S(1)}, bf16[256,768]{1,0:T(8,128)(2,1)S(1)}, bf16[256,768]{1,0:T(8,128)(2,1)...) custom-call(s32[4]{0:T(128)S(1)} %pad_add_fusion.refs_0_, ...), custom_call_target="tpu_custom_call" | custom-call | flops 1024 | bytes 1024 | tf_op jit(solution)/shard_map/backward/pallas_call | solution.py:369
  57.5 1.7 %collective-permute-done.20.refs_5_ = bf16[256,768]{1,0:T(8,128)(2,1)S(1)} collective-permute-done((bf16[256,768]{1,0:T(8,128)(2,1)S(1)}, bf16[256,768]{1,0:T(8,128)(2,1)S(1)}, u32[]{:S(2)}, u32[]{:S(2)}) %collective-permute-start.20) | collective-permute-done | bytes 393248 | tf_op jit(solution)/shard_map/ppermute | solution.py:406
  59.8 3.3 %up_units.1 = (bf16[704,768]{1,0:T(8,128)(2,1)S(1)}, bf16[704,768]{1,0:T(8,128)(2,1)S(1)}, bf16[4,2,64,768]{3,2,1,0:T(8,128)(2,1)S(1)}, bf16[4,2,64,768]{3,2,1,0:T(8,128)(2,1)S(1)}, f32[8,128]{1,0:T(8,128)S(1)}) custom-call(s32[4]{0:T(128)S(1)} %pad_add_fusion.refs_0_, bf16[768,256]{1,0:T(8,128)(2,1)S(1)} %get-tuple-element.194.refs_1_, ...), custom_call_target="tpu_custom_call" | custom-call | flops 1024 | bytes 1024 | tf_op jit(solution)/shard_map/up_units/pallas_call | solution.py:369
  63.1 1.2 collective-permute-done.18.refs_2_
  64.3 1.2 collective-permute-done.19.refs_4_
  65.5 1.1 down_pair_stage.1
  67.2 1.5 collective-permute-start.24
  70.0 10.1 %attention_back.1 = (bf16[512,384]{1,0:T(8,128)(2,1)S(1)}, bf16[1024,384]{1,0:T(8,128)(2,1)S(1)}, bf16[1024,384]{1,0:T(8,128)(2,1)S(1)}, f32[8,128]{1,0:T(8,128)S(1)}) custom-call(s32[4]{0:T(128)S(1)} %pad_add_fusion.refs_0_, s32[2,16]{1,0:T(2,128)S(1)} %copy-done.5, s32[2,16]{1,0:T(2,128)S(1)} %collective-permute-done.2.refs_2_, ...), custom_call_target="tpu_custom_call" | custom-call | flops 1024 | bytes 1024 | tf_op jit(solution)/shard_map/attention_back/pallas_call | solution.py:369
  80.2 2.8 %token_parts.1 = (bf16[256,768]{1,0:T(8,128)(2,1)S(1)}, bf16[256,768]{1,0:T(8,128)(2,1)S(1)}, bf16[256,768]{1,0:T(8,128)(2,1)S(1)}, bf16[256,768]{1,0:T(8,128)(2,1)S(1)}, f32[8,128]{1,0:T(8,128)S(1)}) custom-call(s32[4]{0:T(128)S(1)} %pad_add_fusion.refs_0_, bf16[512,384]{1,0:T(8,128)(2,1)S(1)} %get-tuple-element.208.refs_1_.refs_9_, ...), custom_call_target="tpu_custom_call" | custom-call | flops 1024 | bytes 1024 | tf_op jit(solution)/shard_map/token_parts/pallas_call | solution.py:369
  82.9 2.8 %collective-permute-start.22 = (bf16[256,768]{1,0:T(8,128)(2,1)S(1)}, bf16[256,768]{1,0:T(8,128)(2,1)S(1)}, u32[]{:S(2)}, u32[]{:S(2)}) collective-permute-start(bf16[256,768]{1,0:T(8,128)(2,1)S(1)} %get-tuple-element.213), channel_id=1, source_target_pairs={{0,1},{1,0},{2,3},{3,2},{4,5},{5,4},{6,7},{7,6},{8,9},{9,8},{10,11... | collective-permute-start | bytes 1179656 | tf_op jit(solution)/shard_map/ppermute | solution.py:406
  85.8 1.3 collective-permute-done.22.refs_13_
  87.1 3.2 %joint_units.1 = (bf16[4,2,48,768]{3,2,1,0:T(8,128)(2,1)S(1)}, bf16[4,2,48,768]{3,2,1,0:T(8,128)(2,1)S(1)}, bf16[512,768]{1,0:T(8,128)(2,1)S(1)}, bf16[4,2,32,768]{3,2,1,0:T(8,128)(2,1)S(1)}, f32[8,128]{1,0:T(8,128)S(1)}) custom-call(s32[4]{0:T(128)S(1)} %pad_add_fusion.refs_0_, bf16[128,768]{1,0:T(8,128)(2,1)S(1)} %collective-permute-done.refs_3_.refs_6_.refs_1_, ...), custom_call_target="tpu_custom_call" | custom-call | flops 1024 | bytes 1024 | tf_op jit(solution)/shard_map/joint_units/pallas_call | solution.py:369
  90.3 1.3 collective-permute-done.23.refs_1_
  92.9 1.6 %collective-permute-start.28 = (bf16[256,768]{1,0:T(8,128)(2,1)S(1)}, bf16[256,768]{1,0:T(8,128)(2,1)S(1)}, u32[]{:S(2)}, u32[]{:S(2)}) collective-permute-start(bf16[256,768]{1,0:T(8,128)(2,1)S(1)} %get-tuple-element.230), channel_id=1, source_target_pairs={{0,4},{1,5},{2,6},{3,7},{4,0},{5,1},{6,2},{7,3},{8,12},{9,13},{10,... | collective-permute-start | bytes 1179656 | tf_op jit(solution)/shard_map/ppermute | solution.py:406
  94.5 1.4 collective-permute-start.29
  97.7 5.7 %collective-permute-done.30.refs_6_ = bf16[2,96,768]{2,1,0:T(8,128)(2,1)S(1)} collective-permute-done((bf16[2,96,768]{2,1,0:T(8,128)(2,1)S(1)}, bf16[2,96,768]{2,1,0:T(8,128)(2,1)S(1)}, u32[]{:S(2)}, u32[]{:S(2)}) %collective-permute-start.30) | collective-permute-done | bytes 294944 | tf_op jit(solution)/shard_map/ppermute | solution.py:406
  103.4 1.6 %collective-permute-done.28.refs_1_ = bf16[256,768]{1,0:T(8,128)(2,1)S(1)} collective-permute-done((bf16[256,768]{1,0:T(8,128)(2,1)S(1)}, bf16[256,768]{1,0:T(8,128)(2,1)S(1)}, u32[]{:S(2)}, u32[]{:S(2)}) %collective-permute-start.28) | collective-permute-done | bytes 393248 | tf_op jit(solution)/shard_map/ppermute | solution.py:406
  105.0 1.5 collective-permute-done.29.refs_2_
  108.1 1.8 %collective-permute-start.31 = (bf16[96,768]{1,0:T(8,128)(2,1)S(1)}, bf16[96,768]{1,0:T(8,128)(2,1)S(1)}, u32[]{:S(2)}, u32[]{:S(2)}) collective-permute-start(bf16[96,768]{1,0:T(8,128)(2,1)S(1)} %get-tuple-element.238), channel_id=1, source_target_pairs={{0,16},{1,17},{2,18},{3,19},{4,20},{5,21},{6,22},{7,23},{8,24},{9,... | collective-permute-start | bytes 442376 | tf_op jit(solution)/shard_map/ppermute | solution.py:406
  109.9 5.0 %collective-permute-done.31.refs_4_.refs_2_ = bf16[96,768]{1,0:T(8,128)(2,1)S(1)} collective-permute-done((bf16[96,768]{1,0:T(8,128)(2,1)S(1)}, bf16[96,768]{1,0:T(8,128)(2,1)S(1)}, u32[]{:S(2)}, u32[]{:S(2)}) %collective-permute-start.31) | collective-permute-done | bytes 147488 | tf_op jit(solution)/shard_map/ppermute | solution.py:406
  114.9 1.9 %collective-permute-done.32.refs_2_ = bf16[2,128,768]{2,1,0:T(8,128)(2,1)S(1)} collective-permute-done((bf16[2,128,768]{2,1,0:T(8,128)(2,1)S(1)}, bf16[2,128,768]{2,1,0:T(8,128)(2,1)S(1)}, u32[]{:S(2)}, u32[]{:S(2)}) %collective-permute-start.32) | collective-permute-done | bytes 393248 | tf_op jit(solution)/shard_map/ppermute | solution.py:406
  117.5 2.0 %collective-permute-start.35 = (bf16[128,768]{1,0:T(8,128)(2,1)S(1)}, bf16[128,768]{1,0:T(8,128)(2,1)S(1)}, u32[]{:S(2)}, u32[]{:S(2)}) collective-permute-start(bf16[128,768]{1,0:T(8,128)(2,1)S(1)} %get-tuple-element.250), channel_id=1, source_target_pairs={{0,16},{1,17},{2,18},{3,19},{4,20},{5,21},{6,22},{7,23},{8,24},{9,... | collective-permute-start | bytes 589832 | tf_op jit(solution)/shard_map/ppermute | solution.py:406
  120.0 1.6 collective-permute-start.37
  122.4 1.5 collective-permute-start.34
  124.4 2.4 %collective-permute-done.37.refs_7_.refs_3_ = bf16[96,768]{1,0:T(8,128)(2,1)S(1)} collective-permute-done((bf16[96,768]{1,0:T(8,128)(2,1)S(1)}, bf16[96,768]{1,0:T(8,128)(2,1)S(1)}, u32[]{:S(2)}, u32[]{:S(2)}) %collective-permute-start.37) | collective-permute-done | bytes 147488 | tf_op jit(solution)/shard_map/ppermute | solution.py:406
  128.7 1.6 collective-permute-start.48
  131.0 4.4 %collective-permute-start.40 = (bf16[80,768]{1,0:T(8,128)(2,1)S(1)}, bf16[80,768]{1,0:T(8,128)(2,1)S(1)}, u32[]{:S(2)}, u32[]{:S(2)}) collective-permute-start(bf16[80,768]{1,0:T(8,128)(2,1)S(1)} %get-tuple-element.260), channel_id=1, source_target_pairs={{0,24},{1,25},{2,26},{3,27},{4,28},{5,29},{6,30},{7,31},{8,16},{9,... | collective-permute-start | bytes 368648 | tf_op jit(solution)/shard_map/ppermute | solution.py:406
  136.1 7.3 %collective-permute-done.39.refs_2_ = bf16[80,768]{1,0:T(8,128)(2,1)S(1)} collective-permute-done((bf16[80,768]{1,0:T(8,128)(2,1)S(1)}, bf16[80,768]{1,0:T(8,128)(2,1)S(1)}, u32[]{:S(2)}, u32[]{:S(2)}) %collective-permute-start.39) | collective-permute-done | bytes 122912 | tf_op jit(solution)/shard_map/ppermute | solution.py:406
  145.7 4.0 %collective-permute-start.44 = (bf16[128,768]{1,0:T(8,128)(2,1)S(1)}, bf16[128,768]{1,0:T(8,128)(2,1)S(1)}, u32[]{:S(2)}, u32[]{:S(2)}) collective-permute-start(bf16[128,768]{1,0:T(8,128)(2,1)S(1)} %get-tuple-element.266), channel_id=1, source_target_pairs={{0,8},{1,24},{2,10},{3,26},{4,12},{5,28},{6,14},{7,30},{8,0},{9,16... | collective-permute-start | bytes 589832 | tf_op jit(solution)/shard_map/ppermute | solution.py:406
  150.2 2.2 %dense_outputs.1 = (f32[384,768]{1,0:T(8,128)}, f32[96,3072]{1,0:T(8,128)}, f32[96,768]{1,0:T(8,128)}, f32[1,96]{1,0:T(1,128)}, f32[1,96]{1,0:T(1,128)}, /*index...) custom-call(s32[4]{0:T(128)S(1)} %pad_add_fusion.refs_0_, ...), custom_call_target="tpu_custom_call" | custom-call | flops 1024 | bytes 1024 | tf_op jit(solution)/shard_map/dense_outputs/pallas_call | solution.py:369
  152.5 1.5 joint_outputs.1
  154.9 1.6 %back_rows.1 = (bf16[2,128,768]{2,1,0:T(8,128)(2,1)}, f32[2,128,768]{2,1,0:T(8,128)}, f32[8,128]{1,0:T(8,128)}) custom-call(s32[4]{0:T(128)S(1)} %pad_add_fusion.refs_0_, bf16[128,768]{1,0:T(8,128)(2,1)S(1)} %collective-permute-done.12.refs_6_.refs_1_, bf16[128,768]{1,0:T(8,128)(2,1)S(1)} %collective-permute-done.13.refs_7_.refs_2_, ...), custom_call_target="tpu_custom_call" | custom-call | flops 1024 | bytes 1024 | tf_op jit(solution)/shard_map/back_rows/pallas_call | solution.py:369
  (114 shorter events, 24.4 us)
Async XLA Ops:
  1.8 12.2 %collective-permute-start.1 = (bf16[128,768]{1,0:T(8,128)(2,1)S(1)}, bf16[128,768]{1,0:T(8,128)(2,1)S(1)}, u32[]{:S(2)}, u32[]{:S(2)}) collective-permute-start(bf16[128,768]{1,0:T(8,128)(2,1)S(1)} %get-tuple-element.289), channel_id=1, source_target_pairs={{0,8},{1,24},{2,10},{3,26},{4,12},{5,28},{6,14},{7,30},{8,0},{9,16... | collective-permute-start | bytes 589832 | tf_op jit(solution)/shard_map/ppermute | solution.py:406
  4.9 9.1 %collective-permute-start = (bf16[128,768]{1,0:T(8,128)(2,1)S(1)}, bf16[128,768]{1,0:T(8,128)(2,1)S(1)}, u32[]{:S(2)}, u32[]{:S(2)}) collective-permute-start(bf16[128,768]{1,0:T(8,128)(2,1)S(1)} %get-tuple-element.290), channel_id=1, source_target_pairs={{0,0},{1,16},{2,2},{3,18},{4,4},{5,20},{6,6},{7,22},{8,8},{9,24},{... | collective-permute-start | bytes 589832 | tf_op jit(solution)/shard_map/ppermute | solution.py:406
  5.6 8.4 %collective-permute-start.2 = (s32[2,16]{1,0:T(2,128)}, s32[2,16]{1,0:T(2,128)S(1)}, u32[]{:S(2)}, u32[]{:S(2)}) collective-permute-start(s32[2,16]{1,0:T(2,128)} %refs_1_.4), channel_id=1, source_target_pairs={{0,1},{1,0},{2,3},{3,2},{4,5},{5,4},{6,7},{7,6},{8,9},{9,8},{10,11... | collective-permute-start | bytes 392 | tf_op jit(solution)/shard_map/ppermute | solution.py:406
  14.0 4.8 %collective-permute-start.5 = (bf16[128,768]{1,0:T(8,128)(2,1)S(1)}, bf16[128,768]{1,0:T(8,128)(2,1)S(1)}, u32[]{:S(2)}, u32[]{:S(2)}) collective-permute-start(bf16[128,768]{1,0:T(8,128)(2,1)S(1)} %collective-permute-done.refs_3_.refs_6_.refs_1_), channel_id=1, source_target_pairs={{0,1},{1,0},{2,3},{3,2},{4,5},{5,4},{6,7},{7,6},{8,9},{9,8},{10,11... | collective-permute-start | bytes 589832 | tf_op jit(solution)/shard_map/ppermute | solution.py:406
  16.0 2.9 %collective-permute-start.6 = (bf16[128,768]{1,0:T(8,128)(2,1)S(1)}, bf16[128,768]{1,0:T(8,128)(2,1)S(1)}, u32[]{:S(2)}, u32[]{:S(2)}) collective-permute-start(bf16[128,768]{1,0:T(8,128)(2,1)S(1)} %collective-permute-done.1.refs_4_.refs_7_.refs_2_), channel_id=1, source_target_pairs={{0,1},{1,0},{2,3},{3,2},{4,5},{5,4},{6,7},{7,6},{8,9},{9,8},{10,11... | collective-permute-start | bytes 589832 | tf_op jit(solution)/shard_map/ppermute | solution.py:406
  16.0 7.9 %collective-permute-start.3 = (bf16[128,768]{1,0:T(8,128)(2,1)S(1)}, bf16[128,768]{1,0:T(8,128)(2,1)S(1)}, u32[]{:S(2)}, u32[]{:S(2)}) collective-permute-start(bf16[128,768]{1,0:T(8,128)(2,1)S(1)} %collective-permute-done.refs_3_.refs_6_.refs_1_), channel_id=1, source_target_pairs={{0,4},{1,5},{2,6},{3,7},{4,0},{5,1},{6,2},{7,3},{8,12},{9,13},{10,... | collective-permute-start | bytes 589832 | tf_op jit(solution)/shard_map/ppermute | solution.py:406
  17.5 10.0 %collective-permute-start.4 = (bf16[128,768]{1,0:T(8,128)(2,1)S(1)}, bf16[128,768]{1,0:T(8,128)(2,1)S(1)}, u32[]{:S(2)}, u32[]{:S(2)}) collective-permute-start(bf16[128,768]{1,0:T(8,128)(2,1)S(1)} %collective-permute-done.1.refs_4_.refs_7_.refs_2_), channel_id=1, source_target_pairs={{0,4},{1,5},{2,6},{3,7},{4,0},{5,1},{6,2},{7,3},{8,12},{9,13},{10,... | collective-permute-start | bytes 589832 | tf_op jit(solution)/shard_map/ppermute | solution.py:406
  18.1 16.8 %collective-permute-start.9 = (bf16[144,768]{1,0:T(8,128)(2,1)S(1)}, bf16[144,768]{1,0:T(8,128)(2,1)S(1)}, u32[]{:S(2)}, u32[]{:S(2)}) collective-permute-start(bf16[144,768]{1,0:T(8,128)(2,1)S(1)} %concatenate.6), channel_id=1, source_target_pairs={{0,0},{1,16},{2,2},{3,18},{4,4},{5,20},{6,6},{7,22},{8,8},{9,24},{... | collective-permute-start | bytes 663560 | tf_op jit(solution)/shard_map/ppermute | solution.py:406
  18.8 16.1 %collective-permute-start.10 = (bf16[144,768]{1,0:T(8,128)(2,1)S(1)}, bf16[144,768]{1,0:T(8,128)(2,1)S(1)}, u32[]{:S(2)}, u32[]{:S(2)}) collective-permute-start(bf16[144,768]{1,0:T(8,128)(2,1)S(1)} %concatenate.7), channel_id=1, source_target_pairs={{0,8},{1,24},{2,10},{3,26},{4,12},{5,28},{6,14},{7,30},{8,0},{9,16... | collective-permute-start | bytes 663560 | tf_op jit(solution)/shard_map/ppermute | solution.py:406
  27.5 1.9 %collective-permute-start.7 = (bf16[128,768]{1,0:T(8,128)(2,1)S(1)}, bf16[128,768]{1,0:T(8,128)(2,1)S(1)}, u32[]{:S(2)}, u32[]{:S(2)}) collective-permute-start(bf16[128,768]{1,0:T(8,128)(2,1)S(1)} %collective-permute-done.3.refs_3_.refs_5_), channel_id=1, source_target_pairs={{0,1},{1,0},{2,3},{3,2},{4,5},{5,4},{6,7},{7,6},{8,9},{9,8},{10,11... | collective-permute-start | bytes 589832 | tf_op jit(solution)/shard_map/ppermute | solution.py:406
  43.1 3.0 %collective-permute-start.14 = (bf16[16,96,256]{2,1,0:T(8,128)(2,1)S(1)}, bf16[16,96,256]{2,1,0:T(8,128)(2,1)S(1)}, u32[]{:S(2)}, u32[]{:S(2)}) collective-permute-start(bf16[16,96,256]{2,1,0:T(8,128)(2,1)S(1)} %get-tuple-element.184), channel_id=1, source_target_pairs={{0,1},{1,0},{2,3},{3,2},{4,5},{5,4},{6,7},{7,6},{8,9},{9,8},{10,11... | collective-permute-start | bytes 2359304 | tf_op jit(solution)/shard_map/ppermute | solution.py:406
  43.4 2.6 %collective-permute-start.15 = (bf16[272,768]{1,0:T(8,128)(2,1)S(1)}, bf16[272,768]{1,0:T(8,128)(2,1)S(1)}, u32[]{:S(2)}, u32[]{:S(2)}) collective-permute-start(bf16[272,768]{1,0:T(8,128)(2,1)S(1)} %get-tuple-element.178.refs_3_.refs_1_), channel_id=1, source_target_pairs={{0,1},{1,0},{2,3},{3,2},{4,5},{5,4},{6,7},{7,6},{8,9},{9,8},{10,11... | collective-permute-start | bytes 1253384 | tf_op jit(solution)/shard_map/ppermute | solution.py:406
  43.7 8.1 %collective-permute-start.16 = (bf16[256,768]{1,0:T(8,128)(2,1)S(1)}, bf16[256,768]{1,0:T(8,128)(2,1)S(1)}, u32[]{:S(2)}, u32[]{:S(2)}) collective-permute-start(bf16[256,768]{1,0:T(8,128)(2,1)S(1)} %get-tuple-element.187), channel_id=1, source_target_pairs={{0,1},{1,0},{2,3},{3,2},{4,5},{5,4},{6,7},{7,6},{8,9},{9,8},{10,11... | collective-permute-start | bytes 1179656 | tf_op jit(solution)/shard_map/ppermute | solution.py:406
  48.7 15.6 %collective-permute-start.18 = (bf16[4,2,48,768]{3,2,1,0:T(8,128)(2,1)S(1)}, bf16[4,2,48,768]{3,2,1,0:T(8,128)(2,1)S(1)}, u32[]{:S(2)}, u32[]{:S(2)}) collective-permute-start(bf16[4,2,48,768]{3,2,1,0:T(8,128)(2,1)S(1)} %get-tuple-element.191), channel_id=1, source_target_pairs={{0,2},{1,3},{2,0},{3,1},{4,6},{5,7},{6,4},{7,5},{8,10},{9,11},{10,... | collective-permute-start | bytes 1769480 | tf_op jit(solution)/shard_map/ppermute | solution.py:406
  50.3 15.2 %collective-permute-start.19 = (bf16[4,2,48,768]{3,2,1,0:T(8,128)(2,1)S(1)}, bf16[4,2,48,768]{3,2,1,0:T(8,128)(2,1)S(1)}, u32[]{:S(2)}, u32[]{:S(2)}) collective-permute-start(bf16[4,2,48,768]{3,2,1,0:T(8,128)(2,1)S(1)} %get-tuple-element.193), channel_id=1, source_target_pairs={{0,4},{1,5},{2,6},{3,7},{4,0},{5,1},{6,2},{7,3},{8,12},{9,13},{10,... | collective-permute-start | bytes 1769480 | tf_op jit(solution)/shard_map/ppermute | solution.py:406
  56.8 3.0 %collective-permute-start.17 = (bf16[272,768]{1,0:T(8,128)(2,1)S(1)}, bf16[272,768]{1,0:T(8,128)(2,1)S(1)}, u32[]{:S(2)}, u32[]{:S(2)}) collective-permute-start(bf16[272,768]{1,0:T(8,128)(2,1)S(1)} %get-tuple-element.189), channel_id=1, source_target_pairs={{0,1},{1,0},{2,3},{3,2},{4,5},{5,4},{6,7},{7,6},{8,9},{9,8},{10,11... | collective-permute-start | bytes 1253384 | tf_op jit(solution)/shard_map/ppermute | solution.py:406
  56.9 2.3 %collective-permute-start.20 = (bf16[256,768]{1,0:T(8,128)(2,1)S(1)}, bf16[256,768]{1,0:T(8,128)(2,1)S(1)}, u32[]{:S(2)}, u32[]{:S(2)}) collective-permute-start(bf16[256,768]{1,0:T(8,128)(2,1)S(1)} %get-tuple-element.197), channel_id=1, source_target_pairs={{0,1},{1,0},{2,3},{3,2},{4,5},{5,4},{6,7},{7,6},{8,9},{9,8},{10,11... | collective-permute-start | bytes 1179656 | tf_op jit(solution)/shard_map/ppermute | solution.py:406
  57.4 2.4 %collective-permute-start.21 = (bf16[256,768]{1,0:T(8,128)(2,1)S(1)}, bf16[256,768]{1,0:T(8,128)(2,1)S(1)}, u32[]{:S(2)}, u32[]{:S(2)}) collective-permute-start(bf16[256,768]{1,0:T(8,128)(2,1)S(1)} %get-tuple-element.198), channel_id=1, source_target_pairs={{0,1},{1,0},{2,3},{3,2},{4,5},{5,4},{6,7},{7,6},{8,9},{9,8},{10,11... | collective-permute-start | bytes 1179656 | tf_op jit(solution)/shard_map/ppermute | solution.py:406
  66.6 25.0 %collective-permute-start.23 = (bf16[704,768]{1,0:T(8,128)(2,1)S(1)}, bf16[704,768]{1,0:T(8,128)(2,1)S(1)}, u32[]{:S(2)}, u32[]{:S(2)}) collective-permute-start(bf16[704,768]{1,0:T(8,128)(2,1)S(1)} %get-tuple-element.218), channel_id=1, source_target_pairs={{0,2},{1,3},{2,0},{3,1},{4,6},{5,7},{6,4},{7,5},{8,10},{9,11},{10,... | collective-permute-start | bytes 3244040 | tf_op jit(solution)/shard_map/ppermute | solution.py:406
  67.2 24.7 %collective-permute-start.24 = (bf16[704,768]{1,0:T(8,128)(2,1)S(1)}, bf16[704,768]{1,0:T(8,128)(2,1)S(1)}, u32[]{:S(2)}, u32[]{:S(2)}) collective-permute-start(bf16[704,768]{1,0:T(8,128)(2,1)S(1)} %get-tuple-element.219), channel_id=1, source_target_pairs={{0,4},{1,5},{2,6},{3,7},{4,0},{5,1},{6,2},{7,3},{8,12},{9,13},{10,... | collective-permute-start | bytes 3244040 | tf_op jit(solution)/shard_map/ppermute | solution.py:406
  68.7 11.4 %collective-permute-start.12 = (bf16[128,768]{1,0:T(8,128)(2,1)S(1)}, bf16[128,768]{1,0:T(8,128)(2,1)S(1)}, u32[]{:S(2)}, u32[]{:S(2)}) collective-permute-start(bf16[128,768]{1,0:T(8,128)(2,1)S(1)} %get-tuple-element.171), channel_id=1, source_target_pairs={{0,0},{1,16},{2,2},{3,18},{4,4},{5,20},{6,6},{7,22},{8,8},{9,24},{... | collective-permute-start | bytes 589832 | tf_op jit(solution)/shard_map/ppermute | solution.py:406
  69.4 10.8 %collective-permute-start.13 = (bf16[128,768]{1,0:T(8,128)(2,1)S(1)}, bf16[128,768]{1,0:T(8,128)(2,1)S(1)}, u32[]{:S(2)}, u32[]{:S(2)}) collective-permute-start(bf16[128,768]{1,0:T(8,128)(2,1)S(1)} %get-tuple-element.172), channel_id=1, source_target_pairs={{0,8},{1,24},{2,10},{3,26},{4,12},{5,28},{6,14},{7,30},{8,0},{9,16... | collective-permute-start | bytes 589832 | tf_op jit(solution)/shard_map/ppermute | solution.py:406
  82.9 4.1 %collective-permute-start.22 = (bf16[256,768]{1,0:T(8,128)(2,1)S(1)}, bf16[256,768]{1,0:T(8,128)(2,1)S(1)}, u32[]{:S(2)}, u32[]{:S(2)}) collective-permute-start(bf16[256,768]{1,0:T(8,128)(2,1)S(1)} %get-tuple-element.213), channel_id=1, source_target_pairs={{0,1},{1,0},{2,3},{3,2},{4,5},{5,4},{6,7},{7,6},{8,9},{9,8},{10,11... | collective-permute-start | bytes 1179656 | tf_op jit(solution)/shard_map/ppermute | solution.py:406
  85.7 4.6 %collective-permute-start.25 = (bf16[256,768]{1,0:T(8,128)(2,1)S(1)}, bf16[256,768]{1,0:T(8,128)(2,1)S(1)}, u32[]{:S(2)}, u32[]{:S(2)}) collective-permute-start(bf16[256,768]{1,0:T(8,128)(2,1)S(1)} %get-tuple-element.225), channel_id=1, source_target_pairs={{0,1},{1,0},{2,3},{3,2},{4,5},{5,4},{6,7},{7,6},{8,9},{9,8},{10,11... | collective-permute-start | bytes 1179656 | tf_op jit(solution)/shard_map/ppermute | solution.py:406
  92.9 12.1 %collective-permute-start.28 = (bf16[256,768]{1,0:T(8,128)(2,1)S(1)}, bf16[256,768]{1,0:T(8,128)(2,1)S(1)}, u32[]{:S(2)}, u32[]{:S(2)}) collective-permute-start(bf16[256,768]{1,0:T(8,128)(2,1)S(1)} %get-tuple-element.230), channel_id=1, source_target_pairs={{0,4},{1,5},{2,6},{3,7},{4,0},{5,1},{6,2},{7,3},{8,12},{9,13},{10,... | collective-permute-start | bytes 1179656 | tf_op jit(solution)/shard_map/ppermute | solution.py:406
  94.5 12.1 %collective-permute-start.29 = (bf16[256,768]{1,0:T(8,128)(2,1)S(1)}, bf16[256,768]{1,0:T(8,128)(2,1)S(1)}, u32[]{:S(2)}, u32[]{:S(2)}) collective-permute-start(bf16[256,768]{1,0:T(8,128)(2,1)S(1)} %get-tuple-element.231), channel_id=1, source_target_pairs={{0,2},{1,3},{2,0},{3,1},{4,6},{5,7},{6,4},{7,5},{8,10},{9,11},{10,... | collective-permute-start | bytes 1179656 | tf_op jit(solution)/shard_map/ppermute | solution.py:406
  95.9 25.6 %collective-permute-start.27 = (bf16[512,768]{1,0:T(8,128)(2,1)S(1)}, bf16[512,768]{1,0:T(8,128)(2,1)S(1)}, u32[]{:S(2)}, u32[]{:S(2)}) collective-permute-start(bf16[512,768]{1,0:T(8,128)(2,1)S(1)} %get-tuple-element.229), channel_id=1, source_target_pairs={{0,4},{1,5},{2,6},{3,7},{4,0},{5,1},{6,2},{7,3},{8,12},{9,13},{10,... | collective-permute-start | bytes 2359304 | tf_op jit(solution)/shard_map/ppermute | solution.py:406
  96.4 7.0 %collective-permute-start.30 = (bf16[2,96,768]{2,1,0:T(8,128)(2,1)S(1)}, bf16[2,96,768]{2,1,0:T(8,128)(2,1)S(1)}, u32[]{:S(2)}, u32[]{:S(2)}) collective-permute-start(bf16[2,96,768]{2,1,0:T(8,128)(2,1)S(1)} %get-tuple-element.235), channel_id=1, source_target_pairs={{0,8},{1,9},{2,10},{3,11},{4,12},{5,13},{6,14},{7,15},{8,0},{9,1},... | collective-permute-start | bytes 884744 | tf_op jit(solution)/shard_map/ppermute | solution.py:406
  97.1 24.5 %collective-permute-start.26 = (bf16[4,2,48,768]{3,2,1,0:T(8,128)(2,1)S(1)}, bf16[4,2,48,768]{3,2,1,0:T(8,128)(2,1)S(1)}, u32[]{:S(2)}, u32[]{:S(2)}) collective-permute-start(bf16[4,2,48,768]{3,2,1,0:T(8,128)(2,1)S(1)} %get-tuple-element.227), channel_id=1, source_target_pairs={{0,2},{1,3},{2,0},{3,1},{4,6},{5,7},{6,4},{7,5},{8,10},{9,11},{10,... | collective-permute-start | bytes 1769480 | tf_op jit(solution)/shard_map/ppermute | solution.py:406
  107.4 9.4 %collective-permute-start.32 = (bf16[2,128,768]{2,1,0:T(8,128)(2,1)S(1)}, bf16[2,128,768]{2,1,0:T(8,128)(2,1)S(1)}, u32[]{:S(2)}, u32[]{:S(2)}) collective-permute-start(bf16[2,128,768]{2,1,0:T(8,128)(2,1)S(1)} %get-tuple-element.240), channel_id=1, source_target_pairs={{0,8},{1,9},{2,10},{3,11},{4,12},{5,13},{6,14},{7,15},{8,0},{9,1},... | collective-permute-start | bytes 1179656 | tf_op jit(solution)/shard_map/ppermute | solution.py:406
  108.1 6.9 %collective-permute-start.31 = (bf16[96,768]{1,0:T(8,128)(2,1)S(1)}, bf16[96,768]{1,0:T(8,128)(2,1)S(1)}, u32[]{:S(2)}, u32[]{:S(2)}) collective-permute-start(bf16[96,768]{1,0:T(8,128)(2,1)S(1)} %get-tuple-element.238), channel_id=1, source_target_pairs={{0,16},{1,17},{2,18},{3,19},{4,20},{5,21},{6,22},{7,23},{8,24},{9,... | collective-permute-start | bytes 442376 | tf_op jit(solution)/shard_map/ppermute | solution.py:406
  117.5 9.9 %collective-permute-start.35 = (bf16[128,768]{1,0:T(8,128)(2,1)S(1)}, bf16[128,768]{1,0:T(8,128)(2,1)S(1)}, u32[]{:S(2)}, u32[]{:S(2)}) collective-permute-start(bf16[128,768]{1,0:T(8,128)(2,1)S(1)} %get-tuple-element.250), channel_id=1, source_target_pairs={{0,16},{1,17},{2,18},{3,19},{4,20},{5,21},{6,22},{7,23},{8,24},{9,... | collective-permute-start | bytes 589832 | tf_op jit(solution)/shard_map/ppermute | solution.py:406
  120.0 6.8 %collective-permute-start.37 = (bf16[96,768]{1,0:T(8,128)(2,1)S(1)}, bf16[96,768]{1,0:T(8,128)(2,1)S(1)}, u32[]{:S(2)}, u32[]{:S(2)}) collective-permute-start(bf16[96,768]{1,0:T(8,128)(2,1)S(1)} %get-tuple-element.257.refs_1_), channel_id=1, source_target_pairs={{0,2},{1,3},{2,0},{3,1},{4,6},{5,7},{6,4},{7,5},{8,10},{9,11},{10,... | collective-permute-start | bytes 442376 | tf_op jit(solution)/shard_map/ppermute | solution.py:406
  122.4 7.9 %collective-permute-start.34 = (bf16[4,48,768]{2,1,0:T(8,128)(2,1)S(1)}, bf16[4,48,768]{2,1,0:T(8,128)(2,1)S(1)}, u32[]{:S(2)}, u32[]{:S(2)}) collective-permute-start(bf16[4,48,768]{2,1,0:T(8,128)(2,1)S(1)} %get-tuple-element.245), channel_id=1, source_target_pairs={{0,4},{1,5},{2,6},{3,7},{4,0},{5,1},{6,2},{7,3},{8,12},{9,13},{10,... | collective-permute-start | bytes 884744 | tf_op jit(solution)/shard_map/ppermute | solution.py:406
  123.8 6.4 %collective-permute-start.33 = (bf16[4,32,768]{2,1,0:T(8,128)(2,1)S(1)}, bf16[4,32,768]{2,1,0:T(8,128)(2,1)S(1)}, u32[]{:S(2)}, u32[]{:S(2)}) collective-permute-start(bf16[4,32,768]{2,1,0:T(8,128)(2,1)S(1)} %get-tuple-element.244), channel_id=1, source_target_pairs={{0,2},{1,3},{2,0},{3,1},{4,6},{5,7},{6,4},{7,5},{8,10},{9,11},{10,... | collective-permute-start | bytes 589832 | tf_op jit(solution)/shard_map/ppermute | solution.py:406
  126.8 3.4 %collective-permute-start.38 = (bf16[96,768]{1,0:T(8,128)(2,1)S(1)}, bf16[96,768]{1,0:T(8,128)(2,1)S(1)}, u32[]{:S(2)}, u32[]{:S(2)}) collective-permute-start(bf16[96,768]{1,0:T(8,128)(2,1)S(1)} %collective-permute-done.37.refs_7_.refs_3_), channel_id=1, source_target_pairs={{0,1},{1,0},{2,3},{3,2},{4,5},{5,4},{6,7},{7,6},{8,9},{9,8},{10,11... | collective-permute-start | bytes 442376 | tf_op jit(solution)/shard_map/ppermute | solution.py:406
  127.3 2.9 %collective-permute-start.36 = (bf16[96,768]{1,0:T(8,128)(2,1)S(1)}, bf16[96,768]{1,0:T(8,128)(2,1)S(1)}, u32[]{:S(2)}, u32[]{:S(2)}) collective-permute-start(bf16[96,768]{1,0:T(8,128)(2,1)S(1)} %get-tuple-element.257.refs_1_), channel_id=1, source_target_pairs={{0,1},{1,0},{2,3},{3,2},{4,5},{5,4},{6,7},{7,6},{8,9},{9,8},{10,11... | collective-permute-start | bytes 442376 | tf_op jit(solution)/shard_map/ppermute | solution.py:406
  128.7 16.5 %collective-permute-start.48 = (bf16[128,768]{1,0:T(8,128)(2,1)S(1)}, bf16[128,768]{1,0:T(8,128)(2,1)S(1)}, u32[]{:S(2)}, u32[]{:S(2)}) collective-permute-start(bf16[128,768]{1,0:T(8,128)(2,1)S(1)} %get-tuple-element.268.refs_5_), channel_id=1, source_target_pairs={{0,2},{1,3},{2,0},{3,1},{4,6},{5,7},{6,4},{7,5},{8,10},{9,11},{10,... | collective-permute-start | bytes 589832 | tf_op jit(solution)/shard_map/ppermute | solution.py:406
  130.9 12.4 %collective-permute-start.39 = (bf16[80,768]{1,0:T(8,128)(2,1)S(1)}, bf16[80,768]{1,0:T(8,128)(2,1)S(1)}, u32[]{:S(2)}, u32[]{:S(2)}) collective-permute-start(bf16[80,768]{1,0:T(8,128)(2,1)S(1)} %get-tuple-element.259), channel_id=1, source_target_pairs={{0,16},{1,17},{2,18},{3,19},{4,20},{5,21},{6,22},{7,23},{8,24},{9,... | collective-permute-start | bytes 368648 | tf_op jit(solution)/shard_map/ppermute | solution.py:406
  131.0 12.4 %collective-permute-start.40 = (bf16[80,768]{1,0:T(8,128)(2,1)S(1)}, bf16[80,768]{1,0:T(8,128)(2,1)S(1)}, u32[]{:S(2)}, u32[]{:S(2)}) collective-permute-start(bf16[80,768]{1,0:T(8,128)(2,1)S(1)} %get-tuple-element.260), channel_id=1, source_target_pairs={{0,24},{1,25},{2,26},{3,27},{4,28},{5,29},{6,30},{7,31},{8,16},{9,... | collective-permute-start | bytes 368648 | tf_op jit(solution)/shard_map/ppermute | solution.py:406
  135.4 8.5 %collective-permute-start.41 = (bf16[80,768]{1,0:T(8,128)(2,1)S(1)}, bf16[80,768]{1,0:T(8,128)(2,1)S(1)}, u32[]{:S(2)}, u32[]{:S(2)}) collective-permute-start(bf16[80,768]{1,0:T(8,128)(2,1)S(1)} %get-tuple-element.261), channel_id=1, source_target_pairs={{0,8},{1,9},{2,10},{3,11},{4,12},{5,13},{6,14},{7,15},{8,0},{9,1},... | collective-permute-start | bytes 368648 | tf_op jit(solution)/shard_map/ppermute | solution.py:406
  135.4 14.3 %collective-permute-start.43 = (bf16[128,768]{1,0:T(8,128)(2,1)S(1)}, bf16[128,768]{1,0:T(8,128)(2,1)S(1)}, u32[]{:S(2)}, u32[]{:S(2)}) collective-permute-start(bf16[128,768]{1,0:T(8,128)(2,1)S(1)} %get-tuple-element.264), channel_id=1, source_target_pairs={{0,0},{1,16},{2,2},{3,18},{4,4},{5,20},{6,6},{7,22},{8,8},{9,24},{... | collective-permute-start | bytes 589832 | tf_op jit(solution)/shard_map/ppermute | solution.py:406
  144.6 5.1 %collective-permute-start.42 = (bf16[80,768]{1,0:T(8,128)(2,1)S(1)}, bf16[80,768]{1,0:T(8,128)(2,1)S(1)}, u32[]{:S(2)}, u32[]{:S(2)}) collective-permute-start(bf16[80,768]{1,0:T(8,128)(2,1)S(1)} %get-tuple-element.263.refs_1_), channel_id=1, source_target_pairs={{0,2},{1,3},{2,0},{3,1},{4,6},{5,7},{6,4},{7,5},{8,10},{9,11},{10,... | collective-permute-start | bytes 368648 | tf_op jit(solution)/shard_map/ppermute | solution.py:406
  145.2 5.0 %collective-permute-start.47 = (bf16[128,768]{1,0:T(8,128)(2,1)S(1)}, bf16[128,768]{1,0:T(8,128)(2,1)S(1)}, u32[]{:S(2)}, u32[]{:S(2)}) collective-permute-start(bf16[128,768]{1,0:T(8,128)(2,1)S(1)} %get-tuple-element.268.refs_5_), channel_id=1, source_target_pairs={{0,1},{1,0},{2,3},{3,2},{4,5},{5,4},{6,7},{7,6},{8,9},{9,8},{10,11... | collective-permute-start | bytes 589832 | tf_op jit(solution)/shard_map/ppermute | solution.py:406
  145.2 5.0 %collective-permute-start.49 = (bf16[128,768]{1,0:T(8,128)(2,1)S(1)}, bf16[128,768]{1,0:T(8,128)(2,1)S(1)}, u32[]{:S(2)}, u32[]{:S(2)}) collective-permute-start(bf16[128,768]{1,0:T(8,128)(2,1)S(1)} %collective-permute-done.48.refs_7_), channel_id=1, source_target_pairs={{0,1},{1,0},{2,3},{3,2},{4,5},{5,4},{6,7},{7,6},{8,9},{9,8},{10,11... | collective-permute-start | bytes 589832 | tf_op jit(solution)/shard_map/ppermute | solution.py:406
  145.7 9.2 %collective-permute-start.44 = (bf16[128,768]{1,0:T(8,128)(2,1)S(1)}, bf16[128,768]{1,0:T(8,128)(2,1)S(1)}, u32[]{:S(2)}, u32[]{:S(2)}) collective-permute-start(bf16[128,768]{1,0:T(8,128)(2,1)S(1)} %get-tuple-element.266), channel_id=1, source_target_pairs={{0,8},{1,24},{2,10},{3,26},{4,12},{5,28},{6,14},{7,30},{8,0},{9,16... | collective-permute-start | bytes 589832 | tf_op jit(solution)/shard_map/ppermute | solution.py:406
  149.7 2.8 %collective-permute-start.45 = (bf16[80,768]{1,0:T(8,128)(2,1)S(1)}, bf16[80,768]{1,0:T(8,128)(2,1)S(1)}, u32[]{:S(2)}, u32[]{:S(2)}) collective-permute-start(bf16[80,768]{1,0:T(8,128)(2,1)S(1)} %get-tuple-element.263.refs_1_), channel_id=1, source_target_pairs={{0,1},{1,0},{2,3},{3,2},{4,5},{5,4},{6,7},{7,6},{8,9},{9,8},{10,11... | collective-permute-start | bytes 368648 | tf_op jit(solution)/shard_map/ppermute | solution.py:406
  149.7 2.8 %collective-permute-start.46 = (bf16[80,768]{1,0:T(8,128)(2,1)S(1)}, bf16[80,768]{1,0:T(8,128)(2,1)S(1)}, u32[]{:S(2)}, u32[]{:S(2)}) collective-permute-start(bf16[80,768]{1,0:T(8,128)(2,1)S(1)} %collective-permute-done.42.refs_3_), channel_id=1, source_target_pairs={{0,1},{1,0},{2,3},{3,2},{4,5},{5,4},{6,7},{7,6},{8,9},{9,8},{10,11... | collective-permute-start | bytes 368648 | tf_op jit(solution)/shard_map/ppermute | solution.py:406
  (15 other events, 115.9 us)
